TPU v7x, 256 devices: a whole 4x4x8 slice. The times are simulated.
256 devices in a mesh: dp: 16 (over y_hi, z), mp: 16 (over x, y_lo, core).
Axes of the slice: x: 4, y: 4 (y_hi: 2, y_lo: 2; y = y_hi * 2 + y_lo), z: 8, core: 2. Of those that a mesh axis runs over, the one named last changes fastest.
Arguments:
- tokens: bfloat16 [2048, 8192], P('dp', 'mp'), may hold values from -6 to 6
- pattern: int32 [128, 16], P('mp'), may hold values from 0 to 63, all different within a row
- w_up: bfloat16 [128, 16, 128, 128], P('mp', 'dp'), may hold values from -0.125 to 0.125
- w_down: bfloat16 [128, 16, 128, 128], P('mp', 'dp'), may hold values from -0.09375 to 0.09375
- cotangent: bfloat16 [2048, 8192], P('dp', 'mp'), may hold values from -6 to 6
Outputs:
- mixed: bfloat16 [2048, 8192], P('dp', 'mp')
- grad_tokens: bfloat16 [2048, 8192], P('dp', 'mp')
- grad_up: float32 [128, 16, 128, 128], P('mp', 'dp')
- grad_down: float32 [128, 16, 128, 128], P('mp', 'dp')
Inputs may be any that keep to these rules, and one draw needn't show every extreme that they name: Each row of pattern names 16 different block rows; every block row is named by some row.
All inputs are finite; a program needn't handle non-finite values.
Results may differ from a plain program's by a relative error of at most 0.02.
Values may be sent and summed in bfloat16 or wider, within the bound.
No kernel may reach another device: no remote copies, remote signals or barrier semaphores. Data moves between devices by JAX's collectives and lax.ppermute only.
A program may use at most 128 MiB of HBM per device.

v0:
```python
import jax
import jax.numpy as jnp
from jax import lax
from jax.experimental import pallas as pl
from jax.experimental.pallas import tpu as pltpu
from jax.sharding import PartitionSpec as P

AXES = ("dp", "mp")
B = 128
MIB = 1 << 20
GELU_C = 0.7978845608028654
GELU_A = 0.044715


def where_is(index):
    dp, mp = divmod(index, 16)
    return mp // 4, (dp // 8) * 2 + (mp // 2) % 2, dp % 8, mp % 2


def place_of(x, y, z, core):
    return ((y // 2) * 8 + z) * 16 + x * 4 + (y % 2) * 2 + core


def send(value, step):
    return lax.ppermute(
        value, AXES, [(source, place_of(*step(*where_is(source)))) for source in range(256)]
    )


def across(steps):
    return lambda x, y, z, c: ((x + steps * (1 - c)) % 4, (y + steps * c) % 4, z, c)


def beside(steps):
    return lambda x, y, z, c: ((x + steps * c) % 4, (y + steps * (1 - c)) % 4, z, c)


def other_core(x, y, z, c):
    return x, y, z, 1 - c


def other_half(x, y, z, c):
    return x, (y + 2) % 4, z, c


def gelu_parts(h):
    t = jnp.tanh(GELU_C * (h + GELU_A * (h * h * h)))
    half = 0.5 * (1.0 + t)
    slope = half + 0.5 * h * (1.0 - t * t) * (GELU_C * (1.0 + 3.0 * GELU_A * (h * h)))
    return h * half, slope


NT = (((1,), (1,)), ((), ()))


def dot(a, b, dims=(((1,), (0,)), ((), ()))):
    return lax.dot_general(a, b, dims, preferred_element_type=jnp.float32)


def first_kernel(spots, rows, *refs):
    plane_in, w_in = refs[:8], refs[8]
    act_out, gh_out, grads = refs[9:12]
    xs, gs, ws, sem_x, sem_g, sem_w = refs[12:]

    copies = []
    for n in range(8):
        for r in range(4):
            spot = spots[n * 4 + r]
            half = pl.ds(pl.multiple_of((spot % 2) * B, B), B)
            for m, (scratch, sems) in enumerate(((xs, sem_x), (gs, sem_g))):
                copies.append(
                    pltpu.make_async_copy(
                        plane_in[n].at[r, m], scratch.at[spot // 2, half], sems.at[n * 4 + r]
                    )
                )
    copies.append(pltpu.make_async_copy(w_in, ws, sem_w))
    for copy in copies:
        copy.start()
    for copy in copies:
        copy.wait()

    def pick(scratch, j, s):
        p = rows[j, s]
        q = rows[j, 8 + s]
        return jnp.concatenate(
            [
                scratch[p // 4, :, pl.ds(pl.multiple_of((p % 4) * B, B), B)],
                scratch[q // 4, :, pl.ds(pl.multiple_of((q % 4) * B, B), B)],
            ],
            axis=1,
        )

    def column(j, carry):
        hidden = jnp.zeros((2 * B, B), jnp.float32)
        grad_act = jnp.zeros((2 * B, B), jnp.float32)
        for s in range(8):
            up = jnp.concatenate([ws[s, 0, 0, j], ws[s, 1, 0, j]], axis=0)
            hidden += dot(pick(xs, j, s), up)
            down = jnp.concatenate([ws[s, 0, 1, j], ws[s, 1, 1, j]], axis=1)
            grad_act += dot(pick(gs, j, s), down, NT)
        value, slope = gelu_parts(hidden)
        act = value.astype(jnp.bfloat16)
        gh = (slope * grad_act).astype(jnp.bfloat16)
        act_out[j] = act
        gh_out[j] = gh
        act_t = value.T.astype(jnp.bfloat16)
        gh_t = (slope * grad_act).T.astype(jnp.bfloat16)
        for s in range(8):
            up = dot(gh_t, pick(xs, j, s)).astype(jnp.bfloat16)
            grads[s, 0, 0, j] = up[:, :B]
            grads[s, 1, 0, j] = up[:, B:]
            down = dot(act_t, pick(gs, j, s)).astype(jnp.bfloat16)
            grads[s, 0, 1, j] = down[:, :B]
            grads[s, 1, 1, j] = down[:, B:]
        return carry

    lax.fori_loop(0, 4, column, 0)


def second_kernel(outs_at, rows, act_ref, gh_ref, *refs):
    w_in, parts, ws, out_acc, in_acc, sem_w = refs
    load = pltpu.make_async_copy(w_in, ws, sem_w)
    load.start()

    def clear(p, carry):
        out_acc[p] = jnp.zeros((2 * B, B), jnp.float32)
        in_acc[p] = jnp.zeros((2 * B, B), jnp.float32)
        return carry

    lax.fori_loop(0, 64, clear, 0)
    load.wait()

    def column(j, carry):
        act = act_ref[j]
        gh = gh_ref[j]
        for s in range(8):
            p = rows[j, s]
            q = rows[j, 8 + s]
            down = jnp.concatenate([ws[s, 0, 1, j], ws[s, 1, 1, j]], axis=1)
            term = dot(act, down)
            out_acc[p] += term[:, :B]
            out_acc[q] += term[:, B:]
            up = jnp.concatenate([ws[s, 0, 0, j], ws[s, 1, 0, j]], axis=0)
            term = dot(gh, up, NT)
            in_acc[p] += term[:, :B]
            in_acc[q] += term[:, B:]
        return carry

    lax.fori_loop(0, 4, column, 0)

    def finish(p, carry):
        lanes = pl.ds(pl.multiple_of((p % 4) * B, B), B)
        for half in range(2):
            rows_of = pl.ds(half * B, B)
            at = outs_at[p * 2 + half]
            parts[at // 4, at % 4, 0, :, lanes] = out_acc[p, rows_of].astype(jnp.bfloat16)
            parts[at // 4, at % 4, 1, :, lanes] = in_acc[p, rows_of].astype(jnp.bfloat16)
        return carry

    lax.fori_loop(0, 64, finish, 0)


SMEM = pl.BlockSpec(memory_space=pltpu.SMEM)
VMEM = pl.BlockSpec(memory_space=pltpu.VMEM)
ANY = pl.BlockSpec(memory_space=pl.ANY)
HALVES = [list(range(8)), list(range(8, 16))]
STEPS = (0, 1, 3, 2)


def total(parts):
    value = parts[0].astype(jnp.float32)
    for part in parts[1:]:
        value = value + part.astype(jnp.float32)
    return value


def gather_plane(shard):
    row = jnp.stack([shard] + [send(shard, across(n)) for n in STEPS[1:]])
    own = [row] + [send(row, beside(n)) for n in STEPS[1:]]
    return own + [send(part, other_core) for part in own]


def scatter_plane(parts):
    kept = [None] * 4
    for n in (3, 1, 2, 0):
        kept[n] = total([parts[n], send(parts[4 + n], other_core)]).astype(jnp.bfloat16)
    row = [kept[0]] + [send(kept[n], beside(STEPS[n])) for n in (3, 1, 2)]
    row = total(row).astype(jnp.bfloat16)
    return total([row[0]] + [send(row[n], across(STEPS[n])) for n in (3, 1, 2)]).astype(jnp.bfloat16)


def local(tokens, pattern, w_up, w_down, cotangent):
    dp, mp = lax.axis_index("dp"), lax.axis_index("mp")
    x, y, z, core = mp // 4, (dp // 8) * 2 + (mp // 2) % 2, dp % 8, mp % 2
    yh = dp // 8
    bf16, f32 = jnp.bfloat16, jnp.float32

    steps = jnp.array(STEPS, jnp.int32)
    def spots_of(c_at):
        first, second = steps[None, :], steps[:, None]
        x_at = (x - jnp.where(c_at == 0, first, second)) % 4
        y_at = (y - jnp.where(c_at == 0, second, first)) % 4
        return (x_at * 4 + (y_at % 2) * 2 + c_at) * 2 + y_at // 2

    spots = jnp.concatenate([spots_of(core).reshape(-1), spots_of(1 - core).reshape(-1)])
    spots = spots.astype(jnp.int32)
    own_rows = lax.dynamic_slice_in_dim(pattern, yh * 4, 4, 0)
    rows = jnp.where(yh == 0, own_rows, jnp.roll(own_rows, 8, axis=1))
    order = jnp.array([0, 1, 3, 2], jnp.int32)
    p_all = jnp.arange(64, dtype=jnp.int32)[:, None]
    c_to = (p_all // 4) % 2
    y_to = jnp.arange(2, dtype=jnp.int32)[None, :] * 2 + (p_all // 8) % 2
    x_step = order[(p_all // 16 - x) % 4] + 0 * y_to
    y_step = order[(y_to - y) % 4]
    first, second = jnp.where(c_to == 0, x_step, y_step), jnp.where(c_to == 0, y_step, x_step)
    outs_at = (((c_to ^ core) * 4 + second) * 4 + first).reshape(-1).astype(jnp.int32)

    both = jnp.stack([w_up[:, 0], w_down[:, 0]])
    piece_a = lax.dynamic_slice_in_dim(both, yh * 4, 4, 1)
    piece_b = lax.dynamic_slice_in_dim(both, (1 - yh) * 4, 4, 1)
    plane = gather_plane(jnp.stack([tokens, cotangent]))
    weights = lax.all_gather(
        jnp.stack([piece_a, send(piece_b, other_half)]), "dp", axis_index_groups=HALVES
    )

    act, gh, grads = pl.pallas_call(
        first_kernel,
        out_shape=[jax.ShapeDtypeStruct((4, 2 * B, B), bf16)] * 2
        + [jax.ShapeDtypeStruct((8, 2, 2, 4, B, B), bf16)],
        in_specs=[SMEM, SMEM] + [ANY] * 9,
        out_specs=[VMEM] * 3,
        scratch_shapes=[
            pltpu.VMEM((16, 2 * B, 4 * B), bf16),
            pltpu.VMEM((16, 2 * B, 4 * B), bf16),
            pltpu.VMEM((8, 2, 2, 4, B, B), bf16),
            pltpu.SemaphoreType.DMA((32,)),
            pltpu.SemaphoreType.DMA((32,)),
            pltpu.SemaphoreType.DMA,
        ],
        compiler_params=pltpu.CompilerParams(vmem_limit_bytes=18 * MIB),
        cost_estimate=pl.CostEstimate(
            flops=2_000_000_000, bytes_accessed=16 * MIB, transcendentals=0
        ),
        name="first",
    )(spots, rows, *plane, weights)
    summed = lax.psum_scatter(
        grads, "dp", scatter_dimension=0, axis_index_groups=HALVES, tiled=True
    )[0]

    parts = pl.pallas_call(
        second_kernel,
        out_shape=jax.ShapeDtypeStruct((8, 4, 2, B, 4 * B), bf16),
        in_specs=[SMEM, SMEM, VMEM, VMEM, ANY],
        out_specs=VMEM,
        scratch_shapes=[
            pltpu.VMEM((8, 2, 2, 4, B, B), bf16),
            pltpu.VMEM((64, 2 * B, B), f32),
            pltpu.VMEM((64, 2 * B, B), f32),
            pltpu.SemaphoreType.DMA,
        ],
        compiler_params=pltpu.CompilerParams(vmem_limit_bytes=24 * MIB),
        cost_estimate=pl.CostEstimate(
            flops=1_000_000_000, bytes_accessed=16 * MIB, transcendentals=0
        ),
        name="second",
    )(outs_at, rows, act, gh, weights)

    result = scatter_plane(parts)
    mixed, grad_tokens = result[0], result[1]
    other = send(summed[1], other_half).astype(f32)
    summed_a = summed[0].astype(f32)
    grad_both = jnp.where(
        yh == 0,
        jnp.concatenate([summed_a, other], axis=1),
        jnp.concatenate([other, summed_a], axis=1),
    )
    grad_up = jnp.swapaxes(grad_both[0], 1, 2)[:, None]
    grad_down = grad_both[1][:, None]
    return mixed, grad_tokens, grad_up, grad_down


def solution(mesh):
    return jax.shard_map(
        local,
        mesh=mesh,
        in_specs=(
            P("dp", "mp"),
            P("mp", None),
            P("mp", "dp", None, None),
            P("mp", "dp", None, None),
            P("dp", "mp"),
        ),
        out_specs=(
            P("dp", "mp"),
            P("dp", "mp"),
            P("mp", "dp", None, None),
            P("mp", "dp", None, None),
        ),
        check_vma=False,
    )
```

profile of v0, /device:TPU:1, one launch (start us, length us, event | category | flops | bytes accessed | tf_op | source)
XLA Modules:
  0.0 170.1 jit_solution(11027976828262636196)
XLA Ops:
  7.3 1.2 fusion.9
  8.4 3.8 %collective-permute-start.10 = (bf16[2,4,128,128]{3,2,1,0:T(8,128)(2,1)S(1)}, bf16[2,4,128,128]{3,2,1,0:T(8,128)(2,1)S(1)}, u32[]{:S(2)}, u32[]{:S(2)}) collective-permute-start(bf16[2,4,128,128]{3,2,1,0:T(8,128)(2,1)S(1)} %get-tuple-element.37), channel_id=1, source_target_pairs={{0,128},{1,129},{2,130},{3,131},{4,132},{5,133},{6,134},{7,135},{8... | collective-permute-start | bytes 786440 | tf_op jit(solution)/shard_map/ppermute | solution.py:25
  12.3 5.0 %collective-permute-done.10 = bf16[2,4,128,128]{3,2,1,0:T(8,128)(2,1)S(1)} collective-permute-done((bf16[2,4,128,128]{3,2,1,0:T(8,128)(2,1)S(1)}, bf16[2,4,128,128]{3,2,1,0:T(8,128)(2,1)S(1)}, u32[]{:S(2)}, u32[]{:S(2)}) %collective-permute-start.10) | collective-permute-done | bytes 262176 | tf_op jit(solution)/shard_map/ppermute | solution.py:25
  18.2 3.6 %collective-permute-start.1 = (bf16[2,128,512]{2,1,0:T(8,128)(2,1)S(1)}, bf16[2,128,512]{2,1,0:T(8,128)(2,1)S(1)}, u32[]{:S(2)}, u32[]{:S(2)}) collective-permute-start(bf16[2,128,512]{2,1,0:T(8,128)(2,1)S(1)} %get-tuple-element.41), channel_id=1, source_target_pairs={{0,12},{1,131},{2,14},{3,1},{4,0},{5,135},{6,2},{7,5},{8,4},{9,139... | collective-permute-start | bytes 786440 | tf_op jit(solution)/shard_map/ppermute | solution.py:25
  21.8 1.6 collective-permute-start.2
  23.5 1.7 collective-permute-done.1
  25.1 6.2 %collective-permute-done = bf16[2,128,512]{2,1,0:T(8,128)(2,1)S(1)} collective-permute-done((bf16[2,128,512]{2,1,0:T(8,128)(2,1)S(1)}, bf16[2,128,512]{2,1,0:T(8,128)(2,1)S(1)}, u32[]{:S(2)}, u32[]{:S(2)}) %collective-permute-start) | collective-permute-done | bytes 262176 | tf_op jit(solution)/shard_map/ppermute | solution.py:25
  31.5 2.5 %collective-permute-start.5 = (bf16[4,2,128,512]{3,2,1,0:T(8,128)(2,1)S(1)}, bf16[4,2,128,512]{3,2,1,0:T(8,128)(2,1)S(1)}, u32[]{:S(2)}, u32[]{:S(2)}) collective-permute-start(bf16[4,2,128,512]{3,2,1,0:T(8,128)(2,1)S(1)} %pad_maximum_fusion.refs_0_), channel_id=1, source_target_pairs={{0,128},{1,9},{2,130},{3,11},{4,132},{5,13},{6,134},{7,15},{8,136}... | collective-permute-start | bytes 3145736 | tf_op jit(solution)/shard_map/ppermute | solution.py:25
  35.5 15.1 %collective-permute-start.6 = (bf16[4,2,128,512]{3,2,1,0:T(8,128)(2,1)S(1)}, bf16[4,2,128,512]{3,2,1,0:T(8,128)(2,1)}, u32[]{:S(2)}, u32[]{:S(2)}) collective-permute-start(bf16[4,2,128,512]{3,2,1,0:T(8,128)(2,1)S(1)} %pad_maximum_fusion.refs_0_), channel_id=1, source_target_pairs={{0,1},{1,0},{2,3},{3,2},{4,5},{5,4},{6,7},{7,6},{8,9},{9,8},{10,11... | collective-permute-start | bytes 3145736 | tf_op jit(solution)/shard_map/ppermute | solution.py:25
  50.6 10.9 %collective-permute-start.9 = (bf16[4,2,128,512]{3,2,1,0:T(8,128)(2,1)S(1)}, bf16[4,2,128,512]{3,2,1,0:T(8,128)(2,1)}, u32[]{:S(2)}, u32[]{:S(2)}) collective-permute-start(bf16[4,2,128,512]{3,2,1,0:T(8,128)(2,1)S(1)} %collective-permute-done.5.refs_3_), channel_id=1, source_target_pairs={{0,1},{1,0},{2,3},{3,2},{4,5},{5,4},{6,7},{7,6},{8,9},{9,8},{10,11... | collective-permute-start | bytes 3145736 | tf_op jit(solution)/shard_map/ppermute | solution.py:25
  61.4 12.1 %collective-permute-start.8 = (bf16[4,2,128,512]{3,2,1,0:T(8,128)(2,1)S(1)}, bf16[4,2,128,512]{3,2,1,0:T(8,128)(2,1)}, u32[]{:S(2)}, u32[]{:S(2)}) collective-permute-start(bf16[4,2,128,512]{3,2,1,0:T(8,128)(2,1)S(1)} %collective-permute-done.4.refs_2_), channel_id=1, source_target_pairs={{0,1},{1,0},{2,3},{3,2},{4,5},{5,4},{6,7},{7,6},{8,9},{9,8},{10,11... | collective-permute-start | bytes 3145736 | tf_op jit(solution)/shard_map/ppermute | solution.py:25
  74.2 3.1 %collective-permute-done.8.refs_6_ = bf16[4,2,128,512]{3,2,1,0:T(8,128)(2,1)} collective-permute-done((bf16[4,2,128,512]{3,2,1,0:T(8,128)(2,1)S(1)}, bf16[4,2,128,512]{3,2,1,0:T(8,128)(2,1)}, u32[]{:S(2)}, u32[]{:S(2)}) %collective-permute-start.8) | collective-permute-done | bytes 1048608 | tf_op jit(solution)/shard_map/ppermute | solution.py:25
  77.7 2.2 %copy-done = bf16[16,2,4,128,128]{4,3,2,1,0:T(8,128)(2,1)S(1)} copy-done((bf16[16,2,4,128,128]{4,3,2,1,0:T(8,128)(2,1)S(1)}, bf16[16,2,4,128,128]{4,3,2,1,0:T(8,128)(2,1)}, u32[]{:S(2)}) %copy-start) | copy-done | bytes 4194328
  79.9 13.6 %first.1 = (bf16[4,256,128]{2,1,0:T(8,128)(2,1)S(1)}, bf16[4,256,128]{2,1,0:T(8,128)(2,1)S(1)}, bf16[8,2,2,4,128,128]{5,4,3,2,1,0:T(8,128)(2,1)S(1)}) custom-call(s32[32]{0:T(128)S(1)} %pad_add_fusion.spots, s32[4,16]{1,0:T(4,128)S(1)} %add_select_fusion.rows, bf16[4,2,128,512]{3,2,1,0:T(8,128)(2,1)S(1)} %pad_maximum_fusion.refs_0_, ...), custom_call_target="tpu_custom_call" | custom-call | flops 2000000000 | bytes 16777216 | tf_op jit(solution)/shard_map/first/pallas_call | solution.py:226
  93.5 2.0 %copy-done.2 = bf16[8,2,2,4,128,128]{5,4,3,2,1,0:T(8,128)(2,1)} copy-done((bf16[8,2,2,4,128,128]{5,4,3,2,1,0:T(8,128)(2,1)}, bf16[8,2,2,4,128,128]{5,4,3,2,1,0:T(8,128)(2,1)S(1)}, u32[]{:S(2)}) %copy-start.2) | copy-done | bytes 4194328
  97.2 2.2 %copy-done.1 = bf16[16,2,4,128,128]{4,3,2,1,0:T(8,128)(2,1)S(1)} copy-done((bf16[16,2,4,128,128]{4,3,2,1,0:T(8,128)(2,1)S(1)}, bf16[16,2,4,128,128]{4,3,2,1,0:T(8,128)(2,1)}, u32[]{:S(2)}) %copy-start.1) | copy-done | bytes 4194328
  99.3 6.9 %second.1 = bf16[8,4,2,128,512]{4,3,2,1,0:T(8,128)(2,1)S(1)} custom-call(s32[128]{0:T(128)S(1)} %add.279.outs_at, s32[4,16]{1,0:T(4,128)S(1)} %add_select_fusion.rows, bf16[4,256,128]{2,1,0:T(8,128)(2,1)S(1)} %get-tuple-element.7.act_ref, bf16[4,256,128]{2,1,0:T(8,128)(2,1)S(1)} %copy-done.4, bf16[8,2,2,4,128,128]{5,4,3,2,1,0:T(8,128)(2,1)S(1)} %bitcast.80), custom_call_target="tpu_custom_call" | custom-call | flops 1000000000 | bytes 16777216 | tf_op jit(solution)/shard_map/second/pallas_call | solution.py:250
  107.9 1.7 collective-permute-done.16
  109.6 1.5 collective-permute-done.14
  111.1 1.5 collective-permute-done.12
  112.6 1.2 fusion.2
  113.8 2.8 %collective-permute-start.13 = (bf16[4,2,128,512]{3,2,1,0:T(8,128)(2,1)S(1)}, bf16[4,2,128,512]{3,2,1,0:T(8,128)(2,1)S(1)}, u32[]{:S(2)}, u32[]{:S(2)}) collective-permute-start(bf16[4,2,128,512]{3,2,1,0:T(8,128)(2,1)S(1)} %get-tuple-element.26), channel_id=1, source_target_pairs={{0,128},{1,9},{2,130},{3,11},{4,132},{5,13},{6,134},{7,15},{8,136}... | collective-permute-start | bytes 3145736 | tf_op jit(solution)/shard_map/ppermute | solution.py:25
  116.5 0.9 collective-permute-start.17
  118.0 11.3 %collective-permute-done.13 = bf16[4,2,128,512]{3,2,1,0:T(8,128)(2,1)S(1)} collective-permute-done((bf16[4,2,128,512]{3,2,1,0:T(8,128)(2,1)S(1)}, bf16[4,2,128,512]{3,2,1,0:T(8,128)(2,1)S(1)}, u32[]{:S(2)}, u32[]{:S(2)}) %collective-permute-start.13) | collective-permute-done | bytes 1048608 | tf_op jit(solution)/shard_map/ppermute | solution.py:25
  129.3 11.4 %collective-permute-done.17 = bf16[4,2,128,512]{3,2,1,0:T(8,128)(2,1)S(1)} collective-permute-done((bf16[4,2,128,512]{3,2,1,0:T(8,128)(2,1)S(1)}, bf16[4,2,128,512]{3,2,1,0:T(8,128)(2,1)S(1)}, u32[]{:S(2)}, u32[]{:S(2)}) %collective-permute-start.17) | collective-permute-done | bytes 1048608 | tf_op jit(solution)/shard_map/ppermute | solution.py:25
  141.6 2.8 %collective-permute-start.18 = (bf16[2,128,512]{2,1,0:T(8,128)(2,1)S(1)}, bf16[2,128,512]{2,1,0:T(8,128)(2,1)S(1)}, u32[]{:S(2)}, u32[]{:S(2)}) collective-permute-start(bf16[2,128,512]{2,1,0:T(8,128)(2,1)S(1)} %get-tuple-element.31), channel_id=1, source_target_pairs={{0,8},{1,129},{2,10},{3,131},{4,12},{5,133},{6,14},{7,135},{8,0},{... | collective-permute-start | bytes 786440 | tf_op jit(solution)/shard_map/ppermute | solution.py:25
  145.8 5.5 %reduce-scatter.2.cloned.1.call-done = bf16[1,2,2,4,128,128]{5,4,3,2,1,0:T(8,128)(2,1)} async-done(((bf16[8,2,2,4,128,128]{5,4,3,2,1,0:T(8,128)(2,1)}), bf16[1,2,2,4,128,128]{5,4,3,2,1,0:T(8,128)(2,1)}) %reduce-scatter.2.cloned.1.call-update) | async-done | bytes 524304 | tf_op jit(solution)/shard_map/reduce_scatter | solution.py:246
  151.3 1.1 fusion.10
  152.4 2.8 %collective-permute-start.21 = (bf16[2,4,128,128]{3,2,1,0:T(8,128)(2,1)S(1)}, bf16[2,4,128,128]{3,2,1,0:T(8,128)(2,1)S(1)}, u32[]{:S(2)}, u32[]{:S(2)}) collective-permute-start(bf16[2,4,128,128]{3,2,1,0:T(8,128)(2,1)S(1)} %get-tuple-element.35), channel_id=1, source_target_pairs={{0,128},{1,129},{2,130},{3,131},{4,132},{5,133},{6,134},{7,135},{8... | collective-permute-start | bytes 786440 | tf_op jit(solution)/shard_map/ppermute | solution.py:25
  156.1 5.2 %collective-permute-done.21 = bf16[2,4,128,128]{3,2,1,0:T(8,128)(2,1)S(1)} collective-permute-done((bf16[2,4,128,128]{3,2,1,0:T(8,128)(2,1)S(1)}, bf16[2,4,128,128]{3,2,1,0:T(8,128)(2,1)S(1)}, u32[]{:S(2)}, u32[]{:S(2)}) %collective-permute-start.21) | collective-permute-done | bytes 262176 | tf_op jit(solution)/shard_map/ppermute | solution.py:25
  161.4 0.9 slice_bitcast_fusion.8
  162.3 1.0 copy.18
  (70 shorter events, 10.8 us)
Async XLA Ops:
  7.2 11.0 %copy-start.5 = (bf16[128,512]{1,0:T(8,128)(2,1)S(1)}, bf16[128,512]{1,0:T(8,128)(2,1)}, u32[]{:S(2)}) copy-start(bf16[128,512]{1,0:T(8,128)(2,1)} %param.11) | copy-start | bytes 393220
  7.2 11.0 %copy-start.6 = (bf16[128,512]{1,0:T(8,128)(2,1)S(1)}, bf16[128,512]{1,0:T(8,128)(2,1)}, u32[]{:S(2)}) copy-start(bf16[128,512]{1,0:T(8,128)(2,1)} %param.7) | copy-start | bytes 393220
  7.2 70.5 %all-gather.3.cloned.1.call-start = ((), (), s32[]{:S(2)}) async-start(), calls=%async_computation.2 | async-start | bytes 4718592 | tf_op jit(solution)/shard_map/all_gather | solution.py:222
  8.4 8.8 %collective-permute-start.10 = (bf16[2,4,128,128]{3,2,1,0:T(8,128)(2,1)S(1)}, bf16[2,4,128,128]{3,2,1,0:T(8,128)(2,1)S(1)}, u32[]{:S(2)}, u32[]{:S(2)}) collective-permute-start(bf16[2,4,128,128]{3,2,1,0:T(8,128)(2,1)S(1)} %get-tuple-element.37), channel_id=1, source_target_pairs={{0,128},{1,129},{2,130},{3,131},{4,132},{5,133},{6,134},{7,135},{8... | collective-permute-start | bytes 786440 | tf_op jit(solution)/shard_map/ppermute | solution.py:25
  17.2 56.3 %copy-start.8 = (s32[4]{0:T(128)S(1)}, s32[4]{0:T(128)}, u32[]{:S(2)}) copy-start(s32[4]{0:T(128)} %constant.182.clone) | copy-start | bytes 52
  17.2 56.8 %copy-start.7 = (s32[8,16]{1,0:T(8,128)S(1)}, s32[8,16]{1,0:T(8,128)}, u32[]{:S(2)}) copy-start(s32[8,16]{1,0:T(8,128)} %param.8) | copy-start | bytes 1540
  18.1 133.2 %reduce-scatter.2.cloned.1.call-start = ((), (), s32[]{:S(2)}) async-start(), calls=%async_computation.1 | async-start | bytes 4718592 | tf_op jit(solution)/shard_map/reduce_scatter | solution.py:246
  18.2 6.9 %collective-permute-start.1 = (bf16[2,128,512]{2,1,0:T(8,128)(2,1)S(1)}, bf16[2,128,512]{2,1,0:T(8,128)(2,1)S(1)}, u32[]{:S(2)}, u32[]{:S(2)}) collective-permute-start(bf16[2,128,512]{2,1,0:T(8,128)(2,1)S(1)} %get-tuple-element.41), channel_id=1, source_target_pairs={{0,12},{1,131},{2,14},{3,1},{4,0},{5,135},{6,2},{7,5},{8,4},{9,139... | collective-permute-start | bytes 786440 | tf_op jit(solution)/shard_map/ppermute | solution.py:25
  21.8 9.5 %collective-permute-start = (bf16[2,128,512]{2,1,0:T(8,128)(2,1)S(1)}, bf16[2,128,512]{2,1,0:T(8,128)(2,1)S(1)}, u32[]{:S(2)}, u32[]{:S(2)}) collective-permute-start(bf16[2,128,512]{2,1,0:T(8,128)(2,1)S(1)} %get-tuple-element.41), channel_id=1, source_target_pairs={{0,4},{1,3},{2,6},{3,129},{4,8},{5,7},{6,10},{7,133},{8,12},{9,11}... | collective-permute-start | bytes 786440 | tf_op jit(solution)/shard_map/ppermute | solution.py:25
  21.8 9.5 %collective-permute-start.2 = (bf16[2,128,512]{2,1,0:T(8,128)(2,1)S(1)}, bf16[2,128,512]{2,1,0:T(8,128)(2,1)S(1)}, u32[]{:S(2)}, u32[]{:S(2)}) collective-permute-start(bf16[2,128,512]{2,1,0:T(8,128)(2,1)S(1)} %get-tuple-element.41), channel_id=1, source_target_pairs={{0,8},{1,129},{2,10},{3,131},{4,12},{5,133},{6,14},{7,135},{8,0},{... | collective-permute-start | bytes 786440 | tf_op jit(solution)/shard_map/ppermute | solution.py:25
  31.5 19.1 %collective-permute-start.5 = (bf16[4,2,128,512]{3,2,1,0:T(8,128)(2,1)S(1)}, bf16[4,2,128,512]{3,2,1,0:T(8,128)(2,1)S(1)}, u32[]{:S(2)}, u32[]{:S(2)}) collective-permute-start(bf16[4,2,128,512]{3,2,1,0:T(8,128)(2,1)S(1)} %pad_maximum_fusion.refs_0_), channel_id=1, source_target_pairs={{0,128},{1,9},{2,130},{3,11},{4,132},{5,13},{6,134},{7,15},{8,136}... | collective-permute-start | bytes 3145736 | tf_op jit(solution)/shard_map/ppermute | solution.py:25
  34.0 27.4 %collective-permute-start.4 = (bf16[4,2,128,512]{3,2,1,0:T(8,128)(2,1)S(1)}, bf16[4,2,128,512]{3,2,1,0:T(8,128)(2,1)S(1)}, u32[]{:S(2)}, u32[]{:S(2)}) collective-permute-start(bf16[4,2,128,512]{3,2,1,0:T(8,128)(2,1)S(1)} %pad_maximum_fusion.refs_0_), channel_id=1, source_target_pairs={{0,130},{1,13},{2,0},{3,15},{4,134},{5,1},{6,4},{7,3},{8,138},{9,5... | collective-permute-start | bytes 3145736 | tf_op jit(solution)/shard_map/ppermute | solution.py:25
  34.9 38.6 %collective-permute-start.3 = (bf16[4,2,128,512]{3,2,1,0:T(8,128)(2,1)S(1)}, bf16[4,2,128,512]{3,2,1,0:T(8,128)(2,1)}, u32[]{:S(2)}, u32[]{:S(2)}) collective-permute-start(bf16[4,2,128,512]{3,2,1,0:T(8,128)(2,1)S(1)} %pad_maximum_fusion.refs_0_), channel_id=1, source_target_pairs={{0,2},{1,5},{2,128},{3,7},{4,6},{5,9},{6,132},{7,11},{8,10},{9,13}... | collective-permute-start | bytes 3145736 | tf_op jit(solution)/shard_map/ppermute | solution.py:25
  35.5 38.7 %collective-permute-start.6 = (bf16[4,2,128,512]{3,2,1,0:T(8,128)(2,1)S(1)}, bf16[4,2,128,512]{3,2,1,0:T(8,128)(2,1)}, u32[]{:S(2)}, u32[]{:S(2)}) collective-permute-start(bf16[4,2,128,512]{3,2,1,0:T(8,128)(2,1)S(1)} %pad_maximum_fusion.refs_0_), channel_id=1, source_target_pairs={{0,1},{1,0},{2,3},{3,2},{4,5},{5,4},{6,7},{7,6},{8,9},{9,8},{10,11... | collective-permute-start | bytes 3145736 | tf_op jit(solution)/shard_map/ppermute | solution.py:25
  50.6 23.6 %collective-permute-start.9 = (bf16[4,2,128,512]{3,2,1,0:T(8,128)(2,1)S(1)}, bf16[4,2,128,512]{3,2,1,0:T(8,128)(2,1)}, u32[]{:S(2)}, u32[]{:S(2)}) collective-permute-start(bf16[4,2,128,512]{3,2,1,0:T(8,128)(2,1)S(1)} %collective-permute-done.5.refs_3_), channel_id=1, source_target_pairs={{0,1},{1,0},{2,3},{3,2},{4,5},{5,4},{6,7},{7,6},{8,9},{9,8},{10,11... | collective-permute-start | bytes 3145736 | tf_op jit(solution)/shard_map/ppermute | solution.py:25
  61.4 15.9 %collective-permute-start.8 = (bf16[4,2,128,512]{3,2,1,0:T(8,128)(2,1)S(1)}, bf16[4,2,128,512]{3,2,1,0:T(8,128)(2,1)}, u32[]{:S(2)}, u32[]{:S(2)}) collective-permute-start(bf16[4,2,128,512]{3,2,1,0:T(8,128)(2,1)S(1)} %collective-permute-done.4.refs_2_), channel_id=1, source_target_pairs={{0,1},{1,0},{2,3},{3,2},{4,5},{5,4},{6,7},{7,6},{8,9},{9,8},{10,11... | collective-permute-start | bytes 3145736 | tf_op jit(solution)/shard_map/ppermute | solution.py:25
  73.5 4.1 %collective-permute-start.7 = (bf16[4,2,128,512]{3,2,1,0:T(8,128)(2,1)}, bf16[4,2,128,512]{3,2,1,0:T(8,128)(2,1)}, u32[]{:S(2)}, u32[]{:S(2)}) collective-permute-start(bf16[4,2,128,512]{3,2,1,0:T(8,128)(2,1)} %collective-permute-done.3.refs_1_), channel_id=1, source_target_pairs={{0,1},{1,0},{2,3},{3,2},{4,5},{5,4},{6,7},{7,6},{8,9},{9,8},{10,11... | collective-permute-start | bytes 3145736 | tf_op jit(solution)/shard_map/ppermute | solution.py:25
  77.7 2.2 %copy-start = (bf16[16,2,4,128,128]{4,3,2,1,0:T(8,128)(2,1)S(1)}, bf16[16,2,4,128,128]{4,3,2,1,0:T(8,128)(2,1)}, u32[]{:S(2)}) copy-start(bf16[16,2,4,128,128]{4,3,2,1,0:T(8,128)(2,1)} %all-gather.3.cloned.1.call-done) | copy-start | bytes 12582916
  93.5 2.0 %copy-start.2 = (bf16[8,2,2,4,128,128]{5,4,3,2,1,0:T(8,128)(2,1)}, bf16[8,2,2,4,128,128]{5,4,3,2,1,0:T(8,128)(2,1)S(1)}, u32[]{:S(2)}) copy-start(bf16[8,2,2,4,128,128]{5,4,3,2,1,0:T(8,128)(2,1)S(1)} %get-tuple-element.9) | copy-start | bytes 12582916
  96.2 0.9 copy-start.4
  97.2 2.2 %copy-start.1 = (bf16[16,2,4,128,128]{4,3,2,1,0:T(8,128)(2,1)S(1)}, bf16[16,2,4,128,128]{4,3,2,1,0:T(8,128)(2,1)}, u32[]{:S(2)}) copy-start(bf16[16,2,4,128,128]{4,3,2,1,0:T(8,128)(2,1)} %all-gather.3.cloned.1.call-done) | copy-start | bytes 12582916
  106.5 3.0 %collective-permute-start.16 = (bf16[4,2,128,512]{3,2,1,0:T(8,128)(2,1)S(1)}, bf16[4,2,128,512]{3,2,1,0:T(8,128)(2,1)S(1)}, u32[]{:S(2)}, u32[]{:S(2)}) collective-permute-start(bf16[4,2,128,512]{3,2,1,0:T(8,128)(2,1)S(1)} %get-tuple-element.23), channel_id=1, source_target_pairs={{0,1},{1,0},{2,3},{3,2},{4,5},{5,4},{6,7},{7,6},{8,9},{9,8},{10,11... | collective-permute-start | bytes 3145736 | tf_op jit(solution)/shard_map/ppermute | solution.py:25
  107.3 3.8 %collective-permute-start.14 = (bf16[4,2,128,512]{3,2,1,0:T(8,128)(2,1)S(1)}, bf16[4,2,128,512]{3,2,1,0:T(8,128)(2,1)S(1)}, u32[]{:S(2)}, u32[]{:S(2)}) collective-permute-start(bf16[4,2,128,512]{3,2,1,0:T(8,128)(2,1)S(1)} %get-tuple-element.24), channel_id=1, source_target_pairs={{0,1},{1,0},{2,3},{3,2},{4,5},{5,4},{6,7},{7,6},{8,9},{9,8},{10,11... | collective-permute-start | bytes 3145736 | tf_op jit(solution)/shard_map/ppermute | solution.py:25
  107.4 5.2 %collective-permute-start.12 = (bf16[4,2,128,512]{3,2,1,0:T(8,128)(2,1)S(1)}, bf16[4,2,128,512]{3,2,1,0:T(8,128)(2,1)S(1)}, u32[]{:S(2)}, u32[]{:S(2)}) collective-permute-start(bf16[4,2,128,512]{3,2,1,0:T(8,128)(2,1)S(1)} %get-tuple-element.25), channel_id=1, source_target_pairs={{0,1},{1,0},{2,3},{3,2},{4,5},{5,4},{6,7},{7,6},{8,9},{9,8},{10,11... | collective-permute-start | bytes 3145736 | tf_op jit(solution)/shard_map/ppermute | solution.py:25
  107.8 10.2 %collective-permute-start.11 = (bf16[4,2,128,512]{3,2,1,0:T(8,128)(2,1)S(1)}, bf16[4,2,128,512]{3,2,1,0:T(8,128)(2,1)S(1)}, u32[]{:S(2)}, u32[]{:S(2)}) collective-permute-start(bf16[4,2,128,512]{3,2,1,0:T(8,128)(2,1)S(1)} %get-tuple-element.22), channel_id=1, source_target_pairs={{0,1},{1,0},{2,3},{3,2},{4,5},{5,4},{6,7},{7,6},{8,9},{9,8},{10,11... | collective-permute-start | bytes 3145736 | tf_op jit(solution)/shard_map/ppermute | solution.py:25
  113.8 15.6 %collective-permute-start.13 = (bf16[4,2,128,512]{3,2,1,0:T(8,128)(2,1)S(1)}, bf16[4,2,128,512]{3,2,1,0:T(8,128)(2,1)S(1)}, u32[]{:S(2)}, u32[]{:S(2)}) collective-permute-start(bf16[4,2,128,512]{3,2,1,0:T(8,128)(2,1)S(1)} %get-tuple-element.26), channel_id=1, source_target_pairs={{0,128},{1,9},{2,130},{3,11},{4,132},{5,13},{6,134},{7,15},{8,136}... | collective-permute-start | bytes 3145736 | tf_op jit(solution)/shard_map/ppermute | solution.py:25
  116.5 24.1 %collective-permute-start.17 = (bf16[4,2,128,512]{3,2,1,0:T(8,128)(2,1)S(1)}, bf16[4,2,128,512]{3,2,1,0:T(8,128)(2,1)S(1)}, u32[]{:S(2)}, u32[]{:S(2)}) collective-permute-start(bf16[4,2,128,512]{3,2,1,0:T(8,128)(2,1)S(1)} %get-tuple-element.27), channel_id=1, source_target_pairs={{0,130},{1,13},{2,0},{3,15},{4,134},{5,1},{6,4},{7,3},{8,138},{9,5... | collective-permute-start | bytes 3145736 | tf_op jit(solution)/shard_map/ppermute | solution.py:25
  117.4 23.3 %collective-permute-start.15 = (bf16[4,2,128,512]{3,2,1,0:T(8,128)(2,1)S(1)}, bf16[4,2,128,512]{3,2,1,0:T(8,128)(2,1)S(1)}, u32[]{:S(2)}, u32[]{:S(2)}) collective-permute-start(bf16[4,2,128,512]{3,2,1,0:T(8,128)(2,1)S(1)} %get-tuple-element.28), channel_id=1, source_target_pairs={{0,2},{1,5},{2,128},{3,7},{4,6},{5,9},{6,132},{7,11},{8,10},{9,13}... | collective-permute-start | bytes 3145736 | tf_op jit(solution)/shard_map/ppermute | solution.py:25
  141.6 13.7 %collective-permute-start.18 = (bf16[2,128,512]{2,1,0:T(8,128)(2,1)S(1)}, bf16[2,128,512]{2,1,0:T(8,128)(2,1)S(1)}, u32[]{:S(2)}, u32[]{:S(2)}) collective-permute-start(bf16[2,128,512]{2,1,0:T(8,128)(2,1)S(1)} %get-tuple-element.31), channel_id=1, source_target_pairs={{0,8},{1,129},{2,10},{3,131},{4,12},{5,133},{6,14},{7,135},{8,0},{... | collective-permute-start | bytes 786440 | tf_op jit(solution)/shard_map/ppermute | solution.py:25
  144.4 10.8 %collective-permute-start.20 = (bf16[2,128,512]{2,1,0:T(8,128)(2,1)S(1)}, bf16[2,128,512]{2,1,0:T(8,128)(2,1)S(1)}, u32[]{:S(2)}, u32[]{:S(2)}) collective-permute-start(bf16[2,128,512]{2,1,0:T(8,128)(2,1)S(1)} %get-tuple-element.32), channel_id=1, source_target_pairs={{0,12},{1,131},{2,14},{3,1},{4,0},{5,135},{6,2},{7,5},{8,4},{9,139... | collective-permute-start | bytes 786440 | tf_op jit(solution)/shard_map/ppermute | solution.py:25
  145.2 10.0 %collective-permute-start.19 = (bf16[2,128,512]{2,1,0:T(8,128)(2,1)S(1)}, bf16[2,128,512]{2,1,0:T(8,128)(2,1)S(1)}, u32[]{:S(2)}, u32[]{:S(2)}) collective-permute-start(bf16[2,128,512]{2,1,0:T(8,128)(2,1)S(1)} %get-tuple-element.33), channel_id=1, source_target_pairs={{0,4},{1,3},{2,6},{3,129},{4,8},{5,7},{6,10},{7,133},{8,12},{9,11}... | collective-permute-start | bytes 786440 | tf_op jit(solution)/shard_map/ppermute | solution.py:25
  152.4 8.8 %collective-permute-start.21 = (bf16[2,4,128,128]{3,2,1,0:T(8,128)(2,1)S(1)}, bf16[2,4,128,128]{3,2,1,0:T(8,128)(2,1)S(1)}, u32[]{:S(2)}, u32[]{:S(2)}) collective-permute-start(bf16[2,4,128,128]{3,2,1,0:T(8,128)(2,1)S(1)} %get-tuple-element.35), channel_id=1, source_target_pairs={{0,128},{1,129},{2,130},{3,131},{4,132},{5,133},{6,134},{7,135},{8... | collective-permute-start | bytes 786440 | tf_op jit(solution)/shard_map/ppermute | solution.py:25
  (1 other events, 0.7 us)
Sparse Core Ops, SparseCore 0:
  18.2 59.4 all-gather.2
  96.4 54.9 reduce-scatter.1
where the time goes:
time: 170 us
  starting transfers between devices  63.9 us (38%)
  waiting for transfers between devices  54.4 us (32%)
  Pallas kernels  20.5 us (12%)
  between operations  14.3 us (8%)
  local copies, waits for them, and re-layouts  11.2 us (7%)
  other arithmetic  5.85 us (3%)
    ppermute x22, starting transfers between devices, send(): lax.ppermute(value, AXES, [(source, place_of(*step(*where_is(source)))) f...  63.8 us
    ppermute x22, waiting for transfers between devices, send(): lax.ppermute(value, AXES, [(source, place_of(*step(*where_is(source)))) f...  48.8 us
    pallas_call x1, Pallas kernels, local(): pl.pallas_call(first_kernel, out_shape=[jax.ShapeDtypeStruct((4, 2 * B, B...  13.6 us
    unnamed x20, local copies, waits for them, and re-layouts  9.53 us
    pallas_call x1, Pallas kernels, local(): pl.pallas_call(second_kernel, out_shape=jax.ShapeDtypeStruct((8, 4, 2, B,...  6.91 us
    reduce_scatter x1, waiting for transfers between devices, local(): lax.psum_scatter(grads, 'dp', scatter_dimension=0, axis_index_groups=HALV...  5.46 us
  transfers between devices with their start and end apart: 24, of which 13 were waited for; matrix products, arithmetic and copies ran while one was open for 3% of the time, Pallas kernels for 4%

commit v1 on v0

--- a/solution.py
+++ b/solution.py
@@ -57,70 +57,99 @@
     return lax.dot_general(a, b, dims, preferred_element_type=jnp.float32)
 
 
-def first_kernel(spots, rows, *refs):
-    plane_in, w_in = refs[:8], refs[8]
-    act_out, gh_out, grads = refs[9:12]
-    xs, gs, ws, sem_x, sem_g, sem_w = refs[12:]
-
-    copies = []
-    for n in range(8):
-        for r in range(4):
-            spot = spots[n * 4 + r]
-            half = pl.ds(pl.multiple_of((spot % 2) * B, B), B)
-            for m, (scratch, sems) in enumerate(((xs, sem_x), (gs, sem_g))):
-                copies.append(
+def place_kernel(spots, *refs):
+    parts, x_out, g_out = refs[:8], refs[8], refs[9]
+    xs, gs, sem_x, sem_g, sem_out = refs[10:]
+    copies = ([], [])
+    for m, (scratch, sems) in enumerate(((xs, sem_x), (gs, sem_g))):
+        for n in range(8):
+            for r in range(4):
+                spot = spots[n * 4 + r]
+                half = pl.ds(pl.multiple_of((spot % 2) * B, B), B)
+                copies[m].append(
                     pltpu.make_async_copy(
-                        plane_in[n].at[r, m], scratch.at[spot // 2, half], sems.at[n * 4 + r]
+                        parts[n].at[r, m], scratch.at[spot // 2, half], sems.at[n * 4 + r]
                     )
                 )
-    copies.append(pltpu.make_async_copy(w_in, ws, sem_w))
-    for copy in copies:
+    for copy in copies[0] + copies[1]:
         copy.start()
-    for copy in copies:
-        copy.wait()
+    stores = (
+        pltpu.make_async_copy(xs, x_out, sem_out.at[0]),
+        pltpu.make_async_copy(gs, g_out, sem_out.at[1]),
+    )
+    for m in range(2):
+        for copy in copies[m]:
+            copy.wait()
+        stores[m].start()
+    for store in stores:
+        store.wait()
+
+
+def first_kernel(rows, x_in, g_in, w_in, act_out, gh_out, grads_out, *scratch):
+    xs, gs, ws, grads, sem_x, sem_g, sem_in, sem_out = scratch
+
+    def store(j):
+        return pltpu.make_async_copy(grads.at[j], grads_out.at[:, :, :, j], sem_out.at[j])
+
+    def load_w(j):
+        return pltpu.make_async_copy(w_in.at[:, :, :, j], ws.at[j], sem_in.at[j])
+
+    def load(j):
+        for source, target, sems in ((x_in, xs, sem_x), (g_in, gs, sem_g)):
+            for s in range(8):
+                for half in range(2):
+                    p = rows[j, half * 8 + s]
+                    lanes = pl.ds(pl.multiple_of((p % 4) * B, B), B)
+                    pltpu.make_async_copy(
+                        source.at[p // 4, :, lanes], target.at[j, s, half], sems.at[j]
+                    ).start()
+        load_w(j).start()
 
     def pick(scratch, j, s):
-        p = rows[j, s]
-        q = rows[j, 8 + s]
-        return jnp.concatenate(
-            [
-                scratch[p // 4, :, pl.ds(pl.multiple_of((p % 4) * B, B), B)],
-                scratch[q // 4, :, pl.ds(pl.multiple_of((q % 4) * B, B), B)],
-            ],
-            axis=1,
-        )
+        return jnp.concatenate([scratch[j, s, 0], scratch[j, s, 1]], axis=1)
 
     def column(j, carry):
+        pl.when(j < 3)(lambda: load(j + 1))
+        for target, sems in ((xs, sem_x), (gs, sem_g)):
+            pltpu.make_async_copy(target.at[j], target.at[j], sems.at[j]).wait()
+        load_w(j).wait()
         hidden = jnp.zeros((2 * B, B), jnp.float32)
         grad_act = jnp.zeros((2 * B, B), jnp.float32)
         for s in range(8):
-            up = jnp.concatenate([ws[s, 0, 0, j], ws[s, 1, 0, j]], axis=0)
+            up = jnp.concatenate([ws[j, s, 0, 0], ws[j, s, 1, 0]], axis=0)
             hidden += dot(pick(xs, j, s), up)
-            down = jnp.concatenate([ws[s, 0, 1, j], ws[s, 1, 1, j]], axis=1)
+            down = jnp.concatenate([ws[j, s, 0, 1], ws[j, s, 1, 1]], axis=1)
             grad_act += dot(pick(gs, j, s), down, NT)
         value, slope = gelu_parts(hidden)
-        act = value.astype(jnp.bfloat16)
-        gh = (slope * grad_act).astype(jnp.bfloat16)
-        act_out[j] = act
-        gh_out[j] = gh
+        grad_hidden = slope * grad_act
+        act_out[j] = value.astype(jnp.bfloat16)
+        gh_out[j] = grad_hidden.astype(jnp.bfloat16)
         act_t = value.T.astype(jnp.bfloat16)
-        gh_t = (slope * grad_act).T.astype(jnp.bfloat16)
+        gh_t = grad_hidden.T.astype(jnp.bfloat16)
         for s in range(8):
             up = dot(gh_t, pick(xs, j, s)).astype(jnp.bfloat16)
-            grads[s, 0, 0, j] = up[:, :B]
-            grads[s, 1, 0, j] = up[:, B:]
+            grads[j, s, 0, 0] = up[:, :B]
+            grads[j, s, 1, 0] = up[:, B:]
             down = dot(act_t, pick(gs, j, s)).astype(jnp.bfloat16)
-            grads[s, 0, 1, j] = down[:, :B]
-            grads[s, 1, 1, j] = down[:, B:]
+            grads[j, s, 0, 1] = down[:, :B]
+            grads[j, s, 1, 1] = down[:, B:]
+        store(j).start()
         return carry
 
+    load(0)
     lax.fori_loop(0, 4, column, 0)
+    for j in range(4):
+        store(j).wait()
 
 
 def second_kernel(outs_at, rows, act_ref, gh_ref, *refs):
     w_in, parts, ws, out_acc, in_acc, sem_w = refs
-    load = pltpu.make_async_copy(w_in, ws, sem_w)
-    load.start()
+
+    def load(j):
+        return pltpu.make_async_copy(w_in.at[:, :, :, j], ws.at[j], sem_w.at[j])
+
+    for j in range(4):
+        load(j).start()
 
     def clear(p, carry):
         out_acc[p] = jnp.zeros((2 * B, B), jnp.float32)
@@ -128,19 +157,19 @@
         return carry
 
     lax.fori_loop(0, 64, clear, 0)
-    load.wait()
 
     def column(j, carry):
+        load(j).wait()
         act = act_ref[j]
         gh = gh_ref[j]
         for s in range(8):
             p = rows[j, s]
             q = rows[j, 8 + s]
-            down = jnp.concatenate([ws[s, 0, 1, j], ws[s, 1, 1, j]], axis=1)
+            down = jnp.concatenate([ws[j, s, 0, 1], ws[j, s, 1, 1]], axis=1)
             term = dot(act, down)
             out_acc[p] += term[:, :B]
             out_acc[q] += term[:, B:]
-            up = jnp.concatenate([ws[s, 0, 0, j], ws[s, 1, 0, j]], axis=0)
+            up = jnp.concatenate([ws[j, s, 0, 0], ws[j, s, 1, 0]], axis=0)
             term = dot(gh, up, NT)
             in_acc[p] += term[:, :B]
             in_acc[q] += term[:, B:]
@@ -163,6 +192,7 @@
 SMEM = pl.BlockSpec(memory_space=pltpu.SMEM)
 VMEM = pl.BlockSpec(memory_space=pltpu.VMEM)
 ANY = pl.BlockSpec(memory_space=pl.ANY)
+HBM = pl.BlockSpec(memory_space=pltpu.HBM)
 HALVES = [list(range(8)), list(range(8, 16))]
 STEPS = (0, 1, 3, 2)
 
@@ -218,31 +248,52 @@
     both = jnp.stack([w_up[:, 0], w_down[:, 0]])
     piece_a = lax.dynamic_slice_in_dim(both, yh * 4, 4, 1)
     piece_b = lax.dynamic_slice_in_dim(both, (1 - yh) * 4, 4, 1)
+    other_b = send(piece_b, other_half)
     plane = gather_plane(jnp.stack([tokens, cotangent]))
     weights = lax.all_gather(
-        jnp.stack([piece_a, send(piece_b, other_half)]), "dp", axis_index_groups=HALVES
-    )
-
+        jnp.stack([piece_a, other_b]), "dp", axis_index_groups=HALVES
+    )
+
+    gathered = jax.ShapeDtypeStruct((16, 2 * B, 4 * B), bf16)
+    xs, gs = pl.pallas_call(
+        place_kernel,
+        out_shape=[gathered] * 2,
+        in_specs=[SMEM] + [ANY] * 8,
+        out_specs=[HBM] * 2,
+        scratch_shapes=[
+            pltpu.VMEM((16, 2 * B, 4 * B), bf16),
+            pltpu.VMEM((16, 2 * B, 4 * B), bf16),
+            pltpu.SemaphoreType.DMA((32,)),
+            pltpu.SemaphoreType.DMA((32,)),
+            pltpu.SemaphoreType.DMA((2,)),
+        ],
+        compiler_params=pltpu.CompilerParams(vmem_limit_bytes=56 * MIB),
+        cost_estimate=pl.CostEstimate(flops=0, bytes_accessed=16 * MIB, transcendentals=0),
+        name="place",
+    )(spots, *plane)
     act, gh, grads = pl.pallas_call(
         first_kernel,
         out_shape=[jax.ShapeDtypeStruct((4, 2 * B, B), bf16)] * 2
         + [jax.ShapeDtypeStruct((8, 2, 2, 4, B, B), bf16)],
-        in_specs=[SMEM, SMEM] + [ANY] * 9,
-        out_specs=[VMEM] * 3,
+        in_specs=[SMEM, HBM, HBM, HBM],
+        out_specs=[VMEM, VMEM, HBM],
         scratch_shapes=[
-            pltpu.VMEM((16, 2 * B, 4 * B), bf16),
-            pltpu.VMEM((16, 2 * B, 4 * B), bf16),
-            pltpu.VMEM((8, 2, 2, 4, B, B), bf16),
-            pltpu.SemaphoreType.DMA((32,)),
-            pltpu.SemaphoreType.DMA((32,)),
-            pltpu.SemaphoreType.DMA,
+            pltpu.VMEM((4, 8, 2, 2 * B, B), bf16),
+            pltpu.VMEM((4, 8, 2, 2 * B, B), bf16),
+            pltpu.VMEM((4, 8, 2, 2, B, B), bf16),
+            pltpu.VMEM((4, 8, 2, 2, B, B), bf16),
+            pltpu.SemaphoreType.DMA((4,)),
+            pltpu.SemaphoreType.DMA((4,)),
+            pltpu.SemaphoreType.DMA((4,)),
+            pltpu.SemaphoreType.DMA((4,)),
         ],
-        compiler_params=pltpu.CompilerParams(vmem_limit_bytes=18 * MIB),
+        compiler_params=pltpu.CompilerParams(vmem_limit_bytes=58 * MIB),
         cost_estimate=pl.CostEstimate(
             flops=2_000_000_000, bytes_accessed=16 * MIB, transcendentals=0
         ),
         name="first",
-    )(spots, rows, *plane, weights)
+    )(rows, xs, gs, weights)
+
     summed = lax.psum_scatter(
         grads, "dp", scatter_dimension=0, axis_index_groups=HALVES, tiled=True
     )[0]
@@ -250,13 +301,13 @@
     parts = pl.pallas_call(
         second_kernel,
         out_shape=jax.ShapeDtypeStruct((8, 4, 2, B, 4 * B), bf16),
-        in_specs=[SMEM, SMEM, VMEM, VMEM, ANY],
+        in_specs=[SMEM, SMEM, VMEM, VMEM, HBM],
         out_specs=VMEM,
         scratch_shapes=[
-            pltpu.VMEM((8, 2, 2, 4, B, B), bf16),
+            pltpu.VMEM((4, 8, 2, 2, B, B), bf16),
             pltpu.VMEM((64, 2 * B, B), f32),
             pltpu.VMEM((64, 2 * B, B), f32),
-            pltpu.SemaphoreType.DMA,
+            pltpu.SemaphoreType.DMA((4,)),
         ],
         compiler_params=pltpu.CompilerParams(vmem_limit_bytes=24 * MIB),
         cost_estimate=pl.CostEstimate(

time: 170 us -> 162 us (0.953)
  starting transfers between devices: 63.9 us -> 38.1 us
  waiting for transfers between devices: 54.4 us -> 69.7 us
  Pallas kernels: 20.5 us -> 26.6 us
  local copies, waits for them, and re-layouts: 11.2 us -> 6.4 us
    ppermute x22, starting transfers between devices: 63.8 us -> 38 us  [send(): lax.ppermute(value, AXES, [(source, place_of(*step(*where_is(source)))) f...]
    ppermute x22, waiting for transfers between devices: 48.8 us -> 60.5 us  [send(): lax.ppermute(value, AXES, [(source, place_of(*step(*where_is(source)))) f...]
    pallas_call x0 -> x1, Pallas kernels: none -> 8.19 us  [local(): pl.pallas_call(place_kernel, out_shape=[gathered] * 2, in_specs=[SMEM] +...]
    all_gather x1, waiting for transfers between devices: 0.07 us -> 6.05 us  [local(): lax.all_gather(jnp.stack([piece_a, other_b]), 'dp', axis_index_groups=HAL...]
    unnamed x20 -> x24, local copies, waits for them, and re-layouts: 9.53 us -> 4.69 us
    reduce_scatter x1, waiting for transfers between devices: 5.46 us -> 3.11 us  [local(): lax.psum_scatter(grads, 'dp', scatter_dimension=0, axis_index_groups=HALV...]
    pallas_call x1, Pallas kernels: 13.6 us -> 11.3 us  [local(): pl.pallas_call(first_kernel, out_shape=[jax.ShapeDtypeStruct((4, 2 * B, B...]
  transfers between devices with their start and end apart: 24 -> 24, of which waited for: 13 -> 17; matrix products, arithmetic and copies ran while one was open for 3% -> 4% of each run, Pallas kernels for 4% -> 9%
where the time goes in v1:
time: 162 us
  waiting for transfers between devices  69.7 us (43%)
  starting transfers between devices  38.1 us (24%)
  Pallas kernels  26.6 us (16%)
  between operations  14.3 us (9%)
  other arithmetic  6.93 us (4%)
  local copies, waits for them, and re-layouts  6.4 us (4%)
    ppermute x22, waiting for transfers between devices, send(): lax.ppermute(value, AXES, [(source, place_of(*step(*where_is(source)))) f...  60.5 us
    ppermute x22, starting transfers between devices, send(): lax.ppermute(value, AXES, [(source, place_of(*step(*where_is(source)))) f...  38 us
    pallas_call x1, Pallas kernels, local(): pl.pallas_call(first_kernel, out_shape=[jax.ShapeDtypeStruct((4, 2 * B, B...  11.3 us
    pallas_call x1, Pallas kernels, local(): pl.pallas_call(place_kernel, out_shape=[gathered] * 2, in_specs=[SMEM] +...  8.19 us
    pallas_call x1, Pallas kernels, local(): pl.pallas_call(second_kernel, out_shape=jax.ShapeDtypeStruct((8, 4, 2, B,...  7.04 us
    all_gather x1, waiting for transfers between devices, local(): lax.all_gather(jnp.stack([piece_a, other_b]), 'dp', axis_index_groups=HAL...  6.05 us
    unnamed x24, local copies, waits for them, and re-layouts  4.69 us
  transfers between devices with their start and end apart: 24, of which 17 were waited for; matrix products, arithmetic and copies ran while one was open for 4% of the time, Pallas kernels for 9%

profile of v1, /device:TPU:1, one launch (start us, length us, event | category | flops | bytes accessed | tf_op | source)
XLA Modules:
  0.0 162.0 jit_solution(4782429026447448806)
XLA Ops:
  8.4 3.8 %collective-permute-start.10 = (bf16[2,4,128,128]{3,2,1,0:T(8,128)(2,1)S(1)}, bf16[2,4,128,128]{3,2,1,0:T(8,128)(2,1)S(1)}, u32[]{:S(2)}, u32[]{:S(2)}) collective-permute-start(bf16[2,4,128,128]{3,2,1,0:T(8,128)(2,1)S(1)} %get-tuple-element.41), channel_id=1, source_target_pairs={{0,128},{1,129},{2,130},{3,131},{4,132},{5,133},{6,134},{7,135},{8... | collective-permute-start | bytes 786440 | tf_op jit(solution)/shard_map/ppermute | solution.py:25
  12.3 5.0 %collective-permute-done.10 = bf16[2,4,128,128]{3,2,1,0:T(8,128)(2,1)S(1)} collective-permute-done((bf16[2,4,128,128]{3,2,1,0:T(8,128)(2,1)S(1)}, bf16[2,4,128,128]{3,2,1,0:T(8,128)(2,1)S(1)}, u32[]{:S(2)}, u32[]{:S(2)}) %collective-permute-start.10) | collective-permute-done | bytes 262176 | tf_op jit(solution)/shard_map/ppermute | solution.py:25
  18.2 2.2 %collective-permute-start = (bf16[2,128,512]{2,1,0:T(8,128)(2,1)S(1)}, bf16[2,128,512]{2,1,0:T(8,128)(2,1)S(1)}, u32[]{:S(2)}, u32[]{:S(2)}) collective-permute-start(bf16[2,128,512]{2,1,0:T(8,128)(2,1)S(1)} %get-tuple-element.45), channel_id=1, source_target_pairs={{0,4},{1,3},{2,6},{3,129},{4,8},{5,7},{6,10},{7,133},{8,12},{9,11}... | collective-permute-start | bytes 786440 | tf_op jit(solution)/shard_map/ppermute | solution.py:25
  20.4 1.5 collective-permute-start.1
  21.9 1.6 collective-permute-start.2
  23.5 2.4 %collective-permute-done = bf16[2,128,512]{2,1,0:T(8,128)(2,1)S(1)} collective-permute-done((bf16[2,128,512]{2,1,0:T(8,128)(2,1)S(1)}, bf16[2,128,512]{2,1,0:T(8,128)(2,1)S(1)}, u32[]{:S(2)}, u32[]{:S(2)}) %collective-permute-start) | collective-permute-done | bytes 262176 | tf_op jit(solution)/shard_map/ppermute | solution.py:25
  25.9 2.2 %collective-permute-done.1 = bf16[2,128,512]{2,1,0:T(8,128)(2,1)S(1)} collective-permute-done((bf16[2,128,512]{2,1,0:T(8,128)(2,1)S(1)}, bf16[2,128,512]{2,1,0:T(8,128)(2,1)S(1)}, u32[]{:S(2)}, u32[]{:S(2)}) %collective-permute-start.1) | collective-permute-done | bytes 262176 | tf_op jit(solution)/shard_map/ppermute | solution.py:25
  28.0 1.8 %collective-permute-done.2 = bf16[2,128,512]{2,1,0:T(8,128)(2,1)S(1)} collective-permute-done((bf16[2,128,512]{2,1,0:T(8,128)(2,1)S(1)}, bf16[2,128,512]{2,1,0:T(8,128)(2,1)S(1)}, u32[]{:S(2)}, u32[]{:S(2)}) %collective-permute-start.2) | collective-permute-done | bytes 262176 | tf_op jit(solution)/shard_map/ppermute | solution.py:25
  31.0 1.8 %collective-permute-start.4 = (bf16[4,2,128,512]{3,2,1,0:T(8,128)(2,1)S(1)}, bf16[4,2,128,512]{3,2,1,0:T(8,128)(2,1)S(1)}, u32[]{:S(2)}, u32[]{:S(2)}) collective-permute-start(bf16[4,2,128,512]{3,2,1,0:T(8,128)(2,1)S(1)} %pad_maximum_fusion.refs_0_), channel_id=1, source_target_pairs={{0,130},{1,13},{2,0},{3,15},{4,134},{5,1},{6,4},{7,3},{8,138},{9,5... | collective-permute-start | bytes 3145736 | tf_op jit(solution)/shard_map/ppermute | solution.py:25
  34.0 3.5 %collective-permute-start.6 = (bf16[4,2,128,512]{3,2,1,0:T(8,128)(2,1)S(1)}, bf16[4,2,128,512]{3,2,1,0:T(8,128)(2,1)}, u32[]{:S(2)}, u32[]{:S(2)}) collective-permute-start(bf16[4,2,128,512]{3,2,1,0:T(8,128)(2,1)S(1)} %pad_maximum_fusion.refs_0_), channel_id=1, source_target_pairs={{0,1},{1,0},{2,3},{3,2},{4,5},{5,4},{6,7},{7,6},{8,9},{9,8},{10,11... | collective-permute-start | bytes 3145736 | tf_op jit(solution)/shard_map/ppermute | solution.py:25
  37.5 7.9 %collective-permute-done.3.refs_1_ = bf16[4,2,128,512]{3,2,1,0:T(8,128)(2,1)S(1)} collective-permute-done((bf16[4,2,128,512]{3,2,1,0:T(8,128)(2,1)S(1)}, bf16[4,2,128,512]{3,2,1,0:T(8,128)(2,1)S(1)}, u32[]{:S(2)}, u32[]{:S(2)}) %collective-permute-start.3) | collective-permute-done | bytes 1048608 | tf_op jit(solution)/shard_map/ppermute | solution.py:25
  45.4 2.9 %collective-permute-start.7 = (bf16[4,2,128,512]{3,2,1,0:T(8,128)(2,1)S(1)}, bf16[4,2,128,512]{3,2,1,0:T(8,128)(2,1)}, u32[]{:S(2)}, u32[]{:S(2)}) collective-permute-start(bf16[4,2,128,512]{3,2,1,0:T(8,128)(2,1)S(1)} %collective-permute-done.3.refs_1_), channel_id=1, source_target_pairs={{0,1},{1,0},{2,3},{3,2},{4,5},{5,4},{6,7},{7,6},{8,9},{9,8},{10,11... | collective-permute-start | bytes 3145736 | tf_op jit(solution)/shard_map/ppermute | solution.py:25
  48.3 7.5 %collective-permute-done.4.refs_2_ = bf16[4,2,128,512]{3,2,1,0:T(8,128)(2,1)S(1)} collective-permute-done((bf16[4,2,128,512]{3,2,1,0:T(8,128)(2,1)S(1)}, bf16[4,2,128,512]{3,2,1,0:T(8,128)(2,1)S(1)}, u32[]{:S(2)}, u32[]{:S(2)}) %collective-permute-start.4) | collective-permute-done | bytes 1048608 | tf_op jit(solution)/shard_map/ppermute | solution.py:25
  55.8 1.8 %collective-permute-done.5.refs_3_ = bf16[4,2,128,512]{3,2,1,0:T(8,128)(2,1)} collective-permute-done((bf16[4,2,128,512]{3,2,1,0:T(8,128)(2,1)S(1)}, bf16[4,2,128,512]{3,2,1,0:T(8,128)(2,1)}, u32[]{:S(2)}, u32[]{:S(2)}) %collective-permute-start.5) | collective-permute-done | bytes 1048608 | tf_op jit(solution)/shard_map/ppermute | solution.py:25
  57.6 3.3 %collective-permute-start.9 = (bf16[4,2,128,512]{3,2,1,0:T(8,128)(2,1)}, bf16[4,2,128,512]{3,2,1,0:T(8,128)(2,1)}, u32[]{:S(2)}, u32[]{:S(2)}) collective-permute-start(bf16[4,2,128,512]{3,2,1,0:T(8,128)(2,1)} %collective-permute-done.5.refs_3_), channel_id=1, source_target_pairs={{0,1},{1,0},{2,3},{3,2},{4,5},{5,4},{6,7},{7,6},{8,9},{9,8},{10,11... | collective-permute-start | bytes 3145736 | tf_op jit(solution)/shard_map/ppermute | solution.py:25
  63.5 8.2 %place.1 = (bf16[16,256,512]{2,1,0:T(8,128)(2,1)}, bf16[16,256,512]{2,1,0:T(8,128)(2,1)}) custom-call(s32[32]{0:T(128)} %pad_add_fusion.spots, bf16[4,2,128,512]{3,2,1,0:T(8,128)(2,1)} %copy-done.4, bf16[4,2,128,512]{3,2,1,0:T(8,128)(2,1)} %copy-done.5, bf16[4,2,128,512]{3,2,1,0:T(8,128)(2,1)} %copy-done.6, ...), custom_call_target="tpu_custom_call" | custom-call | bytes 16777216 | tf_op jit(solution)/shard_map/place/pallas_call | solution.py:258
  71.7 6.1 %all-gather.3.cloned.1.call-done = bf16[16,2,4,128,128]{4,3,2,1,0:T(8,128)(2,1)} async-done(((bf16[2,2,4,128,128]{4,3,2,1,0:T(8,128)(2,1)}), bf16[16,2,4,128,128]{4,3,2,1,0:T(8,128)(2,1)}) %all-gather.3.cloned.1.call-update) | async-done | bytes 4194320 | tf_op jit(solution)/shard_map/all_gather | solution.py:253
  77.7 11.3 %first.1 = (bf16[4,256,128]{2,1,0:T(8,128)(2,1)}, bf16[4,256,128]{2,1,0:T(8,128)(2,1)}, bf16[8,2,2,4,128,128]{5,4,3,2,1,0:T(8,128)(2,1)}) custom-call(s32[4,16]{1,0:T(4,128)} %add_select_fusion.rows, bf16[16,256,512]{2,1,0:T(8,128)(2,1)} %get-tuple-element.9.x_in, bf16[16,256,512]{2,1,0:T(8,128)(2,1)} %get-tuple-element.10.g_in, ...), custom_call_target="tpu_custom_call" | custom-call | flops 2000000000 | bytes 16777216 | tf_op jit(solution)/shard_map/first/pallas_call | solution.py:274
  90.1 2.2 %copy-done = bf16[16,2,4,128,128]{4,3,2,1,0:T(8,128)(2,1)S(1)} copy-done((bf16[16,2,4,128,128]{4,3,2,1,0:T(8,128)(2,1)S(1)}, bf16[16,2,4,128,128]{4,3,2,1,0:T(8,128)(2,1)}, u32[]{:S(2)}) %copy-start) | copy-done | bytes 4194328
  92.3 7.0 %second.1 = bf16[8,4,2,128,512]{4,3,2,1,0:T(8,128)(2,1)S(1)} custom-call(s32[128]{0:T(128)S(1)} %add.279.outs_at, s32[4,16]{1,0:T(4,128)S(1)} %copy-done.3, bf16[4,256,128]{2,1,0:T(8,128)(2,1)S(1)} %copy-done.1, bf16[4,256,128]{2,1,0:T(8,128)(2,1)S(1)} %copy-done.2, bf16[8,2,2,4,128,128]{5,4,3,2,1,0:T(8,128)(2,1)S(1)} %bitcast.80), custom_call_target="tpu_custom_call" | custom-call | flops 1000000000 | bytes 16777216 | tf_op jit(solution)/shard_map/second/pallas_call | solution.py:301
  101.2 1.5 collective-permute-done.12
  102.7 1.5 collective-permute-done.14
  104.2 1.5 collective-permute-done.16
  106.8 2.8 %collective-permute-start.13 = (bf16[4,2,128,512]{3,2,1,0:T(8,128)(2,1)S(1)}, bf16[4,2,128,512]{3,2,1,0:T(8,128)(2,1)S(1)}, u32[]{:S(2)}, u32[]{:S(2)}) collective-permute-start(bf16[4,2,128,512]{3,2,1,0:T(8,128)(2,1)S(1)} %get-tuple-element.30), channel_id=1, source_target_pairs={{0,128},{1,9},{2,130},{3,11},{4,132},{5,13},{6,134},{7,15},{8,136}... | collective-permute-start | bytes 3145736 | tf_op jit(solution)/shard_map/ppermute | solution.py:25
  109.9 2.4 %collective-permute-start.17 = (bf16[4,2,128,512]{3,2,1,0:T(8,128)(2,1)S(1)}, bf16[4,2,128,512]{3,2,1,0:T(8,128)(2,1)S(1)}, u32[]{:S(2)}, u32[]{:S(2)}) collective-permute-start(bf16[4,2,128,512]{3,2,1,0:T(8,128)(2,1)S(1)} %get-tuple-element.31), channel_id=1, source_target_pairs={{0,130},{1,13},{2,0},{3,15},{4,134},{5,1},{6,4},{7,3},{8,138},{9,5... | collective-permute-start | bytes 3145736 | tf_op jit(solution)/shard_map/ppermute | solution.py:25
  112.3 10.1 %collective-permute-done.13 = bf16[4,2,128,512]{3,2,1,0:T(8,128)(2,1)S(1)} collective-permute-done((bf16[4,2,128,512]{3,2,1,0:T(8,128)(2,1)S(1)}, bf16[4,2,128,512]{3,2,1,0:T(8,128)(2,1)S(1)}, u32[]{:S(2)}, u32[]{:S(2)}) %collective-permute-start.13) | collective-permute-done | bytes 1048608 | tf_op jit(solution)/shard_map/ppermute | solution.py:25
  122.4 11.3 %collective-permute-done.15 = bf16[4,2,128,512]{3,2,1,0:T(8,128)(2,1)S(1)} collective-permute-done((bf16[4,2,128,512]{3,2,1,0:T(8,128)(2,1)S(1)}, bf16[4,2,128,512]{3,2,1,0:T(8,128)(2,1)S(1)}, u32[]{:S(2)}, u32[]{:S(2)}) %collective-permute-start.15) | collective-permute-done | bytes 1048608 | tf_op jit(solution)/shard_map/ppermute | solution.py:25
  134.6 2.8 %collective-permute-start.18 = (bf16[2,128,512]{2,1,0:T(8,128)(2,1)S(1)}, bf16[2,128,512]{2,1,0:T(8,128)(2,1)S(1)}, u32[]{:S(2)}, u32[]{:S(2)}) collective-permute-start(bf16[2,128,512]{2,1,0:T(8,128)(2,1)S(1)} %get-tuple-element.35), channel_id=1, source_target_pairs={{0,8},{1,129},{2,10},{3,131},{4,12},{5,133},{6,14},{7,135},{8,0},{... | collective-permute-start | bytes 786440 | tf_op jit(solution)/shard_map/ppermute | solution.py:25
  137.8 2.4 %collective-permute-start.20 = (bf16[2,128,512]{2,1,0:T(8,128)(2,1)S(1)}, bf16[2,128,512]{2,1,0:T(8,128)(2,1)S(1)}, u32[]{:S(2)}, u32[]{:S(2)}) collective-permute-start(bf16[2,128,512]{2,1,0:T(8,128)(2,1)S(1)} %get-tuple-element.36), channel_id=1, source_target_pairs={{0,12},{1,131},{2,14},{3,1},{4,0},{5,135},{6,2},{7,5},{8,4},{9,139... | collective-permute-start | bytes 786440 | tf_op jit(solution)/shard_map/ppermute | solution.py:25
  140.1 3.1 %reduce-scatter.2.cloned.1.call-done = bf16[1,2,2,4,128,128]{5,4,3,2,1,0:T(8,128)(2,1)} async-done(((bf16[8,2,2,4,128,128]{5,4,3,2,1,0:T(8,128)(2,1)}), bf16[1,2,2,4,128,128]{5,4,3,2,1,0:T(8,128)(2,1)}) %reduce-scatter.2.cloned.1.call-update) | async-done | bytes 524304 | tf_op jit(solution)/shard_map/reduce_scatter | solution.py:297
  144.3 2.8 %collective-permute-start.21 = (bf16[2,4,128,128]{3,2,1,0:T(8,128)(2,1)S(1)}, bf16[2,4,128,128]{3,2,1,0:T(8,128)(2,1)S(1)}, u32[]{:S(2)}, u32[]{:S(2)}) collective-permute-start(bf16[2,4,128,128]{3,2,1,0:T(8,128)(2,1)S(1)} %get-tuple-element.39), channel_id=1, source_target_pairs={{0,128},{1,129},{2,130},{3,131},{4,132},{5,133},{6,134},{7,135},{8... | collective-permute-start | bytes 786440 | tf_op jit(solution)/shard_map/ppermute | solution.py:25
  148.0 5.1 %collective-permute-done.21 = bf16[2,4,128,128]{3,2,1,0:T(8,128)(2,1)S(1)} collective-permute-done((bf16[2,4,128,128]{3,2,1,0:T(8,128)(2,1)S(1)}, bf16[2,4,128,128]{3,2,1,0:T(8,128)(2,1)S(1)}, u32[]{:S(2)}, u32[]{:S(2)}) %collective-permute-start.21) | collective-permute-done | bytes 262176 | tf_op jit(solution)/shard_map/ppermute | solution.py:25
  (75 shorter events, 16.6 us)
Async XLA Ops:
  7.2 11.0 %copy-start.8 = (bf16[128,512]{1,0:T(8,128)(2,1)S(1)}, bf16[128,512]{1,0:T(8,128)(2,1)}, u32[]{:S(2)}) copy-start(bf16[128,512]{1,0:T(8,128)(2,1)} %param.7) | copy-start | bytes 393220
  7.2 11.0 %copy-start.7 = (bf16[128,512]{1,0:T(8,128)(2,1)S(1)}, bf16[128,512]{1,0:T(8,128)(2,1)}, u32[]{:S(2)}) copy-start(bf16[128,512]{1,0:T(8,128)(2,1)} %param.11) | copy-start | bytes 393220
  7.2 70.5 %all-gather.3.cloned.1.call-start = ((), (), s32[]{:S(2)}) async-start(), calls=%async_computation.2 | async-start | bytes 4718592 | tf_op jit(solution)/shard_map/all_gather | solution.py:253
  8.4 8.8 %collective-permute-start.10 = (bf16[2,4,128,128]{3,2,1,0:T(8,128)(2,1)S(1)}, bf16[2,4,128,128]{3,2,1,0:T(8,128)(2,1)S(1)}, u32[]{:S(2)}, u32[]{:S(2)}) collective-permute-start(bf16[2,4,128,128]{3,2,1,0:T(8,128)(2,1)S(1)} %get-tuple-element.41), channel_id=1, source_target_pairs={{0,128},{1,129},{2,130},{3,131},{4,132},{5,133},{6,134},{7,135},{8... | collective-permute-start | bytes 786440 | tf_op jit(solution)/shard_map/ppermute | solution.py:25
  17.2 43.6 %copy-start.10 = (s32[4]{0:T(128)S(1)}, s32[4]{0:T(128)}, u32[]{:S(2)}) copy-start(s32[4]{0:T(128)} %constant.182.clone) | copy-start | bytes 52
  17.2 44.6 %copy-start.9 = (s32[8,16]{1,0:T(8,128)S(1)}, s32[8,16]{1,0:T(8,128)}, u32[]{:S(2)}) copy-start(s32[8,16]{1,0:T(8,128)} %param.8) | copy-start | bytes 1540
  18.1 125.1 %reduce-scatter.2.cloned.1.call-start = ((), (), s32[]{:S(2)}) async-start(), calls=%async_computation.1 | async-start | bytes 4718592 | tf_op jit(solution)/shard_map/reduce_scatter | solution.py:297
  18.2 7.7 %collective-permute-start = (bf16[2,128,512]{2,1,0:T(8,128)(2,1)S(1)}, bf16[2,128,512]{2,1,0:T(8,128)(2,1)S(1)}, u32[]{:S(2)}, u32[]{:S(2)}) collective-permute-start(bf16[2,128,512]{2,1,0:T(8,128)(2,1)S(1)} %get-tuple-element.45), channel_id=1, source_target_pairs={{0,4},{1,3},{2,6},{3,129},{4,8},{5,7},{6,10},{7,133},{8,12},{9,11}... | collective-permute-start | bytes 786440 | tf_op jit(solution)/shard_map/ppermute | solution.py:25
  20.4 7.7 %collective-permute-start.1 = (bf16[2,128,512]{2,1,0:T(8,128)(2,1)S(1)}, bf16[2,128,512]{2,1,0:T(8,128)(2,1)S(1)}, u32[]{:S(2)}, u32[]{:S(2)}) collective-permute-start(bf16[2,128,512]{2,1,0:T(8,128)(2,1)S(1)} %get-tuple-element.45), channel_id=1, source_target_pairs={{0,12},{1,131},{2,14},{3,1},{4,0},{5,135},{6,2},{7,5},{8,4},{9,139... | collective-permute-start | bytes 786440 | tf_op jit(solution)/shard_map/ppermute | solution.py:25
  21.9 8.0 %collective-permute-start.2 = (bf16[2,128,512]{2,1,0:T(8,128)(2,1)S(1)}, bf16[2,128,512]{2,1,0:T(8,128)(2,1)S(1)}, u32[]{:S(2)}, u32[]{:S(2)}) collective-permute-start(bf16[2,128,512]{2,1,0:T(8,128)(2,1)S(1)} %get-tuple-element.45), channel_id=1, source_target_pairs={{0,8},{1,129},{2,10},{3,131},{4,12},{5,133},{6,14},{7,135},{8,0},{... | collective-permute-start | bytes 786440 | tf_op jit(solution)/shard_map/ppermute | solution.py:25
  30.0 33.5 %copy-start.4 = (bf16[4,2,128,512]{3,2,1,0:T(8,128)(2,1)}, bf16[4,2,128,512]{3,2,1,0:T(8,128)(2,1)S(1)}, u32[]{:S(2)}) copy-start(bf16[4,2,128,512]{3,2,1,0:T(8,128)(2,1)S(1)} %pad_maximum_fusion.refs_0_) | copy-start | bytes 3145732
  30.0 15.3 %collective-permute-start.3 = (bf16[4,2,128,512]{3,2,1,0:T(8,128)(2,1)S(1)}, bf16[4,2,128,512]{3,2,1,0:T(8,128)(2,1)S(1)}, u32[]{:S(2)}, u32[]{:S(2)}) collective-permute-start(bf16[4,2,128,512]{3,2,1,0:T(8,128)(2,1)S(1)} %pad_maximum_fusion.refs_0_), channel_id=1, source_target_pairs={{0,2},{1,5},{2,128},{3,7},{4,6},{5,9},{6,132},{7,11},{8,10},{9,13}... | collective-permute-start | bytes 3145736 | tf_op jit(solution)/shard_map/ppermute | solution.py:25
  31.0 24.7 %collective-permute-start.4 = (bf16[4,2,128,512]{3,2,1,0:T(8,128)(2,1)S(1)}, bf16[4,2,128,512]{3,2,1,0:T(8,128)(2,1)S(1)}, u32[]{:S(2)}, u32[]{:S(2)}) collective-permute-start(bf16[4,2,128,512]{3,2,1,0:T(8,128)(2,1)S(1)} %pad_maximum_fusion.refs_0_), channel_id=1, source_target_pairs={{0,130},{1,13},{2,0},{3,15},{4,134},{5,1},{6,4},{7,3},{8,138},{9,5... | collective-permute-start | bytes 3145736 | tf_op jit(solution)/shard_map/ppermute | solution.py:25
  32.8 24.8 %collective-permute-start.5 = (bf16[4,2,128,512]{3,2,1,0:T(8,128)(2,1)S(1)}, bf16[4,2,128,512]{3,2,1,0:T(8,128)(2,1)}, u32[]{:S(2)}, u32[]{:S(2)}) collective-permute-start(bf16[4,2,128,512]{3,2,1,0:T(8,128)(2,1)S(1)} %pad_maximum_fusion.refs_0_), channel_id=1, source_target_pairs={{0,128},{1,9},{2,130},{3,11},{4,132},{5,13},{6,134},{7,15},{8,136}... | collective-permute-start | bytes 3145736 | tf_op jit(solution)/shard_map/ppermute | solution.py:25
  34.0 28.6 %collective-permute-start.6 = (bf16[4,2,128,512]{3,2,1,0:T(8,128)(2,1)S(1)}, bf16[4,2,128,512]{3,2,1,0:T(8,128)(2,1)}, u32[]{:S(2)}, u32[]{:S(2)}) collective-permute-start(bf16[4,2,128,512]{3,2,1,0:T(8,128)(2,1)S(1)} %pad_maximum_fusion.refs_0_), channel_id=1, source_target_pairs={{0,1},{1,0},{2,3},{3,2},{4,5},{5,4},{6,7},{7,6},{8,9},{9,8},{10,11... | collective-permute-start | bytes 3145736 | tf_op jit(solution)/shard_map/ppermute | solution.py:25
  45.4 18.1 %copy-start.5 = (bf16[4,2,128,512]{3,2,1,0:T(8,128)(2,1)}, bf16[4,2,128,512]{3,2,1,0:T(8,128)(2,1)S(1)}, u32[]{:S(2)}) copy-start(bf16[4,2,128,512]{3,2,1,0:T(8,128)(2,1)S(1)} %collective-permute-done.3.refs_1_) | copy-start | bytes 3145732
  45.4 17.2 %collective-permute-start.7 = (bf16[4,2,128,512]{3,2,1,0:T(8,128)(2,1)S(1)}, bf16[4,2,128,512]{3,2,1,0:T(8,128)(2,1)}, u32[]{:S(2)}, u32[]{:S(2)}) collective-permute-start(bf16[4,2,128,512]{3,2,1,0:T(8,128)(2,1)S(1)} %collective-permute-done.3.refs_1_), channel_id=1, source_target_pairs={{0,1},{1,0},{2,3},{3,2},{4,5},{5,4},{6,7},{7,6},{8,9},{9,8},{10,11... | collective-permute-start | bytes 3145736 | tf_op jit(solution)/shard_map/ppermute | solution.py:25
  55.8 7.7 %copy-start.6 = (bf16[4,2,128,512]{3,2,1,0:T(8,128)(2,1)}, bf16[4,2,128,512]{3,2,1,0:T(8,128)(2,1)S(1)}, u32[]{:S(2)}) copy-start(bf16[4,2,128,512]{3,2,1,0:T(8,128)(2,1)S(1)} %collective-permute-done.4.refs_2_) | copy-start | bytes 3145732
  55.8 6.9 %collective-permute-start.8 = (bf16[4,2,128,512]{3,2,1,0:T(8,128)(2,1)S(1)}, bf16[4,2,128,512]{3,2,1,0:T(8,128)(2,1)}, u32[]{:S(2)}, u32[]{:S(2)}) collective-permute-start(bf16[4,2,128,512]{3,2,1,0:T(8,128)(2,1)S(1)} %collective-permute-done.4.refs_2_), channel_id=1, source_target_pairs={{0,1},{1,0},{2,3},{3,2},{4,5},{5,4},{6,7},{7,6},{8,9},{9,8},{10,11... | collective-permute-start | bytes 3145736 | tf_op jit(solution)/shard_map/ppermute | solution.py:25
  57.6 5.9 %collective-permute-start.9 = (bf16[4,2,128,512]{3,2,1,0:T(8,128)(2,1)}, bf16[4,2,128,512]{3,2,1,0:T(8,128)(2,1)}, u32[]{:S(2)}, u32[]{:S(2)}) collective-permute-start(bf16[4,2,128,512]{3,2,1,0:T(8,128)(2,1)} %collective-permute-done.5.refs_3_), channel_id=1, source_target_pairs={{0,1},{1,0},{2,3},{3,2},{4,5},{5,4},{6,7},{7,6},{8,9},{9,8},{10,11... | collective-permute-start | bytes 3145736 | tf_op jit(solution)/shard_map/ppermute | solution.py:25
  90.1 2.2 %copy-start = (bf16[16,2,4,128,128]{4,3,2,1,0:T(8,128)(2,1)S(1)}, bf16[16,2,4,128,128]{4,3,2,1,0:T(8,128)(2,1)}, u32[]{:S(2)}) copy-start(bf16[16,2,4,128,128]{4,3,2,1,0:T(8,128)(2,1)} %all-gather.3.cloned.1.call-done) | copy-start | bytes 12582916
  99.6 3.0 %collective-permute-start.12 = (bf16[4,2,128,512]{3,2,1,0:T(8,128)(2,1)S(1)}, bf16[4,2,128,512]{3,2,1,0:T(8,128)(2,1)S(1)}, u32[]{:S(2)}, u32[]{:S(2)}) collective-permute-start(bf16[4,2,128,512]{3,2,1,0:T(8,128)(2,1)S(1)} %get-tuple-element.29), channel_id=1, source_target_pairs={{0,1},{1,0},{2,3},{3,2},{4,5},{5,4},{6,7},{7,6},{8,9},{9,8},{10,11... | collective-permute-start | bytes 3145736 | tf_op jit(solution)/shard_map/ppermute | solution.py:25
  100.4 3.8 %collective-permute-start.14 = (bf16[4,2,128,512]{3,2,1,0:T(8,128)(2,1)S(1)}, bf16[4,2,128,512]{3,2,1,0:T(8,128)(2,1)S(1)}, u32[]{:S(2)}, u32[]{:S(2)}) collective-permute-start(bf16[4,2,128,512]{3,2,1,0:T(8,128)(2,1)S(1)} %get-tuple-element.28), channel_id=1, source_target_pairs={{0,1},{1,0},{2,3},{3,2},{4,5},{5,4},{6,7},{7,6},{8,9},{9,8},{10,11... | collective-permute-start | bytes 3145736 | tf_op jit(solution)/shard_map/ppermute | solution.py:25
  100.7 5.0 %collective-permute-start.16 = (bf16[4,2,128,512]{3,2,1,0:T(8,128)(2,1)S(1)}, bf16[4,2,128,512]{3,2,1,0:T(8,128)(2,1)S(1)}, u32[]{:S(2)}, u32[]{:S(2)}) collective-permute-start(bf16[4,2,128,512]{3,2,1,0:T(8,128)(2,1)S(1)} %get-tuple-element.27), channel_id=1, source_target_pairs={{0,1},{1,0},{2,3},{3,2},{4,5},{5,4},{6,7},{7,6},{8,9},{9,8},{10,11... | collective-permute-start | bytes 3145736 | tf_op jit(solution)/shard_map/ppermute | solution.py:25
  100.9 11.4 %collective-permute-start.11 = (bf16[4,2,128,512]{3,2,1,0:T(8,128)(2,1)S(1)}, bf16[4,2,128,512]{3,2,1,0:T(8,128)(2,1)S(1)}, u32[]{:S(2)}, u32[]{:S(2)}) collective-permute-start(bf16[4,2,128,512]{3,2,1,0:T(8,128)(2,1)S(1)} %get-tuple-element.26), channel_id=1, source_target_pairs={{0,1},{1,0},{2,3},{3,2},{4,5},{5,4},{6,7},{7,6},{8,9},{9,8},{10,11... | collective-permute-start | bytes 3145736 | tf_op jit(solution)/shard_map/ppermute | solution.py:25
  106.8 15.6 %collective-permute-start.13 = (bf16[4,2,128,512]{3,2,1,0:T(8,128)(2,1)S(1)}, bf16[4,2,128,512]{3,2,1,0:T(8,128)(2,1)S(1)}, u32[]{:S(2)}, u32[]{:S(2)}) collective-permute-start(bf16[4,2,128,512]{3,2,1,0:T(8,128)(2,1)S(1)} %get-tuple-element.30), channel_id=1, source_target_pairs={{0,128},{1,9},{2,130},{3,11},{4,132},{5,13},{6,134},{7,15},{8,136}... | collective-permute-start | bytes 3145736 | tf_op jit(solution)/shard_map/ppermute | solution.py:25
  109.6 24.1 %collective-permute-start.15 = (bf16[4,2,128,512]{3,2,1,0:T(8,128)(2,1)S(1)}, bf16[4,2,128,512]{3,2,1,0:T(8,128)(2,1)S(1)}, u32[]{:S(2)}, u32[]{:S(2)}) collective-permute-start(bf16[4,2,128,512]{3,2,1,0:T(8,128)(2,1)S(1)} %get-tuple-element.32), channel_id=1, source_target_pairs={{0,2},{1,5},{2,128},{3,7},{4,6},{5,9},{6,132},{7,11},{8,10},{9,13}... | collective-permute-start | bytes 3145736 | tf_op jit(solution)/shard_map/ppermute | solution.py:25
  109.9 23.9 %collective-permute-start.17 = (bf16[4,2,128,512]{3,2,1,0:T(8,128)(2,1)S(1)}, bf16[4,2,128,512]{3,2,1,0:T(8,128)(2,1)S(1)}, u32[]{:S(2)}, u32[]{:S(2)}) collective-permute-start(bf16[4,2,128,512]{3,2,1,0:T(8,128)(2,1)S(1)} %get-tuple-element.31), channel_id=1, source_target_pairs={{0,130},{1,13},{2,0},{3,15},{4,134},{5,1},{6,4},{7,3},{8,138},{9,5... | collective-permute-start | bytes 3145736 | tf_op jit(solution)/shard_map/ppermute | solution.py:25
  134.6 12.5 %collective-permute-start.18 = (bf16[2,128,512]{2,1,0:T(8,128)(2,1)S(1)}, bf16[2,128,512]{2,1,0:T(8,128)(2,1)S(1)}, u32[]{:S(2)}, u32[]{:S(2)}) collective-permute-start(bf16[2,128,512]{2,1,0:T(8,128)(2,1)S(1)} %get-tuple-element.35), channel_id=1, source_target_pairs={{0,8},{1,129},{2,10},{3,131},{4,12},{5,133},{6,14},{7,135},{8,0},{... | collective-permute-start | bytes 786440 | tf_op jit(solution)/shard_map/ppermute | solution.py:25
  137.5 9.7 %collective-permute-start.19 = (bf16[2,128,512]{2,1,0:T(8,128)(2,1)S(1)}, bf16[2,128,512]{2,1,0:T(8,128)(2,1)S(1)}, u32[]{:S(2)}, u32[]{:S(2)}) collective-permute-start(bf16[2,128,512]{2,1,0:T(8,128)(2,1)S(1)} %get-tuple-element.37), channel_id=1, source_target_pairs={{0,4},{1,3},{2,6},{3,129},{4,8},{5,7},{6,10},{7,133},{8,12},{9,11}... | collective-permute-start | bytes 786440 | tf_op jit(solution)/shard_map/ppermute | solution.py:25
  137.8 9.4 %collective-permute-start.20 = (bf16[2,128,512]{2,1,0:T(8,128)(2,1)S(1)}, bf16[2,128,512]{2,1,0:T(8,128)(2,1)S(1)}, u32[]{:S(2)}, u32[]{:S(2)}) collective-permute-start(bf16[2,128,512]{2,1,0:T(8,128)(2,1)S(1)} %get-tuple-element.36), channel_id=1, source_target_pairs={{0,12},{1,131},{2,14},{3,1},{4,0},{5,135},{6,2},{7,5},{8,4},{9,139... | collective-permute-start | bytes 786440 | tf_op jit(solution)/shard_map/ppermute | solution.py:25
  144.3 8.8 %collective-permute-start.21 = (bf16[2,4,128,128]{3,2,1,0:T(8,128)(2,1)S(1)}, bf16[2,4,128,128]{3,2,1,0:T(8,128)(2,1)S(1)}, u32[]{:S(2)}, u32[]{:S(2)}) collective-permute-start(bf16[2,4,128,128]{3,2,1,0:T(8,128)(2,1)S(1)} %get-tuple-element.39), channel_id=1, source_target_pairs={{0,128},{1,129},{2,130},{3,131},{4,132},{5,133},{6,134},{7,135},{8... | collective-permute-start | bytes 786440 | tf_op jit(solution)/shard_map/ppermute | solution.py:25
  (3 other events, 3.0 us)
Sparse Core Ops, SparseCore 0:
  18.2 59.4 all-gather.2
  89.3 53.9 reduce-scatter.1

commit v2 on v1

--- a/solution.py
+++ b/solution.py
@@ -216,7 +216,7 @@
         kept[n] = total([parts[n], send(parts[4 + n], other_core)]).astype(jnp.bfloat16)
     row = [kept[0]] + [send(kept[n], beside(STEPS[n])) for n in (3, 1, 2)]
     row = total(row).astype(jnp.bfloat16)
-    return total([row[0]] + [send(row[n], across(STEPS[n])) for n in (3, 1, 2)]).astype(jnp.bfloat16)
+    return [row[0]] + [send(row[n], across(STEPS[n])) for n in (3, 1, 2)]
 
 
 def local(tokens, pattern, w_up, w_down, cotangent):
@@ -246,9 +246,9 @@
     outs_at = (((c_to ^ core) * 4 + second) * 4 + first).reshape(-1).astype(jnp.int32)
 
     both = jnp.stack([w_up[:, 0], w_down[:, 0]])
+    other_b = send(lax.dynamic_slice_in_dim(both, (1 - yh) * 4, 4, 1), other_half)
+    both = jnp.stack(lax.optimization_barrier((w_up[:, 0], w_down[:, 0])))
     piece_a = lax.dynamic_slice_in_dim(both, yh * 4, 4, 1)
-    piece_b = lax.dynamic_slice_in_dim(both, (1 - yh) * 4, 4, 1)
-    other_b = send(piece_b, other_half)
     plane = gather_plane(jnp.stack([tokens, cotangent]))
     weights = lax.all_gather(
         jnp.stack([piece_a, other_b]), "dp", axis_index_groups=HALVES
@@ -316,17 +316,16 @@
         name="second",
     )(outs_at, rows, act, gh, weights)
 
-    result = scatter_plane(parts)
+    last = scatter_plane(parts)
+    other = send(jnp.stack([jnp.swapaxes(summed[1, 0], 1, 2), summed[1, 1]]), other_half)
+    own, last = lax.optimization_barrier((summed[0], last))
+    own = jnp.stack([jnp.swapaxes(own[0], 1, 2), own[1]])
+    grads = jnp.where(
+        yh == 0, jnp.concatenate([own, other], axis=1), jnp.concatenate([other, own], axis=1)
+    ).astype(f32)
+    grad_up, grad_down = grads[0][:, None], grads[1][:, None]
+    result = total(last).astype(bf16)
     mixed, grad_tokens = result[0], result[1]
-    other = send(summed[1], other_half).astype(f32)
-    summed_a = summed[0].astype(f32)
-    grad_both = jnp.where(
-        yh == 0,
-        jnp.concatenate([summed_a, other], axis=1),
-        jnp.concatenate([other, summed_a], axis=1),
-    )
-    grad_up = jnp.swapaxes(grad_both[0], 1, 2)[:, None]
-    grad_down = grad_both[1][:, None]
     return mixed, grad_tokens, grad_up, grad_down
 
 

time: 162 us -> 165 us (1.019); the launches traced: 162 us -> 163 us
    reduce_scatter x1, waiting for transfers between devices: 3.11 us -> 1.07 us  [local(): lax.psum_scatter(grads, 'dp', scatter_dimension=0, axis_index_groups=HALV...]
    ppermute x22, waiting for transfers between devices: 60.5 us -> 62.5 us  [send(): lax.ppermute(value, AXES, [(source, place_of(*step(*where_is(source)))) f...]
  transfers between devices with their start and end apart: 24 -> 24, of which waited for: 17 -> 18; matrix products, arithmetic and copies ran while one was open for 4% -> 5% of each run, Pallas kernels for 9% -> 9%
where the time goes in v2:
time: 165 us; the launch traced here: 163 us
  waiting for transfers between devices  69.3 us (42%)
  starting transfers between devices  38.1 us (23%)
  Pallas kernels  26.6 us (16%)
  between operations  14.3 us (9%)
  local copies, waits for them, and re-layouts  7.8 us (5%)
  other arithmetic  6.69 us (4%)
    ppermute x22, waiting for transfers between devices, send(): lax.ppermute(value, AXES, [(source, place_of(*step(*where_is(source)))) f...  62.5 us
    ppermute x22, starting transfers between devices, send(): lax.ppermute(value, AXES, [(source, place_of(*step(*where_is(source)))) f...  38 us
    pallas_call x1, Pallas kernels, local(): pl.pallas_call(first_kernel, out_shape=[jax.ShapeDtypeStruct((4, 2 * B, B...  11.3 us
    pallas_call x1, Pallas kernels, local(): pl.pallas_call(place_kernel, out_shape=[gathered] * 2, in_specs=[SMEM] +...  8.19 us
    pallas_call x1, Pallas kernels, local(): pl.pallas_call(second_kernel, out_shape=jax.ShapeDtypeStruct((8, 4, 2, B,...  7.04 us
    all_gather x1, waiting for transfers between devices, local(): lax.all_gather(jnp.stack([piece_a, other_b]), 'dp', axis_index_groups=HAL...  5.67 us
    unnamed x24, local copies, waits for them, and re-layouts  3.99 us
  transfers between devices with their start and end apart: 24, of which 18 were waited for; matrix products, arithmetic and copies ran while one was open for 5% of the time, Pallas kernels for 9%

profile of v2, /device:TPU:1, one launch (start us, length us, event | category | flops | bytes accessed | tf_op | source)
XLA Modules:
  0.0 162.8 jit_solution(15293196415915467015)
XLA Ops:
  8.3 3.8 %collective-permute-start.10 = (bf16[2,4,128,128]{3,2,1,0:T(8,128)(2,1)S(1)}, bf16[2,4,128,128]{3,2,1,0:T(8,128)(2,1)S(1)}, u32[]{:S(2)}, u32[]{:S(2)}) collective-permute-start(bf16[2,4,128,128]{3,2,1,0:T(8,128)(2,1)S(1)} %fusion.5), channel_id=1, source_target_pairs={{0,128},{1,129},{2,130},{3,131},{4,132},{5,133},{6,134},{7,135},{8... | collective-permute-start | bytes 786440 | tf_op jit(solution)/shard_map/ppermute | solution.py:25
  13.1 4.0 %collective-permute-done.10 = bf16[2,4,128,128]{3,2,1,0:T(8,128)(2,1)S(1)} collective-permute-done((bf16[2,4,128,128]{3,2,1,0:T(8,128)(2,1)S(1)}, bf16[2,4,128,128]{3,2,1,0:T(8,128)(2,1)S(1)}, u32[]{:S(2)}, u32[]{:S(2)}) %collective-permute-start.10) | collective-permute-done | bytes 262176 | tf_op jit(solution)/shard_map/ppermute | solution.py:25
  18.1 3.8 %collective-permute-start.2 = (bf16[2,128,512]{2,1,0:T(8,128)(2,1)S(1)}, bf16[2,128,512]{2,1,0:T(8,128)(2,1)S(1)}, u32[]{:S(2)}, u32[]{:S(2)}) collective-permute-start(bf16[2,128,512]{2,1,0:T(8,128)(2,1)S(1)} %get-tuple-element.60), channel_id=1, source_target_pairs={{0,8},{1,129},{2,10},{3,131},{4,12},{5,133},{6,14},{7,135},{8,0},{... | collective-permute-start | bytes 786440 | tf_op jit(solution)/shard_map/ppermute | solution.py:25
  23.3 2.6 %collective-permute-done.2 = bf16[2,128,512]{2,1,0:T(8,128)(2,1)S(1)} collective-permute-done((bf16[2,128,512]{2,1,0:T(8,128)(2,1)S(1)}, bf16[2,128,512]{2,1,0:T(8,128)(2,1)S(1)}, u32[]{:S(2)}, u32[]{:S(2)}) %collective-permute-start.2) | collective-permute-done | bytes 262176 | tf_op jit(solution)/shard_map/ppermute | solution.py:25
  25.9 3.2 %collective-permute-done.1 = bf16[2,128,512]{2,1,0:T(8,128)(2,1)S(1)} collective-permute-done((bf16[2,128,512]{2,1,0:T(8,128)(2,1)S(1)}, bf16[2,128,512]{2,1,0:T(8,128)(2,1)S(1)}, u32[]{:S(2)}, u32[]{:S(2)}) %collective-permute-start.1) | collective-permute-done | bytes 262176 | tf_op jit(solution)/shard_map/ppermute | solution.py:25
  29.5 1.1 collective-permute-start.3
  30.6 1.7 %collective-permute-start.4 = (bf16[4,2,128,512]{3,2,1,0:T(8,128)(2,1)S(1)}, bf16[4,2,128,512]{3,2,1,0:T(8,128)(2,1)S(1)}, u32[]{:S(2)}, u32[]{:S(2)}) collective-permute-start(bf16[4,2,128,512]{3,2,1,0:T(8,128)(2,1)S(1)} %pad_maximum_fusion.refs_0_), channel_id=1, source_target_pairs={{0,130},{1,13},{2,0},{3,15},{4,134},{5,1},{6,4},{7,3},{8,138},{9,5... | collective-permute-start | bytes 3145736 | tf_op jit(solution)/shard_map/ppermute | solution.py:25
  32.3 1.3 collective-permute-start.5
  33.6 4.1 %collective-permute-start.6 = (bf16[4,2,128,512]{3,2,1,0:T(8,128)(2,1)S(1)}, bf16[4,2,128,512]{3,2,1,0:T(8,128)(2,1)}, u32[]{:S(2)}, u32[]{:S(2)}) collective-permute-start(bf16[4,2,128,512]{3,2,1,0:T(8,128)(2,1)S(1)} %pad_maximum_fusion.refs_0_), channel_id=1, source_target_pairs={{0,1},{1,0},{2,3},{3,2},{4,5},{5,4},{6,7},{7,6},{8,9},{9,8},{10,11... | collective-permute-start | bytes 3145736 | tf_op jit(solution)/shard_map/ppermute | solution.py:25
  37.7 7.2 %collective-permute-done.3.refs_1_ = bf16[4,2,128,512]{3,2,1,0:T(8,128)(2,1)S(1)} collective-permute-done((bf16[4,2,128,512]{3,2,1,0:T(8,128)(2,1)S(1)}, bf16[4,2,128,512]{3,2,1,0:T(8,128)(2,1)S(1)}, u32[]{:S(2)}, u32[]{:S(2)}) %collective-permute-start.3) | collective-permute-done | bytes 1048608 | tf_op jit(solution)/shard_map/ppermute | solution.py:25
  44.9 3.6 %collective-permute-start.7 = (bf16[4,2,128,512]{3,2,1,0:T(8,128)(2,1)S(1)}, bf16[4,2,128,512]{3,2,1,0:T(8,128)(2,1)}, u32[]{:S(2)}, u32[]{:S(2)}) collective-permute-start(bf16[4,2,128,512]{3,2,1,0:T(8,128)(2,1)S(1)} %collective-permute-done.3.refs_1_), channel_id=1, source_target_pairs={{0,1},{1,0},{2,3},{3,2},{4,5},{5,4},{6,7},{7,6},{8,9},{9,8},{10,11... | collective-permute-start | bytes 3145736 | tf_op jit(solution)/shard_map/ppermute | solution.py:25
  48.5 6.8 %collective-permute-done.4.refs_2_ = bf16[4,2,128,512]{3,2,1,0:T(8,128)(2,1)S(1)} collective-permute-done((bf16[4,2,128,512]{3,2,1,0:T(8,128)(2,1)S(1)}, bf16[4,2,128,512]{3,2,1,0:T(8,128)(2,1)S(1)}, u32[]{:S(2)}, u32[]{:S(2)}) %collective-permute-start.4) | collective-permute-done | bytes 1048608 | tf_op jit(solution)/shard_map/ppermute | solution.py:25
  55.3 1.8 %collective-permute-done.5.refs_3_ = bf16[4,2,128,512]{3,2,1,0:T(8,128)(2,1)} collective-permute-done((bf16[4,2,128,512]{3,2,1,0:T(8,128)(2,1)S(1)}, bf16[4,2,128,512]{3,2,1,0:T(8,128)(2,1)}, u32[]{:S(2)}, u32[]{:S(2)}) %collective-permute-start.5) | collective-permute-done | bytes 1048608 | tf_op jit(solution)/shard_map/ppermute | solution.py:25
  57.1 4.0 %collective-permute-start.9 = (bf16[4,2,128,512]{3,2,1,0:T(8,128)(2,1)}, bf16[4,2,128,512]{3,2,1,0:T(8,128)(2,1)}, u32[]{:S(2)}, u32[]{:S(2)}) collective-permute-start(bf16[4,2,128,512]{3,2,1,0:T(8,128)(2,1)} %collective-permute-done.5.refs_3_), channel_id=1, source_target_pairs={{0,1},{1,0},{2,3},{3,2},{4,5},{5,4},{6,7},{7,6},{8,9},{9,8},{10,11... | collective-permute-start | bytes 3145736 | tf_op jit(solution)/shard_map/ppermute | solution.py:25
  63.7 8.2 %place.1 = (bf16[16,256,512]{2,1,0:T(8,128)(2,1)}, bf16[16,256,512]{2,1,0:T(8,128)(2,1)}) custom-call(s32[32]{0:T(128)} %pad_add_fusion.spots, bf16[4,2,128,512]{3,2,1,0:T(8,128)(2,1)} %copy-done.4, bf16[4,2,128,512]{3,2,1,0:T(8,128)(2,1)} %copy-done.5, bf16[4,2,128,512]{3,2,1,0:T(8,128)(2,1)} %copy-done.6, ...), custom_call_target="tpu_custom_call" | custom-call | bytes 16777216 | tf_op jit(solution)/shard_map/place/pallas_call | solution.py:258
  71.9 5.7 %all-gather.3.cloned.1.call-done = bf16[16,2,4,128,128]{4,3,2,1,0:T(8,128)(2,1)} async-done(((bf16[2,2,4,128,128]{4,3,2,1,0:T(8,128)(2,1)}), bf16[16,2,4,128,128]{4,3,2,1,0:T(8,128)(2,1)}) %all-gather.3.cloned.1.call-update) | async-done | bytes 4194320 | tf_op jit(solution)/shard_map/all_gather | solution.py:253
  77.6 11.3 %first.1 = (bf16[4,256,128]{2,1,0:T(8,128)(2,1)}, bf16[4,256,128]{2,1,0:T(8,128)(2,1)}, bf16[8,2,2,4,128,128]{5,4,3,2,1,0:T(8,128)(2,1)}) custom-call(s32[4,16]{1,0:T(4,128)} %add_select_fusion.rows, bf16[16,256,512]{2,1,0:T(8,128)(2,1)} %get-tuple-element.16.x_in, bf16[16,256,512]{2,1,0:T(8,128)(2,1)} %get-tuple-element.17.g_in, ...), custom_call_target="tpu_custom_call" | custom-call | flops 2000000000 | bytes 16777216 | tf_op jit(solution)/shard_map/first/pallas_call | solution.py:274
  90.0 2.2 %copy-done = bf16[16,2,4,128,128]{4,3,2,1,0:T(8,128)(2,1)S(1)} copy-done((bf16[16,2,4,128,128]{4,3,2,1,0:T(8,128)(2,1)S(1)}, bf16[16,2,4,128,128]{4,3,2,1,0:T(8,128)(2,1)}, u32[]{:S(2)}) %copy-start) | copy-done | bytes 4194328
  92.1 7.0 %second.1 = bf16[8,4,2,128,512]{4,3,2,1,0:T(8,128)(2,1)S(1)} custom-call(s32[128]{0:T(128)S(1)} %add.295.outs_at, s32[4,16]{1,0:T(4,128)S(1)} %copy-done.3, bf16[4,256,128]{2,1,0:T(8,128)(2,1)S(1)} %copy-done.1, bf16[4,256,128]{2,1,0:T(8,128)(2,1)S(1)} %copy-done.2, bf16[8,2,2,4,128,128]{5,4,3,2,1,0:T(8,128)(2,1)S(1)} %bitcast.88), custom_call_target="tpu_custom_call" | custom-call | flops 1000000000 | bytes 16777216 | tf_op jit(solution)/shard_map/second/pallas_call | solution.py:301
  101.0 1.5 collective-permute-done.12
  102.5 1.5 collective-permute-done.16
  104.0 1.5 collective-permute-done.14
  105.5 1.2 fusion.2
  106.7 2.5 %collective-permute-start.17 = (bf16[4,2,128,512]{3,2,1,0:T(8,128)(2,1)S(1)}, bf16[4,2,128,512]{3,2,1,0:T(8,128)(2,1)S(1)}, u32[]{:S(2)}, u32[]{:S(2)}) collective-permute-start(bf16[4,2,128,512]{3,2,1,0:T(8,128)(2,1)S(1)} %get-tuple-element.45), channel_id=1, source_target_pairs={{0,130},{1,13},{2,0},{3,15},{4,134},{5,1},{6,4},{7,3},{8,138},{9,5... | collective-permute-start | bytes 3145736 | tf_op jit(solution)/shard_map/ppermute | solution.py:25
  109.2 1.7 %collective-permute-start.13 = (bf16[4,2,128,512]{3,2,1,0:T(8,128)(2,1)S(1)}, bf16[4,2,128,512]{3,2,1,0:T(8,128)(2,1)S(1)}, u32[]{:S(2)}, u32[]{:S(2)}) collective-permute-start(bf16[4,2,128,512]{3,2,1,0:T(8,128)(2,1)S(1)} %get-tuple-element.44), channel_id=1, source_target_pairs={{0,128},{1,9},{2,130},{3,11},{4,132},{5,13},{6,134},{7,15},{8,136}... | collective-permute-start | bytes 3145736 | tf_op jit(solution)/shard_map/ppermute | solution.py:25
  110.9 21.2 %collective-permute-done.17 = bf16[4,2,128,512]{3,2,1,0:T(8,128)(2,1)S(1)} collective-permute-done((bf16[4,2,128,512]{3,2,1,0:T(8,128)(2,1)S(1)}, bf16[4,2,128,512]{3,2,1,0:T(8,128)(2,1)S(1)}, u32[]{:S(2)}, u32[]{:S(2)}) %collective-permute-start.17) | collective-permute-done | bytes 1048608 | tf_op jit(solution)/shard_map/ppermute | solution.py:25
  132.2 3.5 %collective-permute-done.15 = bf16[4,2,128,512]{3,2,1,0:T(8,128)(2,1)S(1)} collective-permute-done((bf16[4,2,128,512]{3,2,1,0:T(8,128)(2,1)S(1)}, bf16[4,2,128,512]{3,2,1,0:T(8,128)(2,1)S(1)}, u32[]{:S(2)}, u32[]{:S(2)}) %collective-permute-start.15) | collective-permute-done | bytes 1048608 | tf_op jit(solution)/shard_map/ppermute | solution.py:25
  136.5 2.8 %collective-permute-start.18 = (bf16[2,128,512]{2,1,0:T(8,128)(2,1)S(1)}, bf16[2,128,512]{2,1,0:T(8,128)(2,1)S(1)}, u32[]{:S(2)}, u32[]{:S(2)}) collective-permute-start(bf16[2,128,512]{2,1,0:T(8,128)(2,1)S(1)} %get-tuple-element.51), channel_id=1, source_target_pairs={{0,8},{1,129},{2,10},{3,131},{4,12},{5,133},{6,14},{7,135},{8,0},{... | collective-permute-start | bytes 786440 | tf_op jit(solution)/shard_map/ppermute | solution.py:25
  139.7 2.4 %collective-permute-start.20 = (bf16[2,128,512]{2,1,0:T(8,128)(2,1)S(1)}, bf16[2,128,512]{2,1,0:T(8,128)(2,1)S(1)}, u32[]{:S(2)}, u32[]{:S(2)}) collective-permute-start(bf16[2,128,512]{2,1,0:T(8,128)(2,1)S(1)} %get-tuple-element.49), channel_id=1, source_target_pairs={{0,12},{1,131},{2,14},{3,1},{4,0},{5,135},{6,2},{7,5},{8,4},{9,139... | collective-permute-start | bytes 786440 | tf_op jit(solution)/shard_map/ppermute | solution.py:25
  144.1 2.4 %collective-permute-done.19 = bf16[2,128,512]{2,1,0:T(8,128)(2,1)S(1)} collective-permute-done((bf16[2,128,512]{2,1,0:T(8,128)(2,1)S(1)}, bf16[2,128,512]{2,1,0:T(8,128)(2,1)S(1)}, u32[]{:S(2)}, u32[]{:S(2)}) %collective-permute-start.19) | collective-permute-done | bytes 262176 | tf_op jit(solution)/shard_map/ppermute | solution.py:25
  147.7 1.9 %collective-permute-start.21 = (bf16[2,4,128,128]{3,2,1,0:T(8,128)(2,1)S(1)}, bf16[2,4,128,128]{3,2,1,0:T(8,128)(2,1)S(1)}, u32[]{:S(2)}, u32[]{:S(2)}) collective-permute-start(bf16[2,4,128,128]{3,2,1,0:T(8,128)(2,1)S(1)} %pad_maximum_fusion.3), channel_id=1, source_target_pairs={{0,128},{1,129},{2,130},{3,131},{4,132},{5,133},{6,134},{7,135},{8... | collective-permute-start | bytes 786440 | tf_op jit(solution)/shard_map/ppermute | solution.py:25
  150.6 4.2 %collective-permute-done.21 = bf16[2,4,128,128]{3,2,1,0:T(8,128)(2,1)S(1)} collective-permute-done((bf16[2,4,128,128]{3,2,1,0:T(8,128)(2,1)S(1)}, bf16[2,4,128,128]{3,2,1,0:T(8,128)(2,1)S(1)}, u32[]{:S(2)}, u32[]{:S(2)}) %collective-permute-start.21) | collective-permute-done | bytes 262176 | tf_op jit(solution)/shard_map/ppermute | solution.py:25
  (79 shorter events, 16.8 us)
Async XLA Ops:
  7.2 10.8 %copy-start.7 = (bf16[128,512]{1,0:T(8,128)(2,1)S(1)}, bf16[128,512]{1,0:T(8,128)(2,1)}, u32[]{:S(2)}) copy-start(bf16[128,512]{1,0:T(8,128)(2,1)} %param.11) | copy-start | bytes 393220
  7.2 10.8 %copy-start.8 = (bf16[128,512]{1,0:T(8,128)(2,1)S(1)}, bf16[128,512]{1,0:T(8,128)(2,1)}, u32[]{:S(2)}) copy-start(bf16[128,512]{1,0:T(8,128)(2,1)} %param.7) | copy-start | bytes 393220
  7.2 70.4 %all-gather.3.cloned.1.call-start = ((), (), s32[]{:S(2)}) async-start(), calls=%async_computation.2 | async-start | bytes 4718592 | tf_op jit(solution)/shard_map/all_gather | solution.py:253
  8.3 8.8 %collective-permute-start.10 = (bf16[2,4,128,128]{3,2,1,0:T(8,128)(2,1)S(1)}, bf16[2,4,128,128]{3,2,1,0:T(8,128)(2,1)S(1)}, u32[]{:S(2)}, u32[]{:S(2)}) collective-permute-start(bf16[2,4,128,128]{3,2,1,0:T(8,128)(2,1)S(1)} %fusion.5), channel_id=1, source_target_pairs={{0,128},{1,129},{2,130},{3,131},{4,132},{5,133},{6,134},{7,135},{8... | collective-permute-start | bytes 786440 | tf_op jit(solution)/shard_map/ppermute | solution.py:25
  17.1 44.0 %copy-start.10 = (s32[4]{0:T(128)S(1)}, s32[4]{0:T(128)}, u32[]{:S(2)}) copy-start(s32[4]{0:T(128)} %constant.182.clone) | copy-start | bytes 52
  17.1 45.0 %copy-start.9 = (s32[8,16]{1,0:T(8,128)S(1)}, s32[8,16]{1,0:T(8,128)}, u32[]{:S(2)}) copy-start(s32[8,16]{1,0:T(8,128)} %param.8) | copy-start | bytes 1540
  18.0 125.1 %reduce-scatter.2.cloned.1.call-start = ((), (), s32[]{:S(2)}) async-start(), calls=%async_computation.1 | async-start | bytes 4718592 | tf_op jit(solution)/shard_map/reduce_scatter | solution.py:297
  18.1 7.8 %collective-permute-start.2 = (bf16[2,128,512]{2,1,0:T(8,128)(2,1)S(1)}, bf16[2,128,512]{2,1,0:T(8,128)(2,1)S(1)}, u32[]{:S(2)}, u32[]{:S(2)}) collective-permute-start(bf16[2,128,512]{2,1,0:T(8,128)(2,1)S(1)} %get-tuple-element.60), channel_id=1, source_target_pairs={{0,8},{1,129},{2,10},{3,131},{4,12},{5,133},{6,14},{7,135},{8,0},{... | collective-permute-start | bytes 786440 | tf_op jit(solution)/shard_map/ppermute | solution.py:25
  21.9 7.3 %collective-permute-start.1 = (bf16[2,128,512]{2,1,0:T(8,128)(2,1)S(1)}, bf16[2,128,512]{2,1,0:T(8,128)(2,1)S(1)}, u32[]{:S(2)}, u32[]{:S(2)}) collective-permute-start(bf16[2,128,512]{2,1,0:T(8,128)(2,1)S(1)} %get-tuple-element.60), channel_id=1, source_target_pairs={{0,12},{1,131},{2,14},{3,1},{4,0},{5,135},{6,2},{7,5},{8,4},{9,139... | collective-permute-start | bytes 786440 | tf_op jit(solution)/shard_map/ppermute | solution.py:25
  22.6 6.7 %collective-permute-start = (bf16[2,128,512]{2,1,0:T(8,128)(2,1)S(1)}, bf16[2,128,512]{2,1,0:T(8,128)(2,1)S(1)}, u32[]{:S(2)}, u32[]{:S(2)}) collective-permute-start(bf16[2,128,512]{2,1,0:T(8,128)(2,1)S(1)} %get-tuple-element.60), channel_id=1, source_target_pairs={{0,4},{1,3},{2,6},{3,129},{4,8},{5,7},{6,10},{7,133},{8,12},{9,11}... | collective-permute-start | bytes 786440 | tf_op jit(solution)/shard_map/ppermute | solution.py:25
  29.5 34.2 %copy-start.4 = (bf16[4,2,128,512]{3,2,1,0:T(8,128)(2,1)}, bf16[4,2,128,512]{3,2,1,0:T(8,128)(2,1)S(1)}, u32[]{:S(2)}) copy-start(bf16[4,2,128,512]{3,2,1,0:T(8,128)(2,1)S(1)} %pad_maximum_fusion.refs_0_) | copy-start | bytes 3145732
  29.5 15.3 %collective-permute-start.3 = (bf16[4,2,128,512]{3,2,1,0:T(8,128)(2,1)S(1)}, bf16[4,2,128,512]{3,2,1,0:T(8,128)(2,1)S(1)}, u32[]{:S(2)}, u32[]{:S(2)}) collective-permute-start(bf16[4,2,128,512]{3,2,1,0:T(8,128)(2,1)S(1)} %pad_maximum_fusion.refs_0_), channel_id=1, source_target_pairs={{0,2},{1,5},{2,128},{3,7},{4,6},{5,9},{6,132},{7,11},{8,10},{9,13}... | collective-permute-start | bytes 3145736 | tf_op jit(solution)/shard_map/ppermute | solution.py:25
  30.6 24.6 %collective-permute-start.4 = (bf16[4,2,128,512]{3,2,1,0:T(8,128)(2,1)S(1)}, bf16[4,2,128,512]{3,2,1,0:T(8,128)(2,1)S(1)}, u32[]{:S(2)}, u32[]{:S(2)}) collective-permute-start(bf16[4,2,128,512]{3,2,1,0:T(8,128)(2,1)S(1)} %pad_maximum_fusion.refs_0_), channel_id=1, source_target_pairs={{0,130},{1,13},{2,0},{3,15},{4,134},{5,1},{6,4},{7,3},{8,138},{9,5... | collective-permute-start | bytes 3145736 | tf_op jit(solution)/shard_map/ppermute | solution.py:25
  32.3 24.8 %collective-permute-start.5 = (bf16[4,2,128,512]{3,2,1,0:T(8,128)(2,1)S(1)}, bf16[4,2,128,512]{3,2,1,0:T(8,128)(2,1)}, u32[]{:S(2)}, u32[]{:S(2)}) collective-permute-start(bf16[4,2,128,512]{3,2,1,0:T(8,128)(2,1)S(1)} %pad_maximum_fusion.refs_0_), channel_id=1, source_target_pairs={{0,128},{1,9},{2,130},{3,11},{4,132},{5,13},{6,134},{7,15},{8,136}... | collective-permute-start | bytes 3145736 | tf_op jit(solution)/shard_map/ppermute | solution.py:25
  33.6 29.2 %collective-permute-start.6 = (bf16[4,2,128,512]{3,2,1,0:T(8,128)(2,1)S(1)}, bf16[4,2,128,512]{3,2,1,0:T(8,128)(2,1)}, u32[]{:S(2)}, u32[]{:S(2)}) collective-permute-start(bf16[4,2,128,512]{3,2,1,0:T(8,128)(2,1)S(1)} %pad_maximum_fusion.refs_0_), channel_id=1, source_target_pairs={{0,1},{1,0},{2,3},{3,2},{4,5},{5,4},{6,7},{7,6},{8,9},{9,8},{10,11... | collective-permute-start | bytes 3145736 | tf_op jit(solution)/shard_map/ppermute | solution.py:25
  44.9 18.8 %copy-start.5 = (bf16[4,2,128,512]{3,2,1,0:T(8,128)(2,1)}, bf16[4,2,128,512]{3,2,1,0:T(8,128)(2,1)S(1)}, u32[]{:S(2)}) copy-start(bf16[4,2,128,512]{3,2,1,0:T(8,128)(2,1)S(1)} %collective-permute-done.3.refs_1_) | copy-start | bytes 3145732
  44.9 18.0 %collective-permute-start.7 = (bf16[4,2,128,512]{3,2,1,0:T(8,128)(2,1)S(1)}, bf16[4,2,128,512]{3,2,1,0:T(8,128)(2,1)}, u32[]{:S(2)}, u32[]{:S(2)}) collective-permute-start(bf16[4,2,128,512]{3,2,1,0:T(8,128)(2,1)S(1)} %collective-permute-done.3.refs_1_), channel_id=1, source_target_pairs={{0,1},{1,0},{2,3},{3,2},{4,5},{5,4},{6,7},{7,6},{8,9},{9,8},{10,11... | collective-permute-start | bytes 3145736 | tf_op jit(solution)/shard_map/ppermute | solution.py:25
  55.2 8.4 %copy-start.6 = (bf16[4,2,128,512]{3,2,1,0:T(8,128)(2,1)}, bf16[4,2,128,512]{3,2,1,0:T(8,128)(2,1)S(1)}, u32[]{:S(2)}) copy-start(bf16[4,2,128,512]{3,2,1,0:T(8,128)(2,1)S(1)} %collective-permute-done.4.refs_2_) | copy-start | bytes 3145732
  55.3 7.6 %collective-permute-start.8 = (bf16[4,2,128,512]{3,2,1,0:T(8,128)(2,1)S(1)}, bf16[4,2,128,512]{3,2,1,0:T(8,128)(2,1)}, u32[]{:S(2)}, u32[]{:S(2)}) collective-permute-start(bf16[4,2,128,512]{3,2,1,0:T(8,128)(2,1)S(1)} %collective-permute-done.4.refs_2_), channel_id=1, source_target_pairs={{0,1},{1,0},{2,3},{3,2},{4,5},{5,4},{6,7},{7,6},{8,9},{9,8},{10,11... | collective-permute-start | bytes 3145736 | tf_op jit(solution)/shard_map/ppermute | solution.py:25
  57.1 6.6 %collective-permute-start.9 = (bf16[4,2,128,512]{3,2,1,0:T(8,128)(2,1)}, bf16[4,2,128,512]{3,2,1,0:T(8,128)(2,1)}, u32[]{:S(2)}, u32[]{:S(2)}) collective-permute-start(bf16[4,2,128,512]{3,2,1,0:T(8,128)(2,1)} %collective-permute-done.5.refs_3_), channel_id=1, source_target_pairs={{0,1},{1,0},{2,3},{3,2},{4,5},{5,4},{6,7},{7,6},{8,9},{9,8},{10,11... | collective-permute-start | bytes 3145736 | tf_op jit(solution)/shard_map/ppermute | solution.py:25
  90.0 2.2 %copy-start = (bf16[16,2,4,128,128]{4,3,2,1,0:T(8,128)(2,1)S(1)}, bf16[16,2,4,128,128]{4,3,2,1,0:T(8,128)(2,1)}, u32[]{:S(2)}) copy-start(bf16[16,2,4,128,128]{4,3,2,1,0:T(8,128)(2,1)} %all-gather.3.cloned.1.call-done) | copy-start | bytes 12582916
  99.5 3.0 %collective-permute-start.12 = (bf16[4,2,128,512]{3,2,1,0:T(8,128)(2,1)S(1)}, bf16[4,2,128,512]{3,2,1,0:T(8,128)(2,1)S(1)}, u32[]{:S(2)}, u32[]{:S(2)}) collective-permute-start(bf16[4,2,128,512]{3,2,1,0:T(8,128)(2,1)S(1)} %get-tuple-element.43), channel_id=1, source_target_pairs={{0,1},{1,0},{2,3},{3,2},{4,5},{5,4},{6,7},{7,6},{8,9},{9,8},{10,11... | collective-permute-start | bytes 3145736 | tf_op jit(solution)/shard_map/ppermute | solution.py:25
  100.2 3.8 %collective-permute-start.16 = (bf16[4,2,128,512]{3,2,1,0:T(8,128)(2,1)S(1)}, bf16[4,2,128,512]{3,2,1,0:T(8,128)(2,1)S(1)}, u32[]{:S(2)}, u32[]{:S(2)}) collective-permute-start(bf16[4,2,128,512]{3,2,1,0:T(8,128)(2,1)S(1)} %get-tuple-element.41), channel_id=1, source_target_pairs={{0,1},{1,0},{2,3},{3,2},{4,5},{5,4},{6,7},{7,6},{8,9},{9,8},{10,11... | collective-permute-start | bytes 3145736 | tf_op jit(solution)/shard_map/ppermute | solution.py:25
  100.5 5.0 %collective-permute-start.14 = (bf16[4,2,128,512]{3,2,1,0:T(8,128)(2,1)S(1)}, bf16[4,2,128,512]{3,2,1,0:T(8,128)(2,1)S(1)}, u32[]{:S(2)}, u32[]{:S(2)}) collective-permute-start(bf16[4,2,128,512]{3,2,1,0:T(8,128)(2,1)S(1)} %get-tuple-element.42), channel_id=1, source_target_pairs={{0,1},{1,0},{2,3},{3,2},{4,5},{5,4},{6,7},{7,6},{8,9},{9,8},{10,11... | collective-permute-start | bytes 3145736 | tf_op jit(solution)/shard_map/ppermute | solution.py:25
  100.7 10.2 %collective-permute-start.11 = (bf16[4,2,128,512]{3,2,1,0:T(8,128)(2,1)S(1)}, bf16[4,2,128,512]{3,2,1,0:T(8,128)(2,1)S(1)}, u32[]{:S(2)}, u32[]{:S(2)}) collective-permute-start(bf16[4,2,128,512]{3,2,1,0:T(8,128)(2,1)S(1)} %get-tuple-element.40), channel_id=1, source_target_pairs={{0,1},{1,0},{2,3},{3,2},{4,5},{5,4},{6,7},{7,6},{8,9},{9,8},{10,11... | collective-permute-start | bytes 3145736 | tf_op jit(solution)/shard_map/ppermute | solution.py:25
  106.7 25.5 %collective-permute-start.17 = (bf16[4,2,128,512]{3,2,1,0:T(8,128)(2,1)S(1)}, bf16[4,2,128,512]{3,2,1,0:T(8,128)(2,1)S(1)}, u32[]{:S(2)}, u32[]{:S(2)}) collective-permute-start(bf16[4,2,128,512]{3,2,1,0:T(8,128)(2,1)S(1)} %get-tuple-element.45), channel_id=1, source_target_pairs={{0,130},{1,13},{2,0},{3,15},{4,134},{5,1},{6,4},{7,3},{8,138},{9,5... | collective-permute-start | bytes 3145736 | tf_op jit(solution)/shard_map/ppermute | solution.py:25
  109.2 26.5 %collective-permute-start.15 = (bf16[4,2,128,512]{3,2,1,0:T(8,128)(2,1)S(1)}, bf16[4,2,128,512]{3,2,1,0:T(8,128)(2,1)S(1)}, u32[]{:S(2)}, u32[]{:S(2)}) collective-permute-start(bf16[4,2,128,512]{3,2,1,0:T(8,128)(2,1)S(1)} %get-tuple-element.46), channel_id=1, source_target_pairs={{0,2},{1,5},{2,128},{3,7},{4,6},{5,9},{6,132},{7,11},{8,10},{9,13}... | collective-permute-start | bytes 3145736 | tf_op jit(solution)/shard_map/ppermute | solution.py:25
  109.2 26.5 %collective-permute-start.13 = (bf16[4,2,128,512]{3,2,1,0:T(8,128)(2,1)S(1)}, bf16[4,2,128,512]{3,2,1,0:T(8,128)(2,1)S(1)}, u32[]{:S(2)}, u32[]{:S(2)}) collective-permute-start(bf16[4,2,128,512]{3,2,1,0:T(8,128)(2,1)S(1)} %get-tuple-element.44), channel_id=1, source_target_pairs={{0,128},{1,9},{2,130},{3,11},{4,132},{5,13},{6,134},{7,15},{8,136}... | collective-permute-start | bytes 3145736 | tf_op jit(solution)/shard_map/ppermute | solution.py:25
  136.5 7.5 %collective-permute-start.18 = (bf16[2,128,512]{2,1,0:T(8,128)(2,1)S(1)}, bf16[2,128,512]{2,1,0:T(8,128)(2,1)S(1)}, u32[]{:S(2)}, u32[]{:S(2)}) collective-permute-start(bf16[2,128,512]{2,1,0:T(8,128)(2,1)S(1)} %get-tuple-element.51), channel_id=1, source_target_pairs={{0,8},{1,129},{2,10},{3,131},{4,12},{5,133},{6,14},{7,135},{8,0},{... | collective-permute-start | bytes 786440 | tf_op jit(solution)/shard_map/ppermute | solution.py:25
  139.3 7.1 %collective-permute-start.19 = (bf16[2,128,512]{2,1,0:T(8,128)(2,1)S(1)}, bf16[2,128,512]{2,1,0:T(8,128)(2,1)S(1)}, u32[]{:S(2)}, u32[]{:S(2)}) collective-permute-start(bf16[2,128,512]{2,1,0:T(8,128)(2,1)S(1)} %get-tuple-element.50), channel_id=1, source_target_pairs={{0,4},{1,3},{2,6},{3,129},{4,8},{5,7},{6,10},{7,133},{8,12},{9,11}... | collective-permute-start | bytes 786440 | tf_op jit(solution)/shard_map/ppermute | solution.py:25
  139.7 6.9 %collective-permute-start.20 = (bf16[2,128,512]{2,1,0:T(8,128)(2,1)S(1)}, bf16[2,128,512]{2,1,0:T(8,128)(2,1)S(1)}, u32[]{:S(2)}, u32[]{:S(2)}) collective-permute-start(bf16[2,128,512]{2,1,0:T(8,128)(2,1)S(1)} %get-tuple-element.49), channel_id=1, source_target_pairs={{0,12},{1,131},{2,14},{3,1},{4,0},{5,135},{6,2},{7,5},{8,4},{9,139... | collective-permute-start | bytes 786440 | tf_op jit(solution)/shard_map/ppermute | solution.py:25
  147.7 7.1 %collective-permute-start.21 = (bf16[2,4,128,128]{3,2,1,0:T(8,128)(2,1)S(1)}, bf16[2,4,128,128]{3,2,1,0:T(8,128)(2,1)S(1)}, u32[]{:S(2)}, u32[]{:S(2)}) collective-permute-start(bf16[2,4,128,128]{3,2,1,0:T(8,128)(2,1)S(1)} %pad_maximum_fusion.3), channel_id=1, source_target_pairs={{0,128},{1,129},{2,130},{3,131},{4,132},{5,133},{6,134},{7,135},{8... | collective-permute-start | bytes 786440 | tf_op jit(solution)/shard_map/ppermute | solution.py:25
  (3 other events, 3.0 us)
Sparse Core Ops, SparseCore 0:
  18.1 59.4 all-gather.2
  89.1 53.9 reduce-scatter.1

commit v3 on v2

--- a/solution.py
+++ b/solution.py
@@ -108,36 +108,43 @@
     def pick(scratch, j, s):
         return jnp.concatenate([scratch[j, s, 0], scratch[j, s, 1]], axis=1)
 
-    def column(j, carry):
-        pl.when(j < 3)(lambda: load(j + 1))
-        for target, sems in ((xs, sem_x), (gs, sem_g)):
-            pltpu.make_async_copy(target.at[j], target.at[j], sems.at[j]).wait()
-        load_w(j).wait()
-        hidden = jnp.zeros((2 * B, B), jnp.float32)
-        grad_act = jnp.zeros((2 * B, B), jnp.float32)
+    def two_columns(i, carry):
+        pl.when(i < 1)(lambda: [load(2), load(3)] and None)
+        pair = (2 * i, 2 * i + 1)
+        for j in pair:
+            for target, sems in ((xs, sem_x), (gs, sem_g)):
+                pltpu.make_async_copy(target.at[j], target.at[j], sems.at[j]).wait()
+            load_w(j).wait()
+        hidden = [jnp.zeros((2 * B, B), jnp.float32)] * 2
+        grad_act = [jnp.zeros((2 * B, B), jnp.float32)] * 2
         for s in range(8):
-            up = jnp.concatenate([ws[j, s, 0, 0], ws[j, s, 1, 0]], axis=0)
-            hidden += dot(pick(xs, j, s), up)
-            down = jnp.concatenate([ws[j, s, 0, 1], ws[j, s, 1, 1]], axis=1)
-            grad_act += dot(pick(gs, j, s), down, NT)
-        value, slope = gelu_parts(hidden)
-        grad_hidden = slope * grad_act
-        act_out[j] = value.astype(jnp.bfloat16)
-        gh_out[j] = grad_hidden.astype(jnp.bfloat16)
-        act_t = value.T.astype(jnp.bfloat16)
-        gh_t = grad_hidden.T.astype(jnp.bfloat16)
-        for s in range(8):
-            up = dot(gh_t, pick(xs, j, s)).astype(jnp.bfloat16)
-            grads[j, s, 0, 0] = up[:, :B]
-            grads[j, s, 1, 0] = up[:, B:]
-            down = dot(act_t, pick(gs, j, s)).astype(jnp.bfloat16)
-            grads[j, s, 0, 1] = down[:, :B]
-            grads[j, s, 1, 1] = down[:, B:]
-        store(j).start()
+            for n, j in enumerate(pair):
+                up = jnp.concatenate([ws[j, s, 0, 0], ws[j, s, 1, 0]], axis=0)
+                hidden[n] += dot(pick(xs, j, s), up)
+                down = jnp.concatenate([ws[j, s, 0, 1], ws[j, s, 1, 1]], axis=1)
+                grad_act[n] += dot(pick(gs, j, s), down, NT)
+        turned = []
+        for n, j in enumerate(pair):
+            value, slope = gelu_parts(hidden[n])
+            grad_hidden = slope * grad_act[n]
+            act_out[j] = value.astype(jnp.bfloat16)
+            gh_out[j] = grad_hidden.astype(jnp.bfloat16)
+            turned.append((value.T.astype(jnp.bfloat16), grad_hidden.T.astype(jnp.bfloat16)))
+        for n, j in enumerate(pair):
+            act_t, gh_t = turned[n]
+            for s in range(8):
+                up = dot(gh_t, pick(xs, j, s)).astype(jnp.bfloat16)
+                grads[j, s, 0, 0] = up[:, :B]
+                grads[j, s, 1, 0] = up[:, B:]
+                down = dot(act_t, pick(gs, j, s)).astype(jnp.bfloat16)
+                grads[j, s, 0, 1] = down[:, :B]
+                grads[j, s, 1, 1] = down[:, B:]
+            store(j).start()
         return carry
 
     load(0)
-    lax.fori_loop(0, 4, column, 0)
+    load(1)
+    lax.fori_loop(0, 2, two_columns, 0)
     for j in range(4):
         store(j).wait()
 
@@ -318,12 +325,13 @@
 
     last = scatter_plane(parts)
     other = send(jnp.stack([jnp.swapaxes(summed[1, 0], 1, 2), summed[1, 1]]), other_half)
-    own, last = lax.optimization_barrier((summed[0], last))
+    own = lax.optimization_barrier(summed[0])
     own = jnp.stack([jnp.swapaxes(own[0], 1, 2), own[1]])
     grads = jnp.where(
         yh == 0, jnp.concatenate([own, other], axis=1), jnp.concatenate([other, own], axis=1)
     ).astype(f32)
     grad_up, grad_down = grads[0][:, None], grads[1][:, None]
+    last, grad_up = lax.optimization_barrier((last, grad_up))
     result = total(last).astype(bf16)
     mixed, grad_tokens = result[0], result[1]
     return mixed, grad_tokens, grad_up, grad_down

time: 165 us -> 161 us (0.976); the launches traced: 163 us -> 161 us
    ppermute x22, waiting for transfers between devices: 62.5 us -> 59.5 us  [send(): lax.ppermute(value, AXES, [(source, place_of(*step(*where_is(source)))) f...]
    reduce_scatter x1, waiting for transfers between devices: 1.07 us -> 2.96 us  [local(): lax.psum_scatter(grads, 'dp', scatter_dimension=0, axis_index_groups=HALV...]
  transfers between devices with their start and end apart: 24 -> 24, of which waited for: 18 -> 17; matrix products, arithmetic and copies ran while one was open for 5% -> 6% of each run, Pallas kernels for 9% -> 9%
where the time goes in v3:
time: 161 us
  waiting for transfers between devices  68.5 us (43%)
  starting transfers between devices  37.9 us (24%)
  Pallas kernels  25.2 us (16%)
  between operations  14.3 us (9%)
  local copies, waits for them, and re-layouts  7.96 us (5%)
  other arithmetic  6.69 us (4%)
    ppermute x22, waiting for transfers between devices, send(): lax.ppermute(value, AXES, [(source, place_of(*step(*where_is(source)))) f...  59.5 us
    ppermute x22, starting transfers between devices, send(): lax.ppermute(value, AXES, [(source, place_of(*step(*where_is(source)))) f...  37.8 us
    pallas_call x1, Pallas kernels, local(): pl.pallas_call(first_kernel, out_shape=[jax.ShapeDtypeStruct((4, 2 * B, B...  10 us
    pallas_call x1, Pallas kernels, local(): pl.pallas_call(place_kernel, out_shape=[gathered] * 2, in_specs=[SMEM] +...  8.19 us
    pallas_call x1, Pallas kernels, local(): pl.pallas_call(second_kernel, out_shape=jax.ShapeDtypeStruct((8, 4, 2, B,...  7.04 us
    all_gather x1, waiting for transfers between devices, local(): lax.all_gather(jnp.stack([piece_a, other_b]), 'dp', axis_index_groups=HAL...  6.05 us
    unnamed x24, local copies, waits for them, and re-layouts  3.99 us
  transfers between devices with their start and end apart: 24, of which 17 were waited for; matrix products, arithmetic and copies ran while one was open for 6% of the time, Pallas kernels for 9%

profile of v3, /device:TPU:1, one launch (start us, length us, event | category | flops | bytes accessed | tf_op | source)
XLA Modules:
  0.0 160.6 jit_solution(7082639719532483768)
XLA Ops:
  8.3 3.8 %collective-permute-start.10 = (bf16[2,4,128,128]{3,2,1,0:T(8,128)(2,1)S(1)}, bf16[2,4,128,128]{3,2,1,0:T(8,128)(2,1)S(1)}, u32[]{:S(2)}, u32[]{:S(2)}) collective-permute-start(bf16[2,4,128,128]{3,2,1,0:T(8,128)(2,1)S(1)} %fusion.5), channel_id=1, source_target_pairs={{0,128},{1,129},{2,130},{3,131},{4,132},{5,133},{6,134},{7,135},{8... | collective-permute-start | bytes 786440 | tf_op jit(solution)/shard_map/ppermute | solution.py:25
  13.1 4.0 %collective-permute-done.10 = bf16[2,4,128,128]{3,2,1,0:T(8,128)(2,1)S(1)} collective-permute-done((bf16[2,4,128,128]{3,2,1,0:T(8,128)(2,1)S(1)}, bf16[2,4,128,128]{3,2,1,0:T(8,128)(2,1)S(1)}, u32[]{:S(2)}, u32[]{:S(2)}) %collective-permute-start.10) | collective-permute-done | bytes 262176 | tf_op jit(solution)/shard_map/ppermute | solution.py:25
  18.1 2.2 %collective-permute-start = (bf16[2,128,512]{2,1,0:T(8,128)(2,1)S(1)}, bf16[2,128,512]{2,1,0:T(8,128)(2,1)S(1)}, u32[]{:S(2)}, u32[]{:S(2)}) collective-permute-start(bf16[2,128,512]{2,1,0:T(8,128)(2,1)S(1)} %get-tuple-element.60), channel_id=1, source_target_pairs={{0,4},{1,3},{2,6},{3,129},{4,8},{5,7},{6,10},{7,133},{8,12},{9,11}... | collective-permute-start | bytes 786440 | tf_op jit(solution)/shard_map/ppermute | solution.py:25
  20.2 1.5 collective-permute-start.1
  21.8 1.6 collective-permute-start.2
  23.3 2.4 %collective-permute-done = bf16[2,128,512]{2,1,0:T(8,128)(2,1)S(1)} collective-permute-done((bf16[2,128,512]{2,1,0:T(8,128)(2,1)S(1)}, bf16[2,128,512]{2,1,0:T(8,128)(2,1)S(1)}, u32[]{:S(2)}, u32[]{:S(2)}) %collective-permute-start) | collective-permute-done | bytes 262176 | tf_op jit(solution)/shard_map/ppermute | solution.py:25
  25.7 2.2 %collective-permute-done.1 = bf16[2,128,512]{2,1,0:T(8,128)(2,1)S(1)} collective-permute-done((bf16[2,128,512]{2,1,0:T(8,128)(2,1)S(1)}, bf16[2,128,512]{2,1,0:T(8,128)(2,1)S(1)}, u32[]{:S(2)}, u32[]{:S(2)}) %collective-permute-start.1) | collective-permute-done | bytes 262176 | tf_op jit(solution)/shard_map/ppermute | solution.py:25
  27.9 1.8 %collective-permute-done.2 = bf16[2,128,512]{2,1,0:T(8,128)(2,1)S(1)} collective-permute-done((bf16[2,128,512]{2,1,0:T(8,128)(2,1)S(1)}, bf16[2,128,512]{2,1,0:T(8,128)(2,1)S(1)}, u32[]{:S(2)}, u32[]{:S(2)}) %collective-permute-start.2) | collective-permute-done | bytes 262176 | tf_op jit(solution)/shard_map/ppermute | solution.py:25
  30.9 1.8 %collective-permute-start.4 = (bf16[4,2,128,512]{3,2,1,0:T(8,128)(2,1)S(1)}, bf16[4,2,128,512]{3,2,1,0:T(8,128)(2,1)S(1)}, u32[]{:S(2)}, u32[]{:S(2)}) collective-permute-start(bf16[4,2,128,512]{3,2,1,0:T(8,128)(2,1)S(1)} %pad_maximum_fusion.refs_0_), channel_id=1, source_target_pairs={{0,130},{1,13},{2,0},{3,15},{4,134},{5,1},{6,4},{7,3},{8,138},{9,5... | collective-permute-start | bytes 3145736 | tf_op jit(solution)/shard_map/ppermute | solution.py:25
  33.9 3.5 %collective-permute-start.6 = (bf16[4,2,128,512]{3,2,1,0:T(8,128)(2,1)S(1)}, bf16[4,2,128,512]{3,2,1,0:T(8,128)(2,1)}, u32[]{:S(2)}, u32[]{:S(2)}) collective-permute-start(bf16[4,2,128,512]{3,2,1,0:T(8,128)(2,1)S(1)} %pad_maximum_fusion.refs_0_), channel_id=1, source_target_pairs={{0,1},{1,0},{2,3},{3,2},{4,5},{5,4},{6,7},{7,6},{8,9},{9,8},{10,11... | collective-permute-start | bytes 3145736 | tf_op jit(solution)/shard_map/ppermute | solution.py:25
  37.3 7.9 %collective-permute-done.3.refs_1_ = bf16[4,2,128,512]{3,2,1,0:T(8,128)(2,1)S(1)} collective-permute-done((bf16[4,2,128,512]{3,2,1,0:T(8,128)(2,1)S(1)}, bf16[4,2,128,512]{3,2,1,0:T(8,128)(2,1)S(1)}, u32[]{:S(2)}, u32[]{:S(2)}) %collective-permute-start.3) | collective-permute-done | bytes 1048608 | tf_op jit(solution)/shard_map/ppermute | solution.py:25
  45.2 2.9 %collective-permute-start.7 = (bf16[4,2,128,512]{3,2,1,0:T(8,128)(2,1)S(1)}, bf16[4,2,128,512]{3,2,1,0:T(8,128)(2,1)}, u32[]{:S(2)}, u32[]{:S(2)}) collective-permute-start(bf16[4,2,128,512]{3,2,1,0:T(8,128)(2,1)S(1)} %collective-permute-done.3.refs_1_), channel_id=1, source_target_pairs={{0,1},{1,0},{2,3},{3,2},{4,5},{5,4},{6,7},{7,6},{8,9},{9,8},{10,11... | collective-permute-start | bytes 3145736 | tf_op jit(solution)/shard_map/ppermute | solution.py:25
  48.1 7.5 %collective-permute-done.4.refs_2_ = bf16[4,2,128,512]{3,2,1,0:T(8,128)(2,1)S(1)} collective-permute-done((bf16[4,2,128,512]{3,2,1,0:T(8,128)(2,1)S(1)}, bf16[4,2,128,512]{3,2,1,0:T(8,128)(2,1)S(1)}, u32[]{:S(2)}, u32[]{:S(2)}) %collective-permute-start.4) | collective-permute-done | bytes 1048608 | tf_op jit(solution)/shard_map/ppermute | solution.py:25
  55.6 1.8 %collective-permute-done.5.refs_3_ = bf16[4,2,128,512]{3,2,1,0:T(8,128)(2,1)} collective-permute-done((bf16[4,2,128,512]{3,2,1,0:T(8,128)(2,1)S(1)}, bf16[4,2,128,512]{3,2,1,0:T(8,128)(2,1)}, u32[]{:S(2)}, u32[]{:S(2)}) %collective-permute-start.5) | collective-permute-done | bytes 1048608 | tf_op jit(solution)/shard_map/ppermute | solution.py:25
  57.4 3.3 %collective-permute-start.9 = (bf16[4,2,128,512]{3,2,1,0:T(8,128)(2,1)}, bf16[4,2,128,512]{3,2,1,0:T(8,128)(2,1)}, u32[]{:S(2)}, u32[]{:S(2)}) collective-permute-start(bf16[4,2,128,512]{3,2,1,0:T(8,128)(2,1)} %collective-permute-done.5.refs_3_), channel_id=1, source_target_pairs={{0,1},{1,0},{2,3},{3,2},{4,5},{5,4},{6,7},{7,6},{8,9},{9,8},{10,11... | collective-permute-start | bytes 3145736 | tf_op jit(solution)/shard_map/ppermute | solution.py:25
  63.3 8.2 %place.1 = (bf16[16,256,512]{2,1,0:T(8,128)(2,1)}, bf16[16,256,512]{2,1,0:T(8,128)(2,1)}) custom-call(s32[32]{0:T(128)} %pad_add_fusion.spots, bf16[4,2,128,512]{3,2,1,0:T(8,128)(2,1)} %copy-done.4, bf16[4,2,128,512]{3,2,1,0:T(8,128)(2,1)} %copy-done.5, bf16[4,2,128,512]{3,2,1,0:T(8,128)(2,1)} %copy-done.6, ...), custom_call_target="tpu_custom_call" | custom-call | bytes 16777216 | tf_op jit(solution)/shard_map/place/pallas_call | solution.py:265
  71.5 6.1 %all-gather.3.cloned.1.call-done = bf16[16,2,4,128,128]{4,3,2,1,0:T(8,128)(2,1)} async-done(((bf16[2,2,4,128,128]{4,3,2,1,0:T(8,128)(2,1)}), bf16[16,2,4,128,128]{4,3,2,1,0:T(8,128)(2,1)}) %all-gather.3.cloned.1.call-update) | async-done | bytes 4194320 | tf_op jit(solution)/shard_map/all_gather | solution.py:260
  77.6 10.0 %first.1 = (bf16[4,256,128]{2,1,0:T(8,128)(2,1)}, bf16[4,256,128]{2,1,0:T(8,128)(2,1)}, bf16[8,2,2,4,128,128]{5,4,3,2,1,0:T(8,128)(2,1)}) custom-call(s32[4,16]{1,0:T(4,128)} %add_select_fusion.rows, bf16[16,256,512]{2,1,0:T(8,128)(2,1)} %get-tuple-element.16.x_in, bf16[16,256,512]{2,1,0:T(8,128)(2,1)} %get-tuple-element.17.g_in, ...), custom_call_target="tpu_custom_call" | custom-call | flops 2000000000 | bytes 16777216 | tf_op jit(solution)/shard_map/first/pallas_call | solution.py:281
  88.6 2.2 %copy-done = bf16[16,2,4,128,128]{4,3,2,1,0:T(8,128)(2,1)S(1)} copy-done((bf16[16,2,4,128,128]{4,3,2,1,0:T(8,128)(2,1)S(1)}, bf16[16,2,4,128,128]{4,3,2,1,0:T(8,128)(2,1)}, u32[]{:S(2)}) %copy-start) | copy-done | bytes 4194328
  90.8 7.0 %second.1 = bf16[8,4,2,128,512]{4,3,2,1,0:T(8,128)(2,1)S(1)} custom-call(s32[128]{0:T(128)S(1)} %add.279.outs_at, s32[4,16]{1,0:T(4,128)S(1)} %copy-done.3, bf16[4,256,128]{2,1,0:T(8,128)(2,1)S(1)} %copy-done.1, bf16[4,256,128]{2,1,0:T(8,128)(2,1)S(1)} %copy-done.2, bf16[8,2,2,4,128,128]{5,4,3,2,1,0:T(8,128)(2,1)S(1)} %bitcast.87), custom_call_target="tpu_custom_call" | custom-call | flops 1000000000 | bytes 16777216 | tf_op jit(solution)/shard_map/second/pallas_call | solution.py:308
  99.7 1.7 %collective-permute-done.12 = bf16[4,2,128,512]{3,2,1,0:T(8,128)(2,1)S(1)} collective-permute-done((bf16[4,2,128,512]{3,2,1,0:T(8,128)(2,1)S(1)}, bf16[4,2,128,512]{3,2,1,0:T(8,128)(2,1)S(1)}, u32[]{:S(2)}, u32[]{:S(2)}) %collective-permute-start.12) | collective-permute-done | bytes 1048608 | tf_op jit(solution)/shard_map/ppermute | solution.py:25
  101.4 1.5 collective-permute-done.14
  102.8 1.5 collective-permute-done.16
  105.5 2.8 %collective-permute-start.13 = (bf16[4,2,128,512]{3,2,1,0:T(8,128)(2,1)S(1)}, bf16[4,2,128,512]{3,2,1,0:T(8,128)(2,1)S(1)}, u32[]{:S(2)}, u32[]{:S(2)}) collective-permute-start(bf16[4,2,128,512]{3,2,1,0:T(8,128)(2,1)S(1)} %get-tuple-element.44), channel_id=1, source_target_pairs={{0,128},{1,9},{2,130},{3,11},{4,132},{5,13},{6,134},{7,15},{8,136}... | collective-permute-start | bytes 3145736 | tf_op jit(solution)/shard_map/ppermute | solution.py:25
  108.6 2.4 %collective-permute-start.17 = (bf16[4,2,128,512]{3,2,1,0:T(8,128)(2,1)S(1)}, bf16[4,2,128,512]{3,2,1,0:T(8,128)(2,1)S(1)}, u32[]{:S(2)}, u32[]{:S(2)}) collective-permute-start(bf16[4,2,128,512]{3,2,1,0:T(8,128)(2,1)S(1)} %get-tuple-element.45), channel_id=1, source_target_pairs={{0,130},{1,13},{2,0},{3,15},{4,134},{5,1},{6,4},{7,3},{8,138},{9,5... | collective-permute-start | bytes 3145736 | tf_op jit(solution)/shard_map/ppermute | solution.py:25
  111.0 10.1 %collective-permute-done.13 = bf16[4,2,128,512]{3,2,1,0:T(8,128)(2,1)S(1)} collective-permute-done((bf16[4,2,128,512]{3,2,1,0:T(8,128)(2,1)S(1)}, bf16[4,2,128,512]{3,2,1,0:T(8,128)(2,1)S(1)}, u32[]{:S(2)}, u32[]{:S(2)}) %collective-permute-start.13) | collective-permute-done | bytes 1048608 | tf_op jit(solution)/shard_map/ppermute | solution.py:25
  121.1 11.3 %collective-permute-done.15 = bf16[4,2,128,512]{3,2,1,0:T(8,128)(2,1)S(1)} collective-permute-done((bf16[4,2,128,512]{3,2,1,0:T(8,128)(2,1)S(1)}, bf16[4,2,128,512]{3,2,1,0:T(8,128)(2,1)S(1)}, u32[]{:S(2)}, u32[]{:S(2)}) %collective-permute-start.15) | collective-permute-done | bytes 1048608 | tf_op jit(solution)/shard_map/ppermute | solution.py:25
  133.3 2.8 %collective-permute-start.18 = (bf16[2,128,512]{2,1,0:T(8,128)(2,1)S(1)}, bf16[2,128,512]{2,1,0:T(8,128)(2,1)S(1)}, u32[]{:S(2)}, u32[]{:S(2)}) collective-permute-start(bf16[2,128,512]{2,1,0:T(8,128)(2,1)S(1)} %get-tuple-element.51), channel_id=1, source_target_pairs={{0,8},{1,129},{2,10},{3,131},{4,12},{5,133},{6,14},{7,135},{8,0},{... | collective-permute-start | bytes 786440 | tf_op jit(solution)/shard_map/ppermute | solution.py:25
  136.4 2.4 %collective-permute-start.20 = (bf16[2,128,512]{2,1,0:T(8,128)(2,1)S(1)}, bf16[2,128,512]{2,1,0:T(8,128)(2,1)S(1)}, u32[]{:S(2)}, u32[]{:S(2)}) collective-permute-start(bf16[2,128,512]{2,1,0:T(8,128)(2,1)S(1)} %get-tuple-element.49), channel_id=1, source_target_pairs={{0,12},{1,131},{2,14},{3,1},{4,0},{5,135},{6,2},{7,5},{8,4},{9,139... | collective-permute-start | bytes 786440 | tf_op jit(solution)/shard_map/ppermute | solution.py:25
  138.8 3.0 %reduce-scatter.2.cloned.1.call-done = bf16[1,2,2,4,128,128]{5,4,3,2,1,0:T(8,128)(2,1)} async-done(((bf16[8,2,2,4,128,128]{5,4,3,2,1,0:T(8,128)(2,1)}), bf16[1,2,2,4,128,128]{5,4,3,2,1,0:T(8,128)(2,1)}) %reduce-scatter.2.cloned.1.call-update) | async-done | bytes 524304 | tf_op jit(solution)/shard_map/reduce_scatter | solution.py:304
  142.9 2.8 %collective-permute-start.21 = (bf16[2,4,128,128]{3,2,1,0:T(8,128)(2,1)S(1)}, bf16[2,4,128,128]{3,2,1,0:T(8,128)(2,1)S(1)}, u32[]{:S(2)}, u32[]{:S(2)}) collective-permute-start(bf16[2,4,128,128]{3,2,1,0:T(8,128)(2,1)S(1)} %pad_maximum_fusion.3), channel_id=1, source_target_pairs={{0,128},{1,129},{2,130},{3,131},{4,132},{5,133},{6,134},{7,135},{8... | collective-permute-start | bytes 786440 | tf_op jit(solution)/shard_map/ppermute | solution.py:25
  146.9 4.9 %collective-permute-done.21 = bf16[2,4,128,128]{3,2,1,0:T(8,128)(2,1)S(1)} collective-permute-done((bf16[2,4,128,128]{3,2,1,0:T(8,128)(2,1)S(1)}, bf16[2,4,128,128]{3,2,1,0:T(8,128)(2,1)S(1)}, u32[]{:S(2)}, u32[]{:S(2)}) %collective-permute-start.21) | collective-permute-done | bytes 262176 | tf_op jit(solution)/shard_map/ppermute | solution.py:25
  (79 shorter events, 17.7 us)
Async XLA Ops:
  7.2 10.8 %copy-start.8 = (bf16[128,512]{1,0:T(8,128)(2,1)S(1)}, bf16[128,512]{1,0:T(8,128)(2,1)}, u32[]{:S(2)}) copy-start(bf16[128,512]{1,0:T(8,128)(2,1)} %param.7) | copy-start | bytes 393220
  7.2 10.8 %copy-start.7 = (bf16[128,512]{1,0:T(8,128)(2,1)S(1)}, bf16[128,512]{1,0:T(8,128)(2,1)}, u32[]{:S(2)}) copy-start(bf16[128,512]{1,0:T(8,128)(2,1)} %param.11) | copy-start | bytes 393220
  7.2 70.4 %all-gather.3.cloned.1.call-start = ((), (), s32[]{:S(2)}) async-start(), calls=%async_computation.2 | async-start | bytes 4718592 | tf_op jit(solution)/shard_map/all_gather | solution.py:260
  8.3 8.8 %collective-permute-start.10 = (bf16[2,4,128,128]{3,2,1,0:T(8,128)(2,1)S(1)}, bf16[2,4,128,128]{3,2,1,0:T(8,128)(2,1)S(1)}, u32[]{:S(2)}, u32[]{:S(2)}) collective-permute-start(bf16[2,4,128,128]{3,2,1,0:T(8,128)(2,1)S(1)} %fusion.5), channel_id=1, source_target_pairs={{0,128},{1,129},{2,130},{3,131},{4,132},{5,133},{6,134},{7,135},{8... | collective-permute-start | bytes 786440 | tf_op jit(solution)/shard_map/ppermute | solution.py:25
  17.1 43.6 %copy-start.10 = (s32[4]{0:T(128)S(1)}, s32[4]{0:T(128)}, u32[]{:S(2)}) copy-start(s32[4]{0:T(128)} %constant.182.clone) | copy-start | bytes 52
  17.1 44.6 %copy-start.9 = (s32[8,16]{1,0:T(8,128)S(1)}, s32[8,16]{1,0:T(8,128)}, u32[]{:S(2)}) copy-start(s32[8,16]{1,0:T(8,128)} %param.8) | copy-start | bytes 1540
  18.0 123.8 %reduce-scatter.2.cloned.1.call-start = ((), (), s32[]{:S(2)}) async-start(), calls=%async_computation.1 | async-start | bytes 4718592 | tf_op jit(solution)/shard_map/reduce_scatter | solution.py:304
  18.1 7.7 %collective-permute-start = (bf16[2,128,512]{2,1,0:T(8,128)(2,1)S(1)}, bf16[2,128,512]{2,1,0:T(8,128)(2,1)S(1)}, u32[]{:S(2)}, u32[]{:S(2)}) collective-permute-start(bf16[2,128,512]{2,1,0:T(8,128)(2,1)S(1)} %get-tuple-element.60), channel_id=1, source_target_pairs={{0,4},{1,3},{2,6},{3,129},{4,8},{5,7},{6,10},{7,133},{8,12},{9,11}... | collective-permute-start | bytes 786440 | tf_op jit(solution)/shard_map/ppermute | solution.py:25
  20.2 7.7 %collective-permute-start.1 = (bf16[2,128,512]{2,1,0:T(8,128)(2,1)S(1)}, bf16[2,128,512]{2,1,0:T(8,128)(2,1)S(1)}, u32[]{:S(2)}, u32[]{:S(2)}) collective-permute-start(bf16[2,128,512]{2,1,0:T(8,128)(2,1)S(1)} %get-tuple-element.60), channel_id=1, source_target_pairs={{0,12},{1,131},{2,14},{3,1},{4,0},{5,135},{6,2},{7,5},{8,4},{9,139... | collective-permute-start | bytes 786440 | tf_op jit(solution)/shard_map/ppermute | solution.py:25
  21.8 8.0 %collective-permute-start.2 = (bf16[2,128,512]{2,1,0:T(8,128)(2,1)S(1)}, bf16[2,128,512]{2,1,0:T(8,128)(2,1)S(1)}, u32[]{:S(2)}, u32[]{:S(2)}) collective-permute-start(bf16[2,128,512]{2,1,0:T(8,128)(2,1)S(1)} %get-tuple-element.60), channel_id=1, source_target_pairs={{0,8},{1,129},{2,10},{3,131},{4,12},{5,133},{6,14},{7,135},{8,0},{... | collective-permute-start | bytes 786440 | tf_op jit(solution)/shard_map/ppermute | solution.py:25
  29.9 33.5 %copy-start.4 = (bf16[4,2,128,512]{3,2,1,0:T(8,128)(2,1)}, bf16[4,2,128,512]{3,2,1,0:T(8,128)(2,1)S(1)}, u32[]{:S(2)}) copy-start(bf16[4,2,128,512]{3,2,1,0:T(8,128)(2,1)S(1)} %pad_maximum_fusion.refs_0_) | copy-start | bytes 3145732
  29.9 15.3 %collective-permute-start.3 = (bf16[4,2,128,512]{3,2,1,0:T(8,128)(2,1)S(1)}, bf16[4,2,128,512]{3,2,1,0:T(8,128)(2,1)S(1)}, u32[]{:S(2)}, u32[]{:S(2)}) collective-permute-start(bf16[4,2,128,512]{3,2,1,0:T(8,128)(2,1)S(1)} %pad_maximum_fusion.refs_0_), channel_id=1, source_target_pairs={{0,2},{1,5},{2,128},{3,7},{4,6},{5,9},{6,132},{7,11},{8,10},{9,13}... | collective-permute-start | bytes 3145736 | tf_op jit(solution)/shard_map/ppermute | solution.py:25
  30.9 24.7 %collective-permute-start.4 = (bf16[4,2,128,512]{3,2,1,0:T(8,128)(2,1)S(1)}, bf16[4,2,128,512]{3,2,1,0:T(8,128)(2,1)S(1)}, u32[]{:S(2)}, u32[]{:S(2)}) collective-permute-start(bf16[4,2,128,512]{3,2,1,0:T(8,128)(2,1)S(1)} %pad_maximum_fusion.refs_0_), channel_id=1, source_target_pairs={{0,130},{1,13},{2,0},{3,15},{4,134},{5,1},{6,4},{7,3},{8,138},{9,5... | collective-permute-start | bytes 3145736 | tf_op jit(solution)/shard_map/ppermute | solution.py:25
  32.6 24.8 %collective-permute-start.5 = (bf16[4,2,128,512]{3,2,1,0:T(8,128)(2,1)S(1)}, bf16[4,2,128,512]{3,2,1,0:T(8,128)(2,1)}, u32[]{:S(2)}, u32[]{:S(2)}) collective-permute-start(bf16[4,2,128,512]{3,2,1,0:T(8,128)(2,1)S(1)} %pad_maximum_fusion.refs_0_), channel_id=1, source_target_pairs={{0,128},{1,9},{2,130},{3,11},{4,132},{5,13},{6,134},{7,15},{8,136}... | collective-permute-start | bytes 3145736 | tf_op jit(solution)/shard_map/ppermute | solution.py:25
  33.9 28.6 %collective-permute-start.6 = (bf16[4,2,128,512]{3,2,1,0:T(8,128)(2,1)S(1)}, bf16[4,2,128,512]{3,2,1,0:T(8,128)(2,1)}, u32[]{:S(2)}, u32[]{:S(2)}) collective-permute-start(bf16[4,2,128,512]{3,2,1,0:T(8,128)(2,1)S(1)} %pad_maximum_fusion.refs_0_), channel_id=1, source_target_pairs={{0,1},{1,0},{2,3},{3,2},{4,5},{5,4},{6,7},{7,6},{8,9},{9,8},{10,11... | collective-permute-start | bytes 3145736 | tf_op jit(solution)/shard_map/ppermute | solution.py:25
  45.2 18.1 %copy-start.5 = (bf16[4,2,128,512]{3,2,1,0:T(8,128)(2,1)}, bf16[4,2,128,512]{3,2,1,0:T(8,128)(2,1)S(1)}, u32[]{:S(2)}) copy-start(bf16[4,2,128,512]{3,2,1,0:T(8,128)(2,1)S(1)} %collective-permute-done.3.refs_1_) | copy-start | bytes 3145732
  45.2 17.2 %collective-permute-start.7 = (bf16[4,2,128,512]{3,2,1,0:T(8,128)(2,1)S(1)}, bf16[4,2,128,512]{3,2,1,0:T(8,128)(2,1)}, u32[]{:S(2)}, u32[]{:S(2)}) collective-permute-start(bf16[4,2,128,512]{3,2,1,0:T(8,128)(2,1)S(1)} %collective-permute-done.3.refs_1_), channel_id=1, source_target_pairs={{0,1},{1,0},{2,3},{3,2},{4,5},{5,4},{6,7},{7,6},{8,9},{9,8},{10,11... | collective-permute-start | bytes 3145736 | tf_op jit(solution)/shard_map/ppermute | solution.py:25
  55.6 7.7 %copy-start.6 = (bf16[4,2,128,512]{3,2,1,0:T(8,128)(2,1)}, bf16[4,2,128,512]{3,2,1,0:T(8,128)(2,1)S(1)}, u32[]{:S(2)}) copy-start(bf16[4,2,128,512]{3,2,1,0:T(8,128)(2,1)S(1)} %collective-permute-done.4.refs_2_) | copy-start | bytes 3145732
  55.6 6.9 %collective-permute-start.8 = (bf16[4,2,128,512]{3,2,1,0:T(8,128)(2,1)S(1)}, bf16[4,2,128,512]{3,2,1,0:T(8,128)(2,1)}, u32[]{:S(2)}, u32[]{:S(2)}) collective-permute-start(bf16[4,2,128,512]{3,2,1,0:T(8,128)(2,1)S(1)} %collective-permute-done.4.refs_2_), channel_id=1, source_target_pairs={{0,1},{1,0},{2,3},{3,2},{4,5},{5,4},{6,7},{7,6},{8,9},{9,8},{10,11... | collective-permute-start | bytes 3145736 | tf_op jit(solution)/shard_map/ppermute | solution.py:25
  57.4 5.9 %collective-permute-start.9 = (bf16[4,2,128,512]{3,2,1,0:T(8,128)(2,1)}, bf16[4,2,128,512]{3,2,1,0:T(8,128)(2,1)}, u32[]{:S(2)}, u32[]{:S(2)}) collective-permute-start(bf16[4,2,128,512]{3,2,1,0:T(8,128)(2,1)} %collective-permute-done.5.refs_3_), channel_id=1, source_target_pairs={{0,1},{1,0},{2,3},{3,2},{4,5},{5,4},{6,7},{7,6},{8,9},{9,8},{10,11... | collective-permute-start | bytes 3145736 | tf_op jit(solution)/shard_map/ppermute | solution.py:25
  88.6 2.2 %copy-start = (bf16[16,2,4,128,128]{4,3,2,1,0:T(8,128)(2,1)S(1)}, bf16[16,2,4,128,128]{4,3,2,1,0:T(8,128)(2,1)}, u32[]{:S(2)}) copy-start(bf16[16,2,4,128,128]{4,3,2,1,0:T(8,128)(2,1)} %all-gather.3.cloned.1.call-done) | copy-start | bytes 12582916
  98.3 3.0 %collective-permute-start.12 = (bf16[4,2,128,512]{3,2,1,0:T(8,128)(2,1)S(1)}, bf16[4,2,128,512]{3,2,1,0:T(8,128)(2,1)S(1)}, u32[]{:S(2)}, u32[]{:S(2)}) collective-permute-start(bf16[4,2,128,512]{3,2,1,0:T(8,128)(2,1)S(1)} %get-tuple-element.43), channel_id=1, source_target_pairs={{0,1},{1,0},{2,3},{3,2},{4,5},{5,4},{6,7},{7,6},{8,9},{9,8},{10,11... | collective-permute-start | bytes 3145736 | tf_op jit(solution)/shard_map/ppermute | solution.py:25
  99.1 3.8 %collective-permute-start.14 = (bf16[4,2,128,512]{3,2,1,0:T(8,128)(2,1)S(1)}, bf16[4,2,128,512]{3,2,1,0:T(8,128)(2,1)S(1)}, u32[]{:S(2)}, u32[]{:S(2)}) collective-permute-start(bf16[4,2,128,512]{3,2,1,0:T(8,128)(2,1)S(1)} %get-tuple-element.42), channel_id=1, source_target_pairs={{0,1},{1,0},{2,3},{3,2},{4,5},{5,4},{6,7},{7,6},{8,9},{9,8},{10,11... | collective-permute-start | bytes 3145736 | tf_op jit(solution)/shard_map/ppermute | solution.py:25
  99.2 5.2 %collective-permute-start.16 = (bf16[4,2,128,512]{3,2,1,0:T(8,128)(2,1)S(1)}, bf16[4,2,128,512]{3,2,1,0:T(8,128)(2,1)S(1)}, u32[]{:S(2)}, u32[]{:S(2)}) collective-permute-start(bf16[4,2,128,512]{3,2,1,0:T(8,128)(2,1)S(1)} %get-tuple-element.41), channel_id=1, source_target_pairs={{0,1},{1,0},{2,3},{3,2},{4,5},{5,4},{6,7},{7,6},{8,9},{9,8},{10,11... | collective-permute-start | bytes 3145736 | tf_op jit(solution)/shard_map/ppermute | solution.py:25
  99.6 11.4 %collective-permute-start.11 = (bf16[4,2,128,512]{3,2,1,0:T(8,128)(2,1)S(1)}, bf16[4,2,128,512]{3,2,1,0:T(8,128)(2,1)S(1)}, u32[]{:S(2)}, u32[]{:S(2)}) collective-permute-start(bf16[4,2,128,512]{3,2,1,0:T(8,128)(2,1)S(1)} %get-tuple-element.40), channel_id=1, source_target_pairs={{0,1},{1,0},{2,3},{3,2},{4,5},{5,4},{6,7},{7,6},{8,9},{9,8},{10,11... | collective-permute-start | bytes 3145736 | tf_op jit(solution)/shard_map/ppermute | solution.py:25
  105.5 15.6 %collective-permute-start.13 = (bf16[4,2,128,512]{3,2,1,0:T(8,128)(2,1)S(1)}, bf16[4,2,128,512]{3,2,1,0:T(8,128)(2,1)S(1)}, u32[]{:S(2)}, u32[]{:S(2)}) collective-permute-start(bf16[4,2,128,512]{3,2,1,0:T(8,128)(2,1)S(1)} %get-tuple-element.44), channel_id=1, source_target_pairs={{0,128},{1,9},{2,130},{3,11},{4,132},{5,13},{6,134},{7,15},{8,136}... | collective-permute-start | bytes 3145736 | tf_op jit(solution)/shard_map/ppermute | solution.py:25
  108.3 24.1 %collective-permute-start.15 = (bf16[4,2,128,512]{3,2,1,0:T(8,128)(2,1)S(1)}, bf16[4,2,128,512]{3,2,1,0:T(8,128)(2,1)S(1)}, u32[]{:S(2)}, u32[]{:S(2)}) collective-permute-start(bf16[4,2,128,512]{3,2,1,0:T(8,128)(2,1)S(1)} %get-tuple-element.46), channel_id=1, source_target_pairs={{0,2},{1,5},{2,128},{3,7},{4,6},{5,9},{6,132},{7,11},{8,10},{9,13}... | collective-permute-start | bytes 3145736 | tf_op jit(solution)/shard_map/ppermute | solution.py:25
  108.6 23.9 %collective-permute-start.17 = (bf16[4,2,128,512]{3,2,1,0:T(8,128)(2,1)S(1)}, bf16[4,2,128,512]{3,2,1,0:T(8,128)(2,1)S(1)}, u32[]{:S(2)}, u32[]{:S(2)}) collective-permute-start(bf16[4,2,128,512]{3,2,1,0:T(8,128)(2,1)S(1)} %get-tuple-element.45), channel_id=1, source_target_pairs={{0,130},{1,13},{2,0},{3,15},{4,134},{5,1},{6,4},{7,3},{8,138},{9,5... | collective-permute-start | bytes 3145736 | tf_op jit(solution)/shard_map/ppermute | solution.py:25
  133.3 19.6 %collective-permute-start.18 = (bf16[2,128,512]{2,1,0:T(8,128)(2,1)S(1)}, bf16[2,128,512]{2,1,0:T(8,128)(2,1)S(1)}, u32[]{:S(2)}, u32[]{:S(2)}) collective-permute-start(bf16[2,128,512]{2,1,0:T(8,128)(2,1)S(1)} %get-tuple-element.51), channel_id=1, source_target_pairs={{0,8},{1,129},{2,10},{3,131},{4,12},{5,133},{6,14},{7,135},{8,0},{... | collective-permute-start | bytes 786440 | tf_op jit(solution)/shard_map/ppermute | solution.py:25
  136.1 16.8 %collective-permute-start.19 = (bf16[2,128,512]{2,1,0:T(8,128)(2,1)S(1)}, bf16[2,128,512]{2,1,0:T(8,128)(2,1)S(1)}, u32[]{:S(2)}, u32[]{:S(2)}) collective-permute-start(bf16[2,128,512]{2,1,0:T(8,128)(2,1)S(1)} %get-tuple-element.50), channel_id=1, source_target_pairs={{0,4},{1,3},{2,6},{3,129},{4,8},{5,7},{6,10},{7,133},{8,12},{9,11}... | collective-permute-start | bytes 786440 | tf_op jit(solution)/shard_map/ppermute | solution.py:25
  136.4 16.5 %collective-permute-start.20 = (bf16[2,128,512]{2,1,0:T(8,128)(2,1)S(1)}, bf16[2,128,512]{2,1,0:T(8,128)(2,1)S(1)}, u32[]{:S(2)}, u32[]{:S(2)}) collective-permute-start(bf16[2,128,512]{2,1,0:T(8,128)(2,1)S(1)} %get-tuple-element.49), channel_id=1, source_target_pairs={{0,12},{1,131},{2,14},{3,1},{4,0},{5,135},{6,2},{7,5},{8,4},{9,139... | collective-permute-start | bytes 786440 | tf_op jit(solution)/shard_map/ppermute | solution.py:25
  142.9 8.8 %collective-permute-start.21 = (bf16[2,4,128,128]{3,2,1,0:T(8,128)(2,1)S(1)}, bf16[2,4,128,128]{3,2,1,0:T(8,128)(2,1)S(1)}, u32[]{:S(2)}, u32[]{:S(2)}) collective-permute-start(bf16[2,4,128,128]{3,2,1,0:T(8,128)(2,1)S(1)} %pad_maximum_fusion.3), channel_id=1, source_target_pairs={{0,128},{1,129},{2,130},{3,131},{4,132},{5,133},{6,134},{7,135},{8... | collective-permute-start | bytes 786440 | tf_op jit(solution)/shard_map/ppermute | solution.py:25
  (3 other events, 3.0 us)
Sparse Core Ops, SparseCore 0:
  18.1 59.4 all-gather.2
  87.8 53.9 reduce-scatter.1

commit v4 on v3

--- a/solution.py
+++ b/solution.py
@@ -85,11 +85,14 @@
         store.wait()
 
 
-def first_kernel(rows, x_in, g_in, w_in, act_out, gh_out, grads_out, *scratch):
-    xs, gs, ws, grads, sem_x, sem_g, sem_in, sem_out = scratch
-
-    def store(j):
-        return pltpu.make_async_copy(grads.at[j], grads_out.at[:, :, :, j], sem_out.at[j])
+def first_kernel(rows_in, x_in, g_in, w_in, act_out, gh_out, grads_out, *scratch):
+    xs, gs, ws, grads, rows, sem_x, sem_g, sem_in, sem_out, sem_rows = scratch
+
+    def store(j, half):
+        slots = pl.ds(4 * half, 4)
+        return pltpu.make_async_copy(
+            grads.at[j, slots], grads_out.at[slots, :, :, j], sem_out.at[j, half]
+        )
 
     def load_w(j):
         return pltpu.make_async_copy(w_in.at[:, :, :, j], ws.at[j], sem_in.at[j])
@@ -103,13 +106,17 @@
                     pltpu.make_async_copy(
                         source.at[p // 4, :, lanes], target.at[j, s, half], sems.at[j]
                     ).start()
-        load_w(j).start()
 
     def pick(scratch, j, s):
         return jnp.concatenate([scratch[j, s, 0], scratch[j, s, 1]], axis=1)
 
     def two_columns(i, carry):
-        pl.when(i < 1)(lambda: [load(2), load(3)] and None)
+        @pl.when(i < 1)
+        def _():
+            for j in (2, 3):
+                load_w(j).start()
+                load(j)
+
         pair = (2 * i, 2 * i + 1)
         for j in pair:
             for target, sems in ((xs, sem_x), (gs, sem_g)):
@@ -139,14 +146,21 @@
                 down = dot(act_t, pick(gs, j, s)).astype(jnp.bfloat16)
                 grads[j, s, 0, 1] = down[:, :B]
                 grads[j, s, 1, 1] = down[:, B:]
-            store(j).start()
+                if s % 4 == 3:
+                    store(j, s // 4).start()
         return carry
 
-    load(0)
-    load(1)
+    fetch = pltpu.make_async_copy(rows_in, rows, sem_rows)
+    fetch.start()
+    for j in (0, 1):
+        load_w(j).start()
+    fetch.wait()
+    for j in (0, 1):
+        load(j)
     lax.fori_loop(0, 2, two_columns, 0)
     for j in range(4):
-        store(j).wait()
+        for half in range(2):
+            store(j, half).wait()
 
 
 def second_kernel(outs_at, rows, act_ref, gh_ref, *refs):
@@ -282,17 +296,19 @@
         first_kernel,
         out_shape=[jax.ShapeDtypeStruct((4, 2 * B, B), bf16)] * 2
         + [jax.ShapeDtypeStruct((8, 2, 2, 4, B, B), bf16)],
-        in_specs=[SMEM, HBM, HBM, HBM],
+        in_specs=[HBM, HBM, HBM, HBM],
         out_specs=[VMEM, VMEM, HBM],
         scratch_shapes=[
             pltpu.VMEM((4, 8, 2, 2 * B, B), bf16),
             pltpu.VMEM((4, 8, 2, 2 * B, B), bf16),
             pltpu.VMEM((4, 8, 2, 2, B, B), bf16),
             pltpu.VMEM((4, 8, 2, 2, B, B), bf16),
+            pltpu.SMEM((4, 16), jnp.int32),
             pltpu.SemaphoreType.DMA((4,)),
             pltpu.SemaphoreType.DMA((4,)),
             pltpu.SemaphoreType.DMA((4,)),
-            pltpu.SemaphoreType.DMA((4,)),
+            pltpu.SemaphoreType.DMA((4, 2)),
+            pltpu.SemaphoreType.DMA,
         ],
         compiler_params=pltpu.CompilerParams(vmem_limit_bytes=58 * MIB),
         cost_estimate=pl.CostEstimate(

time: 161 us -> 160 us (level)
  transfers between devices with their start and end apart: 24 -> 24, of which waited for: 17 -> 16; matrix products, arithmetic and copies ran while one was open for 6% -> 6% of each run, Pallas kernels for 9% -> 10%
where the time goes in v4:
time: 160 us
  waiting for transfers between devices  68.3 us (43%)
  starting transfers between devices  38.1 us (24%)
  Pallas kernels  24.6 us (15%)
  between operations  14.3 us (9%)
  local copies, waits for them, and re-layouts  7.96 us (5%)
  other arithmetic  6.69 us (4%)
    ppermute x22, waiting for transfers between devices, send(): lax.ppermute(value, AXES, [(source, place_of(*step(*where_is(source)))) f...  59.3 us
    ppermute x22, starting transfers between devices, send(): lax.ppermute(value, AXES, [(source, place_of(*step(*where_is(source)))) f...  38 us
    pallas_call x1, Pallas kernels, local(): pl.pallas_call(first_kernel, out_shape=[jax.ShapeDtypeStruct((4, 2 * B, B...  9.34 us
    pallas_call x1, Pallas kernels, local(): pl.pallas_call(place_kernel, out_shape=[gathered] * 2, in_specs=[SMEM] +...  8.19 us
    pallas_call x1, Pallas kernels, local(): pl.pallas_call(second_kernel, out_shape=jax.ShapeDtypeStruct((8, 4, 2, B,...  7.05 us
    all_gather x1, waiting for transfers between devices, local(): lax.all_gather(jnp.stack([piece_a, other_b]), 'dp', axis_index_groups=HAL...  6.05 us
    unnamed x24, local copies, waits for them, and re-layouts  3.99 us
  transfers between devices with their start and end apart: 24, of which 16 were waited for; matrix products, arithmetic and copies ran while one was open for 6% of the time, Pallas kernels for 10%

profile of v4, /device:TPU:1, one launch (start us, length us, event | category | flops | bytes accessed | tf_op | source)
XLA Modules:
  0.0 159.9 jit_solution(14829967203585262563)
XLA Ops:
  8.3 3.8 %collective-permute-start.10 = (bf16[2,4,128,128]{3,2,1,0:T(8,128)(2,1)S(1)}, bf16[2,4,128,128]{3,2,1,0:T(8,128)(2,1)S(1)}, u32[]{:S(2)}, u32[]{:S(2)}) collective-permute-start(bf16[2,4,128,128]{3,2,1,0:T(8,128)(2,1)S(1)} %fusion.5), channel_id=1, source_target_pairs={{0,128},{1,129},{2,130},{3,131},{4,132},{5,133},{6,134},{7,135},{8... | collective-permute-start | bytes 786440 | tf_op jit(solution)/shard_map/ppermute | solution.py:25
  13.1 4.0 %collective-permute-done.10 = bf16[2,4,128,128]{3,2,1,0:T(8,128)(2,1)S(1)} collective-permute-done((bf16[2,4,128,128]{3,2,1,0:T(8,128)(2,1)S(1)}, bf16[2,4,128,128]{3,2,1,0:T(8,128)(2,1)S(1)}, u32[]{:S(2)}, u32[]{:S(2)}) %collective-permute-start.10) | collective-permute-done | bytes 262176 | tf_op jit(solution)/shard_map/ppermute | solution.py:25
  18.1 2.2 %collective-permute-start = (bf16[2,128,512]{2,1,0:T(8,128)(2,1)S(1)}, bf16[2,128,512]{2,1,0:T(8,128)(2,1)S(1)}, u32[]{:S(2)}, u32[]{:S(2)}) collective-permute-start(bf16[2,128,512]{2,1,0:T(8,128)(2,1)S(1)} %get-tuple-element.60), channel_id=1, source_target_pairs={{0,4},{1,3},{2,6},{3,129},{4,8},{5,7},{6,10},{7,133},{8,12},{9,11}... | collective-permute-start | bytes 786440 | tf_op jit(solution)/shard_map/ppermute | solution.py:25
  20.2 1.5 collective-permute-start.1
  21.8 1.6 collective-permute-start.2
  23.3 2.4 %collective-permute-done = bf16[2,128,512]{2,1,0:T(8,128)(2,1)S(1)} collective-permute-done((bf16[2,128,512]{2,1,0:T(8,128)(2,1)S(1)}, bf16[2,128,512]{2,1,0:T(8,128)(2,1)S(1)}, u32[]{:S(2)}, u32[]{:S(2)}) %collective-permute-start) | collective-permute-done | bytes 262176 | tf_op jit(solution)/shard_map/ppermute | solution.py:25
  25.7 2.2 %collective-permute-done.1 = bf16[2,128,512]{2,1,0:T(8,128)(2,1)S(1)} collective-permute-done((bf16[2,128,512]{2,1,0:T(8,128)(2,1)S(1)}, bf16[2,128,512]{2,1,0:T(8,128)(2,1)S(1)}, u32[]{:S(2)}, u32[]{:S(2)}) %collective-permute-start.1) | collective-permute-done | bytes 262176 | tf_op jit(solution)/shard_map/ppermute | solution.py:25
  27.9 1.8 %collective-permute-done.2 = bf16[2,128,512]{2,1,0:T(8,128)(2,1)S(1)} collective-permute-done((bf16[2,128,512]{2,1,0:T(8,128)(2,1)S(1)}, bf16[2,128,512]{2,1,0:T(8,128)(2,1)S(1)}, u32[]{:S(2)}, u32[]{:S(2)}) %collective-permute-start.2) | collective-permute-done | bytes 262176 | tf_op jit(solution)/shard_map/ppermute | solution.py:25
  30.9 1.8 %collective-permute-start.4 = (bf16[4,2,128,512]{3,2,1,0:T(8,128)(2,1)S(1)}, bf16[4,2,128,512]{3,2,1,0:T(8,128)(2,1)S(1)}, u32[]{:S(2)}, u32[]{:S(2)}) collective-permute-start(bf16[4,2,128,512]{3,2,1,0:T(8,128)(2,1)S(1)} %pad_maximum_fusion.refs_0_), channel_id=1, source_target_pairs={{0,130},{1,13},{2,0},{3,15},{4,134},{5,1},{6,4},{7,3},{8,138},{9,5... | collective-permute-start | bytes 3145736 | tf_op jit(solution)/shard_map/ppermute | solution.py:25
  33.9 3.5 %collective-permute-start.6 = (bf16[4,2,128,512]{3,2,1,0:T(8,128)(2,1)S(1)}, bf16[4,2,128,512]{3,2,1,0:T(8,128)(2,1)}, u32[]{:S(2)}, u32[]{:S(2)}) collective-permute-start(bf16[4,2,128,512]{3,2,1,0:T(8,128)(2,1)S(1)} %pad_maximum_fusion.refs_0_), channel_id=1, source_target_pairs={{0,1},{1,0},{2,3},{3,2},{4,5},{5,4},{6,7},{7,6},{8,9},{9,8},{10,11... | collective-permute-start | bytes 3145736 | tf_op jit(solution)/shard_map/ppermute | solution.py:25
  37.3 7.9 %collective-permute-done.3.refs_1_ = bf16[4,2,128,512]{3,2,1,0:T(8,128)(2,1)S(1)} collective-permute-done((bf16[4,2,128,512]{3,2,1,0:T(8,128)(2,1)S(1)}, bf16[4,2,128,512]{3,2,1,0:T(8,128)(2,1)S(1)}, u32[]{:S(2)}, u32[]{:S(2)}) %collective-permute-start.3) | collective-permute-done | bytes 1048608 | tf_op jit(solution)/shard_map/ppermute | solution.py:25
  45.2 2.9 %collective-permute-start.7 = (bf16[4,2,128,512]{3,2,1,0:T(8,128)(2,1)S(1)}, bf16[4,2,128,512]{3,2,1,0:T(8,128)(2,1)}, u32[]{:S(2)}, u32[]{:S(2)}) collective-permute-start(bf16[4,2,128,512]{3,2,1,0:T(8,128)(2,1)S(1)} %collective-permute-done.3.refs_1_), channel_id=1, source_target_pairs={{0,1},{1,0},{2,3},{3,2},{4,5},{5,4},{6,7},{7,6},{8,9},{9,8},{10,11... | collective-permute-start | bytes 3145736 | tf_op jit(solution)/shard_map/ppermute | solution.py:25
  48.1 7.5 %collective-permute-done.4.refs_2_ = bf16[4,2,128,512]{3,2,1,0:T(8,128)(2,1)S(1)} collective-permute-done((bf16[4,2,128,512]{3,2,1,0:T(8,128)(2,1)S(1)}, bf16[4,2,128,512]{3,2,1,0:T(8,128)(2,1)S(1)}, u32[]{:S(2)}, u32[]{:S(2)}) %collective-permute-start.4) | collective-permute-done | bytes 1048608 | tf_op jit(solution)/shard_map/ppermute | solution.py:25
  55.6 1.8 %collective-permute-done.5.refs_3_ = bf16[4,2,128,512]{3,2,1,0:T(8,128)(2,1)} collective-permute-done((bf16[4,2,128,512]{3,2,1,0:T(8,128)(2,1)S(1)}, bf16[4,2,128,512]{3,2,1,0:T(8,128)(2,1)}, u32[]{:S(2)}, u32[]{:S(2)}) %collective-permute-start.5) | collective-permute-done | bytes 1048608 | tf_op jit(solution)/shard_map/ppermute | solution.py:25
  57.4 3.3 %collective-permute-start.9 = (bf16[4,2,128,512]{3,2,1,0:T(8,128)(2,1)}, bf16[4,2,128,512]{3,2,1,0:T(8,128)(2,1)}, u32[]{:S(2)}, u32[]{:S(2)}) collective-permute-start(bf16[4,2,128,512]{3,2,1,0:T(8,128)(2,1)} %collective-permute-done.5.refs_3_), channel_id=1, source_target_pairs={{0,1},{1,0},{2,3},{3,2},{4,5},{5,4},{6,7},{7,6},{8,9},{9,8},{10,11... | collective-permute-start | bytes 3145736 | tf_op jit(solution)/shard_map/ppermute | solution.py:25
  63.3 8.2 %place.1 = (bf16[16,256,512]{2,1,0:T(8,128)(2,1)}, bf16[16,256,512]{2,1,0:T(8,128)(2,1)}) custom-call(s32[32]{0:T(128)} %pad_add_fusion.spots, bf16[4,2,128,512]{3,2,1,0:T(8,128)(2,1)} %copy-done.4, bf16[4,2,128,512]{3,2,1,0:T(8,128)(2,1)} %copy-done.5, bf16[4,2,128,512]{3,2,1,0:T(8,128)(2,1)} %copy-done.6, ...), custom_call_target="tpu_custom_call" | custom-call | bytes 16777216 | tf_op jit(solution)/shard_map/place/pallas_call | solution.py:279
  71.5 6.1 %all-gather.3.cloned.1.call-done = bf16[16,2,4,128,128]{4,3,2,1,0:T(8,128)(2,1)} async-done(((bf16[2,2,4,128,128]{4,3,2,1,0:T(8,128)(2,1)}), bf16[16,2,4,128,128]{4,3,2,1,0:T(8,128)(2,1)}) %all-gather.3.cloned.1.call-update) | async-done | bytes 4194320 | tf_op jit(solution)/shard_map/all_gather | solution.py:274
  77.6 9.3 %first.1 = (bf16[4,256,128]{2,1,0:T(8,128)(2,1)}, bf16[4,256,128]{2,1,0:T(8,128)(2,1)}, bf16[8,2,2,4,128,128]{5,4,3,2,1,0:T(8,128)(2,1)}) custom-call(s32[4,16]{1,0:T(4,128)} %add_select_fusion.rows_in.rows, bf16[16,256,512]{2,1,0:T(8,128)(2,1)} %get-tuple-element.16.x_in, bf16[16,256,512]{2,1,0:T(8,128)(2,1)} %get-tuple-element.17.g_in, ...), custom_call_target="tpu_custom_call" | custom-call | flops 2000000000 | bytes 16777216 | tf_op jit(solution)/shard_map/first/pallas_call | solution.py:295
  88.0 2.2 %copy-done = bf16[16,2,4,128,128]{4,3,2,1,0:T(8,128)(2,1)S(1)} copy-done((bf16[16,2,4,128,128]{4,3,2,1,0:T(8,128)(2,1)S(1)}, bf16[16,2,4,128,128]{4,3,2,1,0:T(8,128)(2,1)}, u32[]{:S(2)}) %copy-start) | copy-done | bytes 4194328
  90.1 7.0 %second.1 = bf16[8,4,2,128,512]{4,3,2,1,0:T(8,128)(2,1)S(1)} custom-call(s32[128]{0:T(128)S(1)} %add.279.outs_at, s32[4,16]{1,0:T(4,128)S(1)} %copy-done.3, bf16[4,256,128]{2,1,0:T(8,128)(2,1)S(1)} %copy-done.1, bf16[4,256,128]{2,1,0:T(8,128)(2,1)S(1)} %copy-done.2, bf16[8,2,2,4,128,128]{5,4,3,2,1,0:T(8,128)(2,1)S(1)} %bitcast.87), custom_call_target="tpu_custom_call" | custom-call | flops 1000000000 | bytes 16777216 | tf_op jit(solution)/shard_map/second/pallas_call | solution.py:324
  99.1 1.7 %collective-permute-done.12 = bf16[4,2,128,512]{3,2,1,0:T(8,128)(2,1)S(1)} collective-permute-done((bf16[4,2,128,512]{3,2,1,0:T(8,128)(2,1)S(1)}, bf16[4,2,128,512]{3,2,1,0:T(8,128)(2,1)S(1)}, u32[]{:S(2)}, u32[]{:S(2)}) %collective-permute-start.12) | collective-permute-done | bytes 1048608 | tf_op jit(solution)/shard_map/ppermute | solution.py:25
  100.8 1.5 collective-permute-done.14
  102.3 1.5 collective-permute-done.16
  104.9 2.9 %collective-permute-start.13 = (bf16[4,2,128,512]{3,2,1,0:T(8,128)(2,1)S(1)}, bf16[4,2,128,512]{3,2,1,0:T(8,128)(2,1)S(1)}, u32[]{:S(2)}, u32[]{:S(2)}) collective-permute-start(bf16[4,2,128,512]{3,2,1,0:T(8,128)(2,1)S(1)} %get-tuple-element.44), channel_id=1, source_target_pairs={{0,128},{1,9},{2,130},{3,11},{4,132},{5,13},{6,134},{7,15},{8,136}... | collective-permute-start | bytes 3145736 | tf_op jit(solution)/shard_map/ppermute | solution.py:25
  108.0 2.6 %collective-permute-start.17 = (bf16[4,2,128,512]{3,2,1,0:T(8,128)(2,1)S(1)}, bf16[4,2,128,512]{3,2,1,0:T(8,128)(2,1)S(1)}, u32[]{:S(2)}, u32[]{:S(2)}) collective-permute-start(bf16[4,2,128,512]{3,2,1,0:T(8,128)(2,1)S(1)} %get-tuple-element.45), channel_id=1, source_target_pairs={{0,130},{1,13},{2,0},{3,15},{4,134},{5,1},{6,4},{7,3},{8,138},{9,5... | collective-permute-start | bytes 3145736 | tf_op jit(solution)/shard_map/ppermute | solution.py:25
  110.5 10.0 %collective-permute-done.13 = bf16[4,2,128,512]{3,2,1,0:T(8,128)(2,1)S(1)} collective-permute-done((bf16[4,2,128,512]{3,2,1,0:T(8,128)(2,1)S(1)}, bf16[4,2,128,512]{3,2,1,0:T(8,128)(2,1)S(1)}, u32[]{:S(2)}, u32[]{:S(2)}) %collective-permute-start.13) | collective-permute-done | bytes 1048608 | tf_op jit(solution)/shard_map/ppermute | solution.py:25
  120.5 11.3 %collective-permute-done.15 = bf16[4,2,128,512]{3,2,1,0:T(8,128)(2,1)S(1)} collective-permute-done((bf16[4,2,128,512]{3,2,1,0:T(8,128)(2,1)S(1)}, bf16[4,2,128,512]{3,2,1,0:T(8,128)(2,1)S(1)}, u32[]{:S(2)}, u32[]{:S(2)}) %collective-permute-start.15) | collective-permute-done | bytes 1048608 | tf_op jit(solution)/shard_map/ppermute | solution.py:25
  132.7 2.8 %collective-permute-start.18 = (bf16[2,128,512]{2,1,0:T(8,128)(2,1)S(1)}, bf16[2,128,512]{2,1,0:T(8,128)(2,1)S(1)}, u32[]{:S(2)}, u32[]{:S(2)}) collective-permute-start(bf16[2,128,512]{2,1,0:T(8,128)(2,1)S(1)} %get-tuple-element.51), channel_id=1, source_target_pairs={{0,8},{1,129},{2,10},{3,131},{4,12},{5,133},{6,14},{7,135},{8,0},{... | collective-permute-start | bytes 786440 | tf_op jit(solution)/shard_map/ppermute | solution.py:25
  135.9 2.3 %collective-permute-start.20 = (bf16[2,128,512]{2,1,0:T(8,128)(2,1)S(1)}, bf16[2,128,512]{2,1,0:T(8,128)(2,1)S(1)}, u32[]{:S(2)}, u32[]{:S(2)}) collective-permute-start(bf16[2,128,512]{2,1,0:T(8,128)(2,1)S(1)} %get-tuple-element.49), channel_id=1, source_target_pairs={{0,12},{1,131},{2,14},{3,1},{4,0},{5,135},{6,2},{7,5},{8,4},{9,139... | collective-permute-start | bytes 786440 | tf_op jit(solution)/shard_map/ppermute | solution.py:25
  138.2 2.9 %reduce-scatter.2.cloned.1.call-done = bf16[1,2,2,4,128,128]{5,4,3,2,1,0:T(8,128)(2,1)} async-done(((bf16[8,2,2,4,128,128]{5,4,3,2,1,0:T(8,128)(2,1)}), bf16[1,2,2,4,128,128]{5,4,3,2,1,0:T(8,128)(2,1)}) %reduce-scatter.2.cloned.1.call-update) | async-done | bytes 524304 | tf_op jit(solution)/shard_map/reduce_scatter | solution.py:320
  142.3 2.8 %collective-permute-start.21 = (bf16[2,4,128,128]{3,2,1,0:T(8,128)(2,1)S(1)}, bf16[2,4,128,128]{3,2,1,0:T(8,128)(2,1)S(1)}, u32[]{:S(2)}, u32[]{:S(2)}) collective-permute-start(bf16[2,4,128,128]{3,2,1,0:T(8,128)(2,1)S(1)} %pad_maximum_fusion.3), channel_id=1, source_target_pairs={{0,128},{1,129},{2,130},{3,131},{4,132},{5,133},{6,134},{7,135},{8... | collective-permute-start | bytes 786440 | tf_op jit(solution)/shard_map/ppermute | solution.py:25
  146.2 4.9 %collective-permute-done.21 = bf16[2,4,128,128]{3,2,1,0:T(8,128)(2,1)S(1)} collective-permute-done((bf16[2,4,128,128]{3,2,1,0:T(8,128)(2,1)S(1)}, bf16[2,4,128,128]{3,2,1,0:T(8,128)(2,1)S(1)}, u32[]{:S(2)}, u32[]{:S(2)}) %collective-permute-start.21) | collective-permute-done | bytes 262176 | tf_op jit(solution)/shard_map/ppermute | solution.py:25
  (79 shorter events, 17.7 us)
Async XLA Ops:
  7.2 10.8 %copy-start.8 = (bf16[128,512]{1,0:T(8,128)(2,1)S(1)}, bf16[128,512]{1,0:T(8,128)(2,1)}, u32[]{:S(2)}) copy-start(bf16[128,512]{1,0:T(8,128)(2,1)} %param.7) | copy-start | bytes 393220
  7.2 10.8 %copy-start.7 = (bf16[128,512]{1,0:T(8,128)(2,1)S(1)}, bf16[128,512]{1,0:T(8,128)(2,1)}, u32[]{:S(2)}) copy-start(bf16[128,512]{1,0:T(8,128)(2,1)} %param.11) | copy-start | bytes 393220
  7.2 70.4 %all-gather.3.cloned.1.call-start = ((), (), s32[]{:S(2)}) async-start(), calls=%async_computation.2 | async-start | bytes 4718592 | tf_op jit(solution)/shard_map/all_gather | solution.py:274
  8.3 8.8 %collective-permute-start.10 = (bf16[2,4,128,128]{3,2,1,0:T(8,128)(2,1)S(1)}, bf16[2,4,128,128]{3,2,1,0:T(8,128)(2,1)S(1)}, u32[]{:S(2)}, u32[]{:S(2)}) collective-permute-start(bf16[2,4,128,128]{3,2,1,0:T(8,128)(2,1)S(1)} %fusion.5), channel_id=1, source_target_pairs={{0,128},{1,129},{2,130},{3,131},{4,132},{5,133},{6,134},{7,135},{8... | collective-permute-start | bytes 786440 | tf_op jit(solution)/shard_map/ppermute | solution.py:25
  17.1 43.6 %copy-start.10 = (s32[4]{0:T(128)S(1)}, s32[4]{0:T(128)}, u32[]{:S(2)}) copy-start(s32[4]{0:T(128)} %constant.182.clone) | copy-start | bytes 52
  17.1 44.6 %copy-start.9 = (s32[8,16]{1,0:T(8,128)S(1)}, s32[8,16]{1,0:T(8,128)}, u32[]{:S(2)}) copy-start(s32[8,16]{1,0:T(8,128)} %param.8) | copy-start | bytes 1540
  18.0 123.1 %reduce-scatter.2.cloned.1.call-start = ((), (), s32[]{:S(2)}) async-start(), calls=%async_computation.1 | async-start | bytes 4718592 | tf_op jit(solution)/shard_map/reduce_scatter | solution.py:320
  18.1 7.7 %collective-permute-start = (bf16[2,128,512]{2,1,0:T(8,128)(2,1)S(1)}, bf16[2,128,512]{2,1,0:T(8,128)(2,1)S(1)}, u32[]{:S(2)}, u32[]{:S(2)}) collective-permute-start(bf16[2,128,512]{2,1,0:T(8,128)(2,1)S(1)} %get-tuple-element.60), channel_id=1, source_target_pairs={{0,4},{1,3},{2,6},{3,129},{4,8},{5,7},{6,10},{7,133},{8,12},{9,11}... | collective-permute-start | bytes 786440 | tf_op jit(solution)/shard_map/ppermute | solution.py:25
  20.2 7.7 %collective-permute-start.1 = (bf16[2,128,512]{2,1,0:T(8,128)(2,1)S(1)}, bf16[2,128,512]{2,1,0:T(8,128)(2,1)S(1)}, u32[]{:S(2)}, u32[]{:S(2)}) collective-permute-start(bf16[2,128,512]{2,1,0:T(8,128)(2,1)S(1)} %get-tuple-element.60), channel_id=1, source_target_pairs={{0,12},{1,131},{2,14},{3,1},{4,0},{5,135},{6,2},{7,5},{8,4},{9,139... | collective-permute-start | bytes 786440 | tf_op jit(solution)/shard_map/ppermute | solution.py:25
  21.8 8.0 %collective-permute-start.2 = (bf16[2,128,512]{2,1,0:T(8,128)(2,1)S(1)}, bf16[2,128,512]{2,1,0:T(8,128)(2,1)S(1)}, u32[]{:S(2)}, u32[]{:S(2)}) collective-permute-start(bf16[2,128,512]{2,1,0:T(8,128)(2,1)S(1)} %get-tuple-element.60), channel_id=1, source_target_pairs={{0,8},{1,129},{2,10},{3,131},{4,12},{5,133},{6,14},{7,135},{8,0},{... | collective-permute-start | bytes 786440 | tf_op jit(solution)/shard_map/ppermute | solution.py:25
  29.9 33.5 %copy-start.4 = (bf16[4,2,128,512]{3,2,1,0:T(8,128)(2,1)}, bf16[4,2,128,512]{3,2,1,0:T(8,128)(2,1)S(1)}, u32[]{:S(2)}) copy-start(bf16[4,2,128,512]{3,2,1,0:T(8,128)(2,1)S(1)} %pad_maximum_fusion.refs_0_) | copy-start | bytes 3145732
  29.9 15.3 %collective-permute-start.3 = (bf16[4,2,128,512]{3,2,1,0:T(8,128)(2,1)S(1)}, bf16[4,2,128,512]{3,2,1,0:T(8,128)(2,1)S(1)}, u32[]{:S(2)}, u32[]{:S(2)}) collective-permute-start(bf16[4,2,128,512]{3,2,1,0:T(8,128)(2,1)S(1)} %pad_maximum_fusion.refs_0_), channel_id=1, source_target_pairs={{0,2},{1,5},{2,128},{3,7},{4,6},{5,9},{6,132},{7,11},{8,10},{9,13}... | collective-permute-start | bytes 3145736 | tf_op jit(solution)/shard_map/ppermute | solution.py:25
  30.9 24.7 %collective-permute-start.4 = (bf16[4,2,128,512]{3,2,1,0:T(8,128)(2,1)S(1)}, bf16[4,2,128,512]{3,2,1,0:T(8,128)(2,1)S(1)}, u32[]{:S(2)}, u32[]{:S(2)}) collective-permute-start(bf16[4,2,128,512]{3,2,1,0:T(8,128)(2,1)S(1)} %pad_maximum_fusion.refs_0_), channel_id=1, source_target_pairs={{0,130},{1,13},{2,0},{3,15},{4,134},{5,1},{6,4},{7,3},{8,138},{9,5... | collective-permute-start | bytes 3145736 | tf_op jit(solution)/shard_map/ppermute | solution.py:25
  32.6 24.8 %collective-permute-start.5 = (bf16[4,2,128,512]{3,2,1,0:T(8,128)(2,1)S(1)}, bf16[4,2,128,512]{3,2,1,0:T(8,128)(2,1)}, u32[]{:S(2)}, u32[]{:S(2)}) collective-permute-start(bf16[4,2,128,512]{3,2,1,0:T(8,128)(2,1)S(1)} %pad_maximum_fusion.refs_0_), channel_id=1, source_target_pairs={{0,128},{1,9},{2,130},{3,11},{4,132},{5,13},{6,134},{7,15},{8,136}... | collective-permute-start | bytes 3145736 | tf_op jit(solution)/shard_map/ppermute | solution.py:25
  33.9 28.6 %collective-permute-start.6 = (bf16[4,2,128,512]{3,2,1,0:T(8,128)(2,1)S(1)}, bf16[4,2,128,512]{3,2,1,0:T(8,128)(2,1)}, u32[]{:S(2)}, u32[]{:S(2)}) collective-permute-start(bf16[4,2,128,512]{3,2,1,0:T(8,128)(2,1)S(1)} %pad_maximum_fusion.refs_0_), channel_id=1, source_target_pairs={{0,1},{1,0},{2,3},{3,2},{4,5},{5,4},{6,7},{7,6},{8,9},{9,8},{10,11... | collective-permute-start | bytes 3145736 | tf_op jit(solution)/shard_map/ppermute | solution.py:25
  45.2 18.1 %copy-start.5 = (bf16[4,2,128,512]{3,2,1,0:T(8,128)(2,1)}, bf16[4,2,128,512]{3,2,1,0:T(8,128)(2,1)S(1)}, u32[]{:S(2)}) copy-start(bf16[4,2,128,512]{3,2,1,0:T(8,128)(2,1)S(1)} %collective-permute-done.3.refs_1_) | copy-start | bytes 3145732
  45.2 17.2 %collective-permute-start.7 = (bf16[4,2,128,512]{3,2,1,0:T(8,128)(2,1)S(1)}, bf16[4,2,128,512]{3,2,1,0:T(8,128)(2,1)}, u32[]{:S(2)}, u32[]{:S(2)}) collective-permute-start(bf16[4,2,128,512]{3,2,1,0:T(8,128)(2,1)S(1)} %collective-permute-done.3.refs_1_), channel_id=1, source_target_pairs={{0,1},{1,0},{2,3},{3,2},{4,5},{5,4},{6,7},{7,6},{8,9},{9,8},{10,11... | collective-permute-start | bytes 3145736 | tf_op jit(solution)/shard_map/ppermute | solution.py:25
  55.6 7.7 %copy-start.6 = (bf16[4,2,128,512]{3,2,1,0:T(8,128)(2,1)}, bf16[4,2,128,512]{3,2,1,0:T(8,128)(2,1)S(1)}, u32[]{:S(2)}) copy-start(bf16[4,2,128,512]{3,2,1,0:T(8,128)(2,1)S(1)} %collective-permute-done.4.refs_2_) | copy-start | bytes 3145732
  55.6 6.9 %collective-permute-start.8 = (bf16[4,2,128,512]{3,2,1,0:T(8,128)(2,1)S(1)}, bf16[4,2,128,512]{3,2,1,0:T(8,128)(2,1)}, u32[]{:S(2)}, u32[]{:S(2)}) collective-permute-start(bf16[4,2,128,512]{3,2,1,0:T(8,128)(2,1)S(1)} %collective-permute-done.4.refs_2_), channel_id=1, source_target_pairs={{0,1},{1,0},{2,3},{3,2},{4,5},{5,4},{6,7},{7,6},{8,9},{9,8},{10,11... | collective-permute-start | bytes 3145736 | tf_op jit(solution)/shard_map/ppermute | solution.py:25
  57.4 5.9 %collective-permute-start.9 = (bf16[4,2,128,512]{3,2,1,0:T(8,128)(2,1)}, bf16[4,2,128,512]{3,2,1,0:T(8,128)(2,1)}, u32[]{:S(2)}, u32[]{:S(2)}) collective-permute-start(bf16[4,2,128,512]{3,2,1,0:T(8,128)(2,1)} %collective-permute-done.5.refs_3_), channel_id=1, source_target_pairs={{0,1},{1,0},{2,3},{3,2},{4,5},{5,4},{6,7},{7,6},{8,9},{9,8},{10,11... | collective-permute-start | bytes 3145736 | tf_op jit(solution)/shard_map/ppermute | solution.py:25
  88.0 2.2 %copy-start = (bf16[16,2,4,128,128]{4,3,2,1,0:T(8,128)(2,1)S(1)}, bf16[16,2,4,128,128]{4,3,2,1,0:T(8,128)(2,1)}, u32[]{:S(2)}) copy-start(bf16[16,2,4,128,128]{4,3,2,1,0:T(8,128)(2,1)} %all-gather.3.cloned.1.call-done) | copy-start | bytes 12582916
  97.6 3.1 %collective-permute-start.12 = (bf16[4,2,128,512]{3,2,1,0:T(8,128)(2,1)S(1)}, bf16[4,2,128,512]{3,2,1,0:T(8,128)(2,1)S(1)}, u32[]{:S(2)}, u32[]{:S(2)}) collective-permute-start(bf16[4,2,128,512]{3,2,1,0:T(8,128)(2,1)S(1)} %get-tuple-element.43), channel_id=1, source_target_pairs={{0,1},{1,0},{2,3},{3,2},{4,5},{5,4},{6,7},{7,6},{8,9},{9,8},{10,11... | collective-permute-start | bytes 3145736 | tf_op jit(solution)/shard_map/ppermute | solution.py:25
  98.5 3.8 %collective-permute-start.14 = (bf16[4,2,128,512]{3,2,1,0:T(8,128)(2,1)S(1)}, bf16[4,2,128,512]{3,2,1,0:T(8,128)(2,1)S(1)}, u32[]{:S(2)}, u32[]{:S(2)}) collective-permute-start(bf16[4,2,128,512]{3,2,1,0:T(8,128)(2,1)S(1)} %get-tuple-element.42), channel_id=1, source_target_pairs={{0,1},{1,0},{2,3},{3,2},{4,5},{5,4},{6,7},{7,6},{8,9},{9,8},{10,11... | collective-permute-start | bytes 3145736 | tf_op jit(solution)/shard_map/ppermute | solution.py:25
  98.6 5.2 %collective-permute-start.16 = (bf16[4,2,128,512]{3,2,1,0:T(8,128)(2,1)S(1)}, bf16[4,2,128,512]{3,2,1,0:T(8,128)(2,1)S(1)}, u32[]{:S(2)}, u32[]{:S(2)}) collective-permute-start(bf16[4,2,128,512]{3,2,1,0:T(8,128)(2,1)S(1)} %get-tuple-element.41), channel_id=1, source_target_pairs={{0,1},{1,0},{2,3},{3,2},{4,5},{5,4},{6,7},{7,6},{8,9},{9,8},{10,11... | collective-permute-start | bytes 3145736 | tf_op jit(solution)/shard_map/ppermute | solution.py:25
  99.0 11.5 %collective-permute-start.11 = (bf16[4,2,128,512]{3,2,1,0:T(8,128)(2,1)S(1)}, bf16[4,2,128,512]{3,2,1,0:T(8,128)(2,1)S(1)}, u32[]{:S(2)}, u32[]{:S(2)}) collective-permute-start(bf16[4,2,128,512]{3,2,1,0:T(8,128)(2,1)S(1)} %get-tuple-element.40), channel_id=1, source_target_pairs={{0,1},{1,0},{2,3},{3,2},{4,5},{5,4},{6,7},{7,6},{8,9},{9,8},{10,11... | collective-permute-start | bytes 3145736 | tf_op jit(solution)/shard_map/ppermute | solution.py:25
  104.9 15.6 %collective-permute-start.13 = (bf16[4,2,128,512]{3,2,1,0:T(8,128)(2,1)S(1)}, bf16[4,2,128,512]{3,2,1,0:T(8,128)(2,1)S(1)}, u32[]{:S(2)}, u32[]{:S(2)}) collective-permute-start(bf16[4,2,128,512]{3,2,1,0:T(8,128)(2,1)S(1)} %get-tuple-element.44), channel_id=1, source_target_pairs={{0,128},{1,9},{2,130},{3,11},{4,132},{5,13},{6,134},{7,15},{8,136}... | collective-permute-start | bytes 3145736 | tf_op jit(solution)/shard_map/ppermute | solution.py:25
  107.9 23.9 %collective-permute-start.15 = (bf16[4,2,128,512]{3,2,1,0:T(8,128)(2,1)S(1)}, bf16[4,2,128,512]{3,2,1,0:T(8,128)(2,1)S(1)}, u32[]{:S(2)}, u32[]{:S(2)}) collective-permute-start(bf16[4,2,128,512]{3,2,1,0:T(8,128)(2,1)S(1)} %get-tuple-element.46), channel_id=1, source_target_pairs={{0,2},{1,5},{2,128},{3,7},{4,6},{5,9},{6,132},{7,11},{8,10},{9,13}... | collective-permute-start | bytes 3145736 | tf_op jit(solution)/shard_map/ppermute | solution.py:25
  108.0 23.9 %collective-permute-start.17 = (bf16[4,2,128,512]{3,2,1,0:T(8,128)(2,1)S(1)}, bf16[4,2,128,512]{3,2,1,0:T(8,128)(2,1)S(1)}, u32[]{:S(2)}, u32[]{:S(2)}) collective-permute-start(bf16[4,2,128,512]{3,2,1,0:T(8,128)(2,1)S(1)} %get-tuple-element.45), channel_id=1, source_target_pairs={{0,130},{1,13},{2,0},{3,15},{4,134},{5,1},{6,4},{7,3},{8,138},{9,5... | collective-permute-start | bytes 3145736 | tf_op jit(solution)/shard_map/ppermute | solution.py:25
  132.7 19.5 %collective-permute-start.18 = (bf16[2,128,512]{2,1,0:T(8,128)(2,1)S(1)}, bf16[2,128,512]{2,1,0:T(8,128)(2,1)S(1)}, u32[]{:S(2)}, u32[]{:S(2)}) collective-permute-start(bf16[2,128,512]{2,1,0:T(8,128)(2,1)S(1)} %get-tuple-element.51), channel_id=1, source_target_pairs={{0,8},{1,129},{2,10},{3,131},{4,12},{5,133},{6,14},{7,135},{8,0},{... | collective-permute-start | bytes 786440 | tf_op jit(solution)/shard_map/ppermute | solution.py:25
  135.5 16.7 %collective-permute-start.19 = (bf16[2,128,512]{2,1,0:T(8,128)(2,1)S(1)}, bf16[2,128,512]{2,1,0:T(8,128)(2,1)S(1)}, u32[]{:S(2)}, u32[]{:S(2)}) collective-permute-start(bf16[2,128,512]{2,1,0:T(8,128)(2,1)S(1)} %get-tuple-element.50), channel_id=1, source_target_pairs={{0,4},{1,3},{2,6},{3,129},{4,8},{5,7},{6,10},{7,133},{8,12},{9,11}... | collective-permute-start | bytes 786440 | tf_op jit(solution)/shard_map/ppermute | solution.py:25
  135.9 16.3 %collective-permute-start.20 = (bf16[2,128,512]{2,1,0:T(8,128)(2,1)S(1)}, bf16[2,128,512]{2,1,0:T(8,128)(2,1)S(1)}, u32[]{:S(2)}, u32[]{:S(2)}) collective-permute-start(bf16[2,128,512]{2,1,0:T(8,128)(2,1)S(1)} %get-tuple-element.49), channel_id=1, source_target_pairs={{0,12},{1,131},{2,14},{3,1},{4,0},{5,135},{6,2},{7,5},{8,4},{9,139... | collective-permute-start | bytes 786440 | tf_op jit(solution)/shard_map/ppermute | solution.py:25
  142.3 8.8 %collective-permute-start.21 = (bf16[2,4,128,128]{3,2,1,0:T(8,128)(2,1)S(1)}, bf16[2,4,128,128]{3,2,1,0:T(8,128)(2,1)S(1)}, u32[]{:S(2)}, u32[]{:S(2)}) collective-permute-start(bf16[2,4,128,128]{3,2,1,0:T(8,128)(2,1)S(1)} %pad_maximum_fusion.3), channel_id=1, source_target_pairs={{0,128},{1,129},{2,130},{3,131},{4,132},{5,133},{6,134},{7,135},{8... | collective-permute-start | bytes 786440 | tf_op jit(solution)/shard_map/ppermute | solution.py:25
  (3 other events, 3.0 us)
Sparse Core Ops, SparseCore 0:
  18.1 59.4 all-gather.2
  87.1 53.9 reduce-scatter.1

commit v5 on v4

--- a/solution.py
+++ b/solution.py
@@ -164,7 +164,8 @@
 
 
 def second_kernel(outs_at, rows, act_ref, gh_ref, *refs):
-    w_in, parts, ws, out_acc, in_acc, sem_w = refs
+    w_in, parts = refs[0], refs[1:9]
+    ws, out_acc, in_acc, stage, sem_w, sem_out = refs[9:]
 
     def load(j):
         return pltpu.make_async_copy(w_in.at[:, :, :, j], ws.at[j], sem_w.at[j])
@@ -179,35 +180,43 @@
 
     lax.fori_loop(0, 64, clear, 0)
 
-    def column(j, carry):
-        load(j).wait()
-        act = act_ref[j]
-        gh = gh_ref[j]
+    def two_columns(i, carry):
+        pair = (2 * i, 2 * i + 1)
+        for j in pair:
+            load(j).wait()
         for s in range(8):
-            p = rows[j, s]
-            q = rows[j, 8 + s]
-            down = jnp.concatenate([ws[j, s, 0, 1], ws[j, s, 1, 1]], axis=1)
-            term = dot(act, down)
-            out_acc[p] += term[:, :B]
-            out_acc[q] += term[:, B:]
-            up = jnp.concatenate([ws[j, s, 0, 0], ws[j, s, 1, 0]], axis=0)
-            term = dot(gh, up, NT)
-            in_acc[p] += term[:, :B]
-            in_acc[q] += term[:, B:]
+            terms = []
+            for j in pair:
+                down = jnp.concatenate([ws[j, s, 0, 1], ws[j, s, 1, 1]], axis=1)
+                up = jnp.concatenate([ws[j, s, 0, 0], ws[j, s, 1, 0]], axis=0)
+                terms.append((dot(act_ref[j], down), dot(gh_ref[j], up, NT)))
+            for j, (out_term, in_term) in zip(pair, terms):
+                for half in range(2):
+                    p = rows[j, half * 8 + s]
+                    out_acc[p] += out_term[:, half * B : (half + 1) * B]
+                    in_acc[p] += in_term[:, half * B : (half + 1) * B]
         return carry
 
-    lax.fori_loop(0, 4, column, 0)
-
-    def finish(p, carry):
-        lanes = pl.ds(pl.multiple_of((p % 4) * B, B), B)
+    lax.fori_loop(0, 2, two_columns, 0)
+
+    def finish(m, carry):
         for half in range(2):
             rows_of = pl.ds(half * B, B)
-            at = outs_at[p * 2 + half]
-            parts[at // 4, at % 4, 0, :, lanes] = out_acc[p, rows_of].astype(jnp.bfloat16)
-            parts[at // 4, at % 4, 1, :, lanes] = in_acc[p, rows_of].astype(jnp.bfloat16)
+            for n in range(4):
+                lanes = pl.ds(n * B, B)
+                stage[m, half, 0, :, lanes] = out_acc[m * 4 + n, rows_of].astype(jnp.bfloat16)
+                stage[m, half, 1, :, lanes] = in_acc[m * 4 + n, rows_of].astype(jnp.bfloat16)
+            at = outs_at[m * 8 + half]
+            for n, part in enumerate(parts):
+
+                @pl.when(at // 4 == n)
+                def _(part=part):
+                    pltpu.make_async_copy(stage.at[m, half], part.at[at % 4], sem_out).start()
+
         return carry
 
-    lax.fori_loop(0, 64, finish, 0)
+    lax.fori_loop(0, 16, finish, 0)
+    pltpu.make_async_copy(stage, stage, sem_out).wait()
 
 
 SMEM = pl.BlockSpec(memory_space=pltpu.SMEM)
@@ -323,16 +332,18 @@
 
     parts = pl.pallas_call(
         second_kernel,
-        out_shape=jax.ShapeDtypeStruct((8, 4, 2, B, 4 * B), bf16),
+        out_shape=[jax.ShapeDtypeStruct((4, 2, B, 4 * B), bf16)] * 8,
         in_specs=[SMEM, SMEM, VMEM, VMEM, HBM],
-        out_specs=VMEM,
+        out_specs=[HBM] * 8,
         scratch_shapes=[
             pltpu.VMEM((4, 8, 2, 2, B, B), bf16),
             pltpu.VMEM((64, 2 * B, B), f32),
             pltpu.VMEM((64, 2 * B, B), f32),
+            pltpu.VMEM((16, 2, 2, B, 4 * B), bf16),
             pltpu.SemaphoreType.DMA((4,)),
+            pltpu.SemaphoreType.DMA,
         ],
-        compiler_params=pltpu.CompilerParams(vmem_limit_bytes=24 * MIB),
+        compiler_params=pltpu.CompilerParams(vmem_limit_bytes=58 * MIB),
         cost_estimate=pl.CostEstimate(
             flops=1_000_000_000, bytes_accessed=16 * MIB, transcendentals=0
         ),
@@ -340,14 +351,18 @@
     )(outs_at, rows, act, gh, weights)
 
     last = scatter_plane(parts)
-    other = send(jnp.stack([jnp.swapaxes(summed[1, 0], 1, 2), summed[1, 1]]), other_half)
-    own = lax.optimization_barrier(summed[0])
-    own = jnp.stack([jnp.swapaxes(own[0], 1, 2), own[1]])
-    grads = jnp.where(
-        yh == 0, jnp.concatenate([own, other], axis=1), jnp.concatenate([other, own], axis=1)
-    ).astype(f32)
-    grad_up, grad_down = grads[0][:, None], grads[1][:, None]
-    last, grad_up = lax.optimization_barrier((last, grad_up))
+    def assemble(own, other):
+        halves = jnp.where(
+            yh == 0, jnp.concatenate([own, other]), jnp.concatenate([other, own])
+        )
+        return halves.astype(f32)[:, None]
+
+    other_down = send(summed[1, 1], other_half)
+    other_up = send(jnp.swapaxes(summed[1, 0], 1, 2), other_half)
+    own_up = jnp.swapaxes(lax.optimization_barrier(summed[0, 0]), 1, 2)
+    last, other_down = lax.optimization_barrier((last, other_down))
+    grad_down = assemble(summed[0, 1], other_down)
+    grad_up = assemble(own_up, other_up)
     result = total(last).astype(bf16)
     mixed, grad_tokens = result[0], result[1]
     return mixed, grad_tokens, grad_up, grad_down

time: 160 us -> 160 us (level)
  local copies, waits for them, and re-layouts: 7.96 us -> 3.38 us
  other arithmetic: 6.69 us -> 9.25 us
    unnamed x24 -> x22, local copies, waits for them, and re-layouts: 3.99 us -> 0.3 us
    ppermute x22 -> x23, waiting for transfers between devices: 59.3 us -> 56.8 us  [send(): lax.ppermute(value, AXES, [(source, place_of(*step(*where_is(source)))) f...]
    unnamed x0 -> x2, other arithmetic: none -> 1.66 us
    ppermute x22 -> x23, starting transfers between devices: 38 us -> 39.3 us  [send(): lax.ppermute(value, AXES, [(source, place_of(*step(*where_is(source)))) f...]
  transfers between devices with their start and end apart: 24 -> 25, of which waited for: 16 -> 15; matrix products, arithmetic and copies ran while one was open for 6% -> 6% of each run, Pallas kernels for 10% -> 10%
where the time goes in v5:
time: 160 us; the launch traced here: 159 us
  waiting for transfers between devices  66.8 us (42%)
  starting transfers between devices  39.3 us (25%)
  Pallas kernels  25.9 us (16%)
  between operations  14.3 us (9%)
  other arithmetic  9.25 us (6%)
  local copies, waits for them, and re-layouts  3.38 us (2%)
    ppermute x23, waiting for transfers between devices, send(): lax.ppermute(value, AXES, [(source, place_of(*step(*where_is(source)))) f...  56.8 us
    ppermute x23, starting transfers between devices, send(): lax.ppermute(value, AXES, [(source, place_of(*step(*where_is(source)))) f...  39.3 us
    pallas_call x1, Pallas kernels, local(): pl.pallas_call(first_kernel, out_shape=[jax.ShapeDtypeStruct((4, 2 * B, B...  9.26 us
    pallas_call x1, Pallas kernels, local(): pl.pallas_call(second_kernel, out_shape=[jax.ShapeDtypeStruct((4, 2, B, 4...  8.52 us
    pallas_call x1, Pallas kernels, local(): pl.pallas_call(place_kernel, out_shape=[gathered] * 2, in_specs=[SMEM] +...  8.12 us
    all_gather x1, waiting for transfers between devices, local(): lax.all_gather(jnp.stack([piece_a, other_b]), 'dp', axis_index_groups=HAL...  5.74 us
    reduce_scatter x1, waiting for transfers between devices, local(): lax.psum_scatter(grads, 'dp', scatter_dimension=0, axis_index_groups=HALV...  4.15 us
  transfers between devices with their start and end apart: 25, of which 15 were waited for; matrix products, arithmetic and copies ran while one was open for 6% of the time, Pallas kernels for 10%

profile of v5, /device:TPU:1, one launch (start us, length us, event | category | flops | bytes accessed | tf_op | source)
XLA Modules:
  0.0 159.0 jit_solution(14354192278004417642)
XLA Ops:
  7.3 1.0 fusion
  8.3 3.8 %collective-permute-start.10 = (bf16[2,4,128,128]{3,2,1,0:T(8,128)(2,1)S(1)}, bf16[2,4,128,128]{3,2,1,0:T(8,128)(2,1)S(1)}, u32[]{:S(2)}, u32[]{:S(2)}) collective-permute-start(bf16[2,4,128,128]{3,2,1,0:T(8,128)(2,1)S(1)} %fusion), channel_id=1, source_target_pairs={{0,128},{1,129},{2,130},{3,131},{4,132},{5,133},{6,134},{7,135},{8... | collective-permute-start | bytes 786440 | tf_op jit(solution)/shard_map/ppermute | solution.py:25
  13.1 4.0 %collective-permute-done.10 = bf16[2,4,128,128]{3,2,1,0:T(8,128)(2,1)S(1)} collective-permute-done((bf16[2,4,128,128]{3,2,1,0:T(8,128)(2,1)S(1)}, bf16[2,4,128,128]{3,2,1,0:T(8,128)(2,1)S(1)}, u32[]{:S(2)}, u32[]{:S(2)}) %collective-permute-start.10) | collective-permute-done | bytes 262176 | tf_op jit(solution)/shard_map/ppermute | solution.py:25
  18.1 3.8 %collective-permute-start.2 = (bf16[2,128,512]{2,1,0:T(8,128)(2,1)S(1)}, bf16[2,128,512]{2,1,0:T(8,128)(2,1)S(1)}, u32[]{:S(2)}, u32[]{:S(2)}) collective-permute-start(bf16[2,128,512]{2,1,0:T(8,128)(2,1)S(1)} %get-tuple-element.67), channel_id=1, source_target_pairs={{0,8},{1,129},{2,10},{3,131},{4,12},{5,133},{6,14},{7,135},{8,0},{... | collective-permute-start | bytes 786440 | tf_op jit(solution)/shard_map/ppermute | solution.py:25
  23.3 2.6 %collective-permute-done.2 = bf16[2,128,512]{2,1,0:T(8,128)(2,1)S(1)} collective-permute-done((bf16[2,128,512]{2,1,0:T(8,128)(2,1)S(1)}, bf16[2,128,512]{2,1,0:T(8,128)(2,1)S(1)}, u32[]{:S(2)}, u32[]{:S(2)}) %collective-permute-start.2) | collective-permute-done | bytes 262176 | tf_op jit(solution)/shard_map/ppermute | solution.py:25
  25.9 3.2 %collective-permute-done.1 = bf16[2,128,512]{2,1,0:T(8,128)(2,1)S(1)} collective-permute-done((bf16[2,128,512]{2,1,0:T(8,128)(2,1)S(1)}, bf16[2,128,512]{2,1,0:T(8,128)(2,1)S(1)}, u32[]{:S(2)}, u32[]{:S(2)}) %collective-permute-start.1) | collective-permute-done | bytes 262176 | tf_op jit(solution)/shard_map/ppermute | solution.py:25
  29.5 1.1 collective-permute-start.3
  30.6 1.7 %collective-permute-start.4 = (bf16[4,2,128,512]{3,2,1,0:T(8,128)(2,1)S(1)}, bf16[4,2,128,512]{3,2,1,0:T(8,128)(2,1)S(1)}, u32[]{:S(2)}, u32[]{:S(2)}) collective-permute-start(bf16[4,2,128,512]{3,2,1,0:T(8,128)(2,1)S(1)} %pad_maximum_fusion.refs_0_), channel_id=1, source_target_pairs={{0,130},{1,13},{2,0},{3,15},{4,134},{5,1},{6,4},{7,3},{8,138},{9,5... | collective-permute-start | bytes 3145736 | tf_op jit(solution)/shard_map/ppermute | solution.py:25
  32.3 1.3 collective-permute-start.5
  33.6 4.1 %collective-permute-start.6 = (bf16[4,2,128,512]{3,2,1,0:T(8,128)(2,1)S(1)}, bf16[4,2,128,512]{3,2,1,0:T(8,128)(2,1)}, u32[]{:S(2)}, u32[]{:S(2)}) collective-permute-start(bf16[4,2,128,512]{3,2,1,0:T(8,128)(2,1)S(1)} %pad_maximum_fusion.refs_0_), channel_id=1, source_target_pairs={{0,1},{1,0},{2,3},{3,2},{4,5},{5,4},{6,7},{7,6},{8,9},{9,8},{10,11... | collective-permute-start | bytes 3145736 | tf_op jit(solution)/shard_map/ppermute | solution.py:25
  37.7 7.2 %collective-permute-done.3.refs_1_ = bf16[4,2,128,512]{3,2,1,0:T(8,128)(2,1)S(1)} collective-permute-done((bf16[4,2,128,512]{3,2,1,0:T(8,128)(2,1)S(1)}, bf16[4,2,128,512]{3,2,1,0:T(8,128)(2,1)S(1)}, u32[]{:S(2)}, u32[]{:S(2)}) %collective-permute-start.3) | collective-permute-done | bytes 1048608 | tf_op jit(solution)/shard_map/ppermute | solution.py:25
  44.9 3.6 %collective-permute-start.7 = (bf16[4,2,128,512]{3,2,1,0:T(8,128)(2,1)S(1)}, bf16[4,2,128,512]{3,2,1,0:T(8,128)(2,1)}, u32[]{:S(2)}, u32[]{:S(2)}) collective-permute-start(bf16[4,2,128,512]{3,2,1,0:T(8,128)(2,1)S(1)} %collective-permute-done.3.refs_1_), channel_id=1, source_target_pairs={{0,1},{1,0},{2,3},{3,2},{4,5},{5,4},{6,7},{7,6},{8,9},{9,8},{10,11... | collective-permute-start | bytes 3145736 | tf_op jit(solution)/shard_map/ppermute | solution.py:25
  48.5 6.8 %collective-permute-done.4.refs_2_ = bf16[4,2,128,512]{3,2,1,0:T(8,128)(2,1)S(1)} collective-permute-done((bf16[4,2,128,512]{3,2,1,0:T(8,128)(2,1)S(1)}, bf16[4,2,128,512]{3,2,1,0:T(8,128)(2,1)S(1)}, u32[]{:S(2)}, u32[]{:S(2)}) %collective-permute-start.4) | collective-permute-done | bytes 1048608 | tf_op jit(solution)/shard_map/ppermute | solution.py:25
  55.3 1.8 %collective-permute-done.5.refs_3_ = bf16[4,2,128,512]{3,2,1,0:T(8,128)(2,1)} collective-permute-done((bf16[4,2,128,512]{3,2,1,0:T(8,128)(2,1)S(1)}, bf16[4,2,128,512]{3,2,1,0:T(8,128)(2,1)}, u32[]{:S(2)}, u32[]{:S(2)}) %collective-permute-start.5) | collective-permute-done | bytes 1048608 | tf_op jit(solution)/shard_map/ppermute | solution.py:25
  57.1 4.0 %collective-permute-start.9 = (bf16[4,2,128,512]{3,2,1,0:T(8,128)(2,1)}, bf16[4,2,128,512]{3,2,1,0:T(8,128)(2,1)}, u32[]{:S(2)}, u32[]{:S(2)}) collective-permute-start(bf16[4,2,128,512]{3,2,1,0:T(8,128)(2,1)} %collective-permute-done.5.refs_3_), channel_id=1, source_target_pairs={{0,1},{1,0},{2,3},{3,2},{4,5},{5,4},{6,7},{7,6},{8,9},{9,8},{10,11... | collective-permute-start | bytes 3145736 | tf_op jit(solution)/shard_map/ppermute | solution.py:25
  63.7 8.1 %place.1 = (bf16[16,256,512]{2,1,0:T(8,128)(2,1)}, bf16[16,256,512]{2,1,0:T(8,128)(2,1)}) custom-call(s32[32]{0:T(128)} %pad_add_fusion.spots, bf16[4,2,128,512]{3,2,1,0:T(8,128)(2,1)} %copy-done, bf16[4,2,128,512]{3,2,1,0:T(8,128)(2,1)} %copy-done.1, bf16[4,2,128,512]{3,2,1,0:T(8,128)(2,1)} %copy-done.2, ...), custom_call_target="tpu_custom_call" | custom-call | bytes 16777216 | tf_op jit(solution)/shard_map/place/pallas_call | solution.py:288
  71.8 5.7 %all-gather.3.cloned.1.call-done = bf16[16,2,4,128,128]{4,3,2,1,0:T(8,128)(2,1)} async-done(((bf16[2,2,4,128,128]{4,3,2,1,0:T(8,128)(2,1)}), bf16[16,2,4,128,128]{4,3,2,1,0:T(8,128)(2,1)}) %all-gather.3.cloned.1.call-update) | async-done | bytes 4194320 | tf_op jit(solution)/shard_map/all_gather | solution.py:283
  77.6 9.3 %first.1 = (bf16[4,256,128]{2,1,0:T(8,128)(2,1)}, bf16[4,256,128]{2,1,0:T(8,128)(2,1)}, bf16[8,2,2,4,128,128]{5,4,3,2,1,0:T(8,128)(2,1)}) custom-call(s32[4,16]{1,0:T(4,128)} %add_select_fusion.rows_in.rows, bf16[16,256,512]{2,1,0:T(8,128)(2,1)} %get-tuple-element.24.x_in, bf16[16,256,512]{2,1,0:T(8,128)(2,1)} %get-tuple-element.25.g_in, ...), custom_call_target="tpu_custom_call" | custom-call | flops 2000000000 | bytes 16777216 | tf_op jit(solution)/shard_map/first/pallas_call | solution.py:304
  87.8 8.5 %second.1 = (bf16[4,2,128,512]{3,2,1,0:T(8,128)(2,1)}, bf16[4,2,128,512]{3,2,1,0:T(8,128)(2,1)}, bf16[4,2,128,512]{3,2,1,0:T(8,128)(2,1)}, bf16[4,2,128,512]{3,2...) custom-call(s32[128]{0:T(128)} %add.279.outs_at, ...), custom_call_target="tpu_custom_call" | custom-call | flops 1000000000 | bytes 16777216 | tf_op jit(solution)/shard_map/second/pallas_call | solution.py:333
  97.6 1.9 %collective-permute-done.16 = bf16[4,2,128,512]{3,2,1,0:T(8,128)(2,1)S(1)} collective-permute-done((bf16[4,2,128,512]{3,2,1,0:T(8,128)(2,1)}, bf16[4,2,128,512]{3,2,1,0:T(8,128)(2,1)S(1)}, u32[]{:S(2)}, u32[]{:S(2)}) %collective-permute-start.16) | collective-permute-done | bytes 1048608 | tf_op jit(solution)/shard_map/ppermute | solution.py:25
  99.5 1.5 add_convert_fusion.1
  101.1 2.4 %collective-permute-start.17 = (bf16[4,2,128,512]{3,2,1,0:T(8,128)(2,1)S(1)}, bf16[4,2,128,512]{3,2,1,0:T(8,128)(2,1)S(1)}, u32[]{:S(2)}, u32[]{:S(2)}) collective-permute-start(bf16[4,2,128,512]{3,2,1,0:T(8,128)(2,1)S(1)} %add_convert_fusion.1), channel_id=1, source_target_pairs={{0,130},{1,13},{2,0},{3,15},{4,134},{5,1},{6,4},{7,3},{8,138},{9,5... | collective-permute-start | bytes 3145736 | tf_op jit(solution)/shard_map/ppermute | solution.py:25
  104.3 1.9 %collective-permute-start.13 = (bf16[4,2,128,512]{3,2,1,0:T(8,128)(2,1)S(1)}, bf16[4,2,128,512]{3,2,1,0:T(8,128)(2,1)S(1)}, u32[]{:S(2)}, u32[]{:S(2)}) collective-permute-start(bf16[4,2,128,512]{3,2,1,0:T(8,128)(2,1)S(1)} %add_convert_fusion.3), channel_id=1, source_target_pairs={{0,128},{1,9},{2,130},{3,11},{4,132},{5,13},{6,134},{7,15},{8,136}... | collective-permute-start | bytes 3145736 | tf_op jit(solution)/shard_map/ppermute | solution.py:25
  106.2 20.3 %collective-permute-done.17 = bf16[4,2,128,512]{3,2,1,0:T(8,128)(2,1)S(1)} collective-permute-done((bf16[4,2,128,512]{3,2,1,0:T(8,128)(2,1)S(1)}, bf16[4,2,128,512]{3,2,1,0:T(8,128)(2,1)S(1)}, u32[]{:S(2)}, u32[]{:S(2)}) %collective-permute-start.17) | collective-permute-done | bytes 1048608 | tf_op jit(solution)/shard_map/ppermute | solution.py:25
  126.5 3.9 %collective-permute-done.15 = bf16[4,2,128,512]{3,2,1,0:T(8,128)(2,1)S(1)} collective-permute-done((bf16[4,2,128,512]{3,2,1,0:T(8,128)(2,1)S(1)}, bf16[4,2,128,512]{3,2,1,0:T(8,128)(2,1)S(1)}, u32[]{:S(2)}, u32[]{:S(2)}) %collective-permute-start.15) | collective-permute-done | bytes 1048608 | tf_op jit(solution)/shard_map/ppermute | solution.py:25
  131.3 2.8 %collective-permute-start.18 = (bf16[2,128,512]{2,1,0:T(8,128)(2,1)S(1)}, bf16[2,128,512]{2,1,0:T(8,128)(2,1)S(1)}, u32[]{:S(2)}, u32[]{:S(2)}) collective-permute-start(bf16[2,128,512]{2,1,0:T(8,128)(2,1)S(1)} %get-tuple-element.58), channel_id=1, source_target_pairs={{0,8},{1,129},{2,10},{3,131},{4,12},{5,133},{6,14},{7,135},{8,0},{... | collective-permute-start | bytes 786440 | tf_op jit(solution)/shard_map/ppermute | solution.py:25
  134.4 2.4 %collective-permute-start.20 = (bf16[2,128,512]{2,1,0:T(8,128)(2,1)S(1)}, bf16[2,128,512]{2,1,0:T(8,128)(2,1)S(1)}, u32[]{:S(2)}, u32[]{:S(2)}) collective-permute-start(bf16[2,128,512]{2,1,0:T(8,128)(2,1)S(1)} %get-tuple-element.56), channel_id=1, source_target_pairs={{0,12},{1,131},{2,14},{3,1},{4,0},{5,135},{6,2},{7,5},{8,4},{9,139... | collective-permute-start | bytes 786440 | tf_op jit(solution)/shard_map/ppermute | solution.py:25
  136.8 4.2 %reduce-scatter.2.cloned.1.call-done = bf16[1,2,2,4,128,128]{5,4,3,2,1,0:T(8,128)(2,1)} async-done(((bf16[8,2,2,4,128,128]{5,4,3,2,1,0:T(8,128)(2,1)}), bf16[1,2,2,4,128,128]{5,4,3,2,1,0:T(8,128)(2,1)}) %reduce-scatter.2.cloned.1.call-update) | async-done | bytes 524304 | tf_op jit(solution)/shard_map/reduce_scatter | solution.py:329
  141.0 1.1 slice_bitcast_fusion.4
  142.1 2.8 %collective-permute-start.21 = (bf16[4,128,128]{2,1,0:T(8,128)(2,1)S(1)}, bf16[4,128,128]{2,1,0:T(8,128)(2,1)S(1)}, u32[]{:S(2)}, u32[]{:S(2)}) collective-permute-start(bf16[4,128,128]{2,1,0:T(8,128)(2,1)S(1)} %get-tuple-element.63), channel_id=1, source_target_pairs={{0,128},{1,129},{2,130},{3,131},{4,132},{5,133},{6,134},{7,135},{8... | collective-permute-start | bytes 393224 | tf_op jit(solution)/shard_map/ppermute | solution.py:25
  145.6 2.6 %collective-permute-done.21 = bf16[4,128,128]{2,1,0:T(8,128)(2,1)S(1)} collective-permute-done((bf16[4,128,128]{2,1,0:T(8,128)(2,1)S(1)}, bf16[4,128,128]{2,1,0:T(8,128)(2,1)S(1)}, u32[]{:S(2)}, u32[]{:S(2)}) %collective-permute-start.21) | collective-permute-done | bytes 131104 | tf_op jit(solution)/shard_map/ppermute | solution.py:25
  149.0 1.5 collective-permute-done.22
  (77 shorter events, 13.7 us)
Async XLA Ops:
  7.2 10.8 %copy-start.6 = (bf16[128,512]{1,0:T(8,128)(2,1)S(1)}, bf16[128,512]{1,0:T(8,128)(2,1)}, u32[]{:S(2)}) copy-start(bf16[128,512]{1,0:T(8,128)(2,1)} %param.11) | copy-start | bytes 393220
  7.2 10.8 %copy-start.7 = (bf16[128,512]{1,0:T(8,128)(2,1)S(1)}, bf16[128,512]{1,0:T(8,128)(2,1)}, u32[]{:S(2)}) copy-start(bf16[128,512]{1,0:T(8,128)(2,1)} %param.7) | copy-start | bytes 393220
  7.2 70.4 %all-gather.3.cloned.1.call-start = ((), (), s32[]{:S(2)}) async-start(), calls=%async_computation.2 | async-start | bytes 4718592 | tf_op jit(solution)/shard_map/all_gather | solution.py:283
  8.3 8.8 %collective-permute-start.10 = (bf16[2,4,128,128]{3,2,1,0:T(8,128)(2,1)S(1)}, bf16[2,4,128,128]{3,2,1,0:T(8,128)(2,1)S(1)}, u32[]{:S(2)}, u32[]{:S(2)}) collective-permute-start(bf16[2,4,128,128]{3,2,1,0:T(8,128)(2,1)S(1)} %fusion), channel_id=1, source_target_pairs={{0,128},{1,129},{2,130},{3,131},{4,132},{5,133},{6,134},{7,135},{8... | collective-permute-start | bytes 786440 | tf_op jit(solution)/shard_map/ppermute | solution.py:25
  17.1 44.0 %copy-start.9 = (s32[4]{0:T(128)S(1)}, s32[4]{0:T(128)}, u32[]{:S(2)}) copy-start(s32[4]{0:T(128)} %constant.182.clone) | copy-start | bytes 52
  17.1 45.0 %copy-start.8 = (s32[8,16]{1,0:T(8,128)S(1)}, s32[8,16]{1,0:T(8,128)}, u32[]{:S(2)}) copy-start(s32[8,16]{1,0:T(8,128)} %param.8) | copy-start | bytes 1540
  18.0 123.0 %reduce-scatter.2.cloned.1.call-start = ((), (), s32[]{:S(2)}) async-start(), calls=%async_computation.1 | async-start | bytes 4718592 | tf_op jit(solution)/shard_map/reduce_scatter | solution.py:329
  18.1 7.8 %collective-permute-start.2 = (bf16[2,128,512]{2,1,0:T(8,128)(2,1)S(1)}, bf16[2,128,512]{2,1,0:T(8,128)(2,1)S(1)}, u32[]{:S(2)}, u32[]{:S(2)}) collective-permute-start(bf16[2,128,512]{2,1,0:T(8,128)(2,1)S(1)} %get-tuple-element.67), channel_id=1, source_target_pairs={{0,8},{1,129},{2,10},{3,131},{4,12},{5,133},{6,14},{7,135},{8,0},{... | collective-permute-start | bytes 786440 | tf_op jit(solution)/shard_map/ppermute | solution.py:25
  21.9 7.3 %collective-permute-start.1 = (bf16[2,128,512]{2,1,0:T(8,128)(2,1)S(1)}, bf16[2,128,512]{2,1,0:T(8,128)(2,1)S(1)}, u32[]{:S(2)}, u32[]{:S(2)}) collective-permute-start(bf16[2,128,512]{2,1,0:T(8,128)(2,1)S(1)} %get-tuple-element.67), channel_id=1, source_target_pairs={{0,12},{1,131},{2,14},{3,1},{4,0},{5,135},{6,2},{7,5},{8,4},{9,139... | collective-permute-start | bytes 786440 | tf_op jit(solution)/shard_map/ppermute | solution.py:25
  22.6 6.7 %collective-permute-start = (bf16[2,128,512]{2,1,0:T(8,128)(2,1)S(1)}, bf16[2,128,512]{2,1,0:T(8,128)(2,1)S(1)}, u32[]{:S(2)}, u32[]{:S(2)}) collective-permute-start(bf16[2,128,512]{2,1,0:T(8,128)(2,1)S(1)} %get-tuple-element.67), channel_id=1, source_target_pairs={{0,4},{1,3},{2,6},{3,129},{4,8},{5,7},{6,10},{7,133},{8,12},{9,11}... | collective-permute-start | bytes 786440 | tf_op jit(solution)/shard_map/ppermute | solution.py:25
  29.5 34.2 %copy-start = (bf16[4,2,128,512]{3,2,1,0:T(8,128)(2,1)}, bf16[4,2,128,512]{3,2,1,0:T(8,128)(2,1)S(1)}, u32[]{:S(2)}) copy-start(bf16[4,2,128,512]{3,2,1,0:T(8,128)(2,1)S(1)} %pad_maximum_fusion.refs_0_) | copy-start | bytes 3145732
  29.5 15.3 %collective-permute-start.3 = (bf16[4,2,128,512]{3,2,1,0:T(8,128)(2,1)S(1)}, bf16[4,2,128,512]{3,2,1,0:T(8,128)(2,1)S(1)}, u32[]{:S(2)}, u32[]{:S(2)}) collective-permute-start(bf16[4,2,128,512]{3,2,1,0:T(8,128)(2,1)S(1)} %pad_maximum_fusion.refs_0_), channel_id=1, source_target_pairs={{0,2},{1,5},{2,128},{3,7},{4,6},{5,9},{6,132},{7,11},{8,10},{9,13}... | collective-permute-start | bytes 3145736 | tf_op jit(solution)/shard_map/ppermute | solution.py:25
  30.6 24.6 %collective-permute-start.4 = (bf16[4,2,128,512]{3,2,1,0:T(8,128)(2,1)S(1)}, bf16[4,2,128,512]{3,2,1,0:T(8,128)(2,1)S(1)}, u32[]{:S(2)}, u32[]{:S(2)}) collective-permute-start(bf16[4,2,128,512]{3,2,1,0:T(8,128)(2,1)S(1)} %pad_maximum_fusion.refs_0_), channel_id=1, source_target_pairs={{0,130},{1,13},{2,0},{3,15},{4,134},{5,1},{6,4},{7,3},{8,138},{9,5... | collective-permute-start | bytes 3145736 | tf_op jit(solution)/shard_map/ppermute | solution.py:25
  32.3 24.8 %collective-permute-start.5 = (bf16[4,2,128,512]{3,2,1,0:T(8,128)(2,1)S(1)}, bf16[4,2,128,512]{3,2,1,0:T(8,128)(2,1)}, u32[]{:S(2)}, u32[]{:S(2)}) collective-permute-start(bf16[4,2,128,512]{3,2,1,0:T(8,128)(2,1)S(1)} %pad_maximum_fusion.refs_0_), channel_id=1, source_target_pairs={{0,128},{1,9},{2,130},{3,11},{4,132},{5,13},{6,134},{7,15},{8,136}... | collective-permute-start | bytes 3145736 | tf_op jit(solution)/shard_map/ppermute | solution.py:25
  33.6 29.2 %collective-permute-start.6 = (bf16[4,2,128,512]{3,2,1,0:T(8,128)(2,1)S(1)}, bf16[4,2,128,512]{3,2,1,0:T(8,128)(2,1)}, u32[]{:S(2)}, u32[]{:S(2)}) collective-permute-start(bf16[4,2,128,512]{3,2,1,0:T(8,128)(2,1)S(1)} %pad_maximum_fusion.refs_0_), channel_id=1, source_target_pairs={{0,1},{1,0},{2,3},{3,2},{4,5},{5,4},{6,7},{7,6},{8,9},{9,8},{10,11... | collective-permute-start | bytes 3145736 | tf_op jit(solution)/shard_map/ppermute | solution.py:25
  44.9 18.8 %copy-start.1 = (bf16[4,2,128,512]{3,2,1,0:T(8,128)(2,1)}, bf16[4,2,128,512]{3,2,1,0:T(8,128)(2,1)S(1)}, u32[]{:S(2)}) copy-start(bf16[4,2,128,512]{3,2,1,0:T(8,128)(2,1)S(1)} %collective-permute-done.3.refs_1_) | copy-start | bytes 3145732
  44.9 18.0 %collective-permute-start.7 = (bf16[4,2,128,512]{3,2,1,0:T(8,128)(2,1)S(1)}, bf16[4,2,128,512]{3,2,1,0:T(8,128)(2,1)}, u32[]{:S(2)}, u32[]{:S(2)}) collective-permute-start(bf16[4,2,128,512]{3,2,1,0:T(8,128)(2,1)S(1)} %collective-permute-done.3.refs_1_), channel_id=1, source_target_pairs={{0,1},{1,0},{2,3},{3,2},{4,5},{5,4},{6,7},{7,6},{8,9},{9,8},{10,11... | collective-permute-start | bytes 3145736 | tf_op jit(solution)/shard_map/ppermute | solution.py:25
  55.3 7.6 %collective-permute-start.8 = (bf16[4,2,128,512]{3,2,1,0:T(8,128)(2,1)S(1)}, bf16[4,2,128,512]{3,2,1,0:T(8,128)(2,1)}, u32[]{:S(2)}, u32[]{:S(2)}) collective-permute-start(bf16[4,2,128,512]{3,2,1,0:T(8,128)(2,1)S(1)} %collective-permute-done.4.refs_2_), channel_id=1, source_target_pairs={{0,1},{1,0},{2,3},{3,2},{4,5},{5,4},{6,7},{7,6},{8,9},{9,8},{10,11... | collective-permute-start | bytes 3145736 | tf_op jit(solution)/shard_map/ppermute | solution.py:25
  57.1 6.6 %collective-permute-start.9 = (bf16[4,2,128,512]{3,2,1,0:T(8,128)(2,1)}, bf16[4,2,128,512]{3,2,1,0:T(8,128)(2,1)}, u32[]{:S(2)}, u32[]{:S(2)}) collective-permute-start(bf16[4,2,128,512]{3,2,1,0:T(8,128)(2,1)} %collective-permute-done.5.refs_3_), channel_id=1, source_target_pairs={{0,1},{1,0},{2,3},{3,2},{4,5},{5,4},{6,7},{7,6},{8,9},{9,8},{10,11... | collective-permute-start | bytes 3145736 | tf_op jit(solution)/shard_map/ppermute | solution.py:25
  96.3 3.2 %collective-permute-start.16 = (bf16[4,2,128,512]{3,2,1,0:T(8,128)(2,1)}, bf16[4,2,128,512]{3,2,1,0:T(8,128)(2,1)S(1)}, u32[]{:S(2)}, u32[]{:S(2)}) collective-permute-start(bf16[4,2,128,512]{3,2,1,0:T(8,128)(2,1)} %get-tuple-element.37), channel_id=1, source_target_pairs={{0,1},{1,0},{2,3},{3,2},{4,5},{5,4},{6,7},{7,6},{8,9},{9,8},{10,11... | collective-permute-start | bytes 3145736 | tf_op jit(solution)/shard_map/ppermute | solution.py:25
  97.0 6.5 %collective-permute-start.14 = (bf16[4,2,128,512]{3,2,1,0:T(8,128)(2,1)}, bf16[4,2,128,512]{3,2,1,0:T(8,128)(2,1)S(1)}, u32[]{:S(2)}, u32[]{:S(2)}) collective-permute-start(bf16[4,2,128,512]{3,2,1,0:T(8,128)(2,1)} %get-tuple-element.35), channel_id=1, source_target_pairs={{0,1},{1,0},{2,3},{3,2},{4,5},{5,4},{6,7},{7,6},{8,9},{9,8},{10,11... | collective-permute-start | bytes 3145736 | tf_op jit(solution)/shard_map/ppermute | solution.py:25
  97.1 6.8 %collective-permute-start.12 = (bf16[4,2,128,512]{3,2,1,0:T(8,128)(2,1)}, bf16[4,2,128,512]{3,2,1,0:T(8,128)(2,1)S(1)}, u32[]{:S(2)}, u32[]{:S(2)}) collective-permute-start(bf16[4,2,128,512]{3,2,1,0:T(8,128)(2,1)} %get-tuple-element.33), channel_id=1, source_target_pairs={{0,1},{1,0},{2,3},{3,2},{4,5},{5,4},{6,7},{7,6},{8,9},{9,8},{10,11... | collective-permute-start | bytes 3145736 | tf_op jit(solution)/shard_map/ppermute | solution.py:25
  97.5 8.6 %collective-permute-start.11 = (bf16[4,2,128,512]{3,2,1,0:T(8,128)(2,1)}, bf16[4,2,128,512]{3,2,1,0:T(8,128)(2,1)S(1)}, u32[]{:S(2)}, u32[]{:S(2)}) collective-permute-start(bf16[4,2,128,512]{3,2,1,0:T(8,128)(2,1)} %get-tuple-element.31), channel_id=1, source_target_pairs={{0,1},{1,0},{2,3},{3,2},{4,5},{5,4},{6,7},{7,6},{8,9},{9,8},{10,11... | collective-permute-start | bytes 3145736 | tf_op jit(solution)/shard_map/ppermute | solution.py:25
  101.1 25.4 %collective-permute-start.17 = (bf16[4,2,128,512]{3,2,1,0:T(8,128)(2,1)S(1)}, bf16[4,2,128,512]{3,2,1,0:T(8,128)(2,1)S(1)}, u32[]{:S(2)}, u32[]{:S(2)}) collective-permute-start(bf16[4,2,128,512]{3,2,1,0:T(8,128)(2,1)S(1)} %add_convert_fusion.1), channel_id=1, source_target_pairs={{0,130},{1,13},{2,0},{3,15},{4,134},{5,1},{6,4},{7,3},{8,138},{9,5... | collective-permute-start | bytes 3145736 | tf_op jit(solution)/shard_map/ppermute | solution.py:25
  103.9 26.6 %copy-start.5 = (bf16[4,2,128,512]{3,2,1,0:T(8,128)(2,1)S(1)}, bf16[4,2,128,512]{3,2,1,0:T(8,128)(2,1)}, u32[]{:S(2)}) copy-start(bf16[4,2,128,512]{3,2,1,0:T(8,128)(2,1)} %get-tuple-element.30) | copy-start | bytes 3145732
  103.9 26.6 %collective-permute-start.15 = (bf16[4,2,128,512]{3,2,1,0:T(8,128)(2,1)S(1)}, bf16[4,2,128,512]{3,2,1,0:T(8,128)(2,1)S(1)}, u32[]{:S(2)}, u32[]{:S(2)}) collective-permute-start(bf16[4,2,128,512]{3,2,1,0:T(8,128)(2,1)S(1)} %add_convert_fusion.2), channel_id=1, source_target_pairs={{0,2},{1,5},{2,128},{3,7},{4,6},{5,9},{6,132},{7,11},{8,10},{9,13}... | collective-permute-start | bytes 3145736 | tf_op jit(solution)/shard_map/ppermute | solution.py:25
  104.3 26.1 %collective-permute-start.13 = (bf16[4,2,128,512]{3,2,1,0:T(8,128)(2,1)S(1)}, bf16[4,2,128,512]{3,2,1,0:T(8,128)(2,1)S(1)}, u32[]{:S(2)}, u32[]{:S(2)}) collective-permute-start(bf16[4,2,128,512]{3,2,1,0:T(8,128)(2,1)S(1)} %add_convert_fusion.3), channel_id=1, source_target_pairs={{0,128},{1,9},{2,130},{3,11},{4,132},{5,13},{6,134},{7,15},{8,136}... | collective-permute-start | bytes 3145736 | tf_op jit(solution)/shard_map/ppermute | solution.py:25
  131.3 14.2 %collective-permute-start.18 = (bf16[2,128,512]{2,1,0:T(8,128)(2,1)S(1)}, bf16[2,128,512]{2,1,0:T(8,128)(2,1)S(1)}, u32[]{:S(2)}, u32[]{:S(2)}) collective-permute-start(bf16[2,128,512]{2,1,0:T(8,128)(2,1)S(1)} %get-tuple-element.58), channel_id=1, source_target_pairs={{0,8},{1,129},{2,10},{3,131},{4,12},{5,133},{6,14},{7,135},{8,0},{... | collective-permute-start | bytes 786440 | tf_op jit(solution)/shard_map/ppermute | solution.py:25
  134.1 11.4 %collective-permute-start.19 = (bf16[2,128,512]{2,1,0:T(8,128)(2,1)S(1)}, bf16[2,128,512]{2,1,0:T(8,128)(2,1)S(1)}, u32[]{:S(2)}, u32[]{:S(2)}) collective-permute-start(bf16[2,128,512]{2,1,0:T(8,128)(2,1)S(1)} %get-tuple-element.57), channel_id=1, source_target_pairs={{0,4},{1,3},{2,6},{3,129},{4,8},{5,7},{6,10},{7,133},{8,12},{9,11}... | collective-permute-start | bytes 786440 | tf_op jit(solution)/shard_map/ppermute | solution.py:25
  134.4 11.1 %collective-permute-start.20 = (bf16[2,128,512]{2,1,0:T(8,128)(2,1)S(1)}, bf16[2,128,512]{2,1,0:T(8,128)(2,1)S(1)}, u32[]{:S(2)}, u32[]{:S(2)}) collective-permute-start(bf16[2,128,512]{2,1,0:T(8,128)(2,1)S(1)} %get-tuple-element.56), channel_id=1, source_target_pairs={{0,12},{1,131},{2,14},{3,1},{4,0},{5,135},{6,2},{7,5},{8,4},{9,139... | collective-permute-start | bytes 786440 | tf_op jit(solution)/shard_map/ppermute | solution.py:25
  142.1 6.0 %collective-permute-start.21 = (bf16[4,128,128]{2,1,0:T(8,128)(2,1)S(1)}, bf16[4,128,128]{2,1,0:T(8,128)(2,1)S(1)}, u32[]{:S(2)}, u32[]{:S(2)}) collective-permute-start(bf16[4,128,128]{2,1,0:T(8,128)(2,1)S(1)} %get-tuple-element.63), channel_id=1, source_target_pairs={{0,128},{1,129},{2,130},{3,131},{4,132},{5,133},{6,134},{7,135},{8... | collective-permute-start | bytes 393224 | tf_op jit(solution)/shard_map/ppermute | solution.py:25
  145.0 5.4 %collective-permute-start.22 = (bf16[4,128,128]{2,1,0:T(8,128)(2,1)S(1)}, bf16[4,128,128]{2,1,0:T(8,128)(2,1)S(1)}, u32[]{:S(2)}, u32[]{:S(2)}) collective-permute-start(bf16[4,128,128]{2,1,0:T(8,128)(2,1)S(1)} %bitcast.71), channel_id=1, source_target_pairs={{0,128},{1,129},{2,130},{3,131},{4,132},{5,133},{6,134},{7,135},{8... | collective-permute-start | bytes 393224 | tf_op jit(solution)/shard_map/ppermute | solution.py:25
  (3 other events, 18.6 us)
Sparse Core Ops, SparseCore 0:
  18.1 59.4 all-gather.2
  87.0 53.9 reduce-scatter.1

commit v6 on v5

--- a/solution.py
+++ b/solution.py
@@ -357,10 +357,10 @@
         )
         return halves.astype(f32)[:, None]
 
+    other_up = send(jnp.swapaxes(summed[1, 0], 1, 2), other_half)
     other_down = send(summed[1, 1], other_half)
-    other_up = send(jnp.swapaxes(summed[1, 0], 1, 2), other_half)
     own_up = jnp.swapaxes(lax.optimization_barrier(summed[0, 0]), 1, 2)
-    last, other_down = lax.optimization_barrier((last, other_down))
+    last, other_up = lax.optimization_barrier((last, other_up))
     grad_down = assemble(summed[0, 1], other_down)
     grad_up = assemble(own_up, other_up)
     result = total(last).astype(bf16)

time: 160 us -> 159 us (level)
  transfers between devices with their start and end apart: 25 -> 25, of which waited for: 15 -> 15; matrix products, arithmetic and copies ran while one was open for 6% -> 6% of each run, Pallas kernels for 10% -> 11%
where the time goes in v6:
time: 159 us; the launch traced here: 158 us
  waiting for transfers between devices  66.1 us (42%)
  starting transfers between devices  39.3 us (25%)
  Pallas kernels  25.9 us (16%)
  between operations  14.3 us (9%)
  other arithmetic  9.25 us (6%)
  local copies, waits for them, and re-layouts  3.38 us (2%)
    ppermute x23, waiting for transfers between devices, send(): lax.ppermute(value, AXES, [(source, place_of(*step(*where_is(source)))) f...  56.2 us
    ppermute x23, starting transfers between devices, send(): lax.ppermute(value, AXES, [(source, place_of(*step(*where_is(source)))) f...  39.3 us
    pallas_call x1, Pallas kernels, local(): pl.pallas_call(first_kernel, out_shape=[jax.ShapeDtypeStruct((4, 2 * B, B...  9.26 us
    pallas_call x1, Pallas kernels, local(): pl.pallas_call(second_kernel, out_shape=[jax.ShapeDtypeStruct((4, 2, B, 4...  8.52 us
    pallas_call x1, Pallas kernels, local(): pl.pallas_call(place_kernel, out_shape=[gathered] * 2, in_specs=[SMEM] +...  8.12 us
    all_gather x1, waiting for transfers between devices, local(): lax.all_gather(jnp.stack([piece_a, other_b]), 'dp', axis_index_groups=HAL...  5.74 us
    reduce_scatter x1, waiting for transfers between devices, local(): lax.psum_scatter(grads, 'dp', scatter_dimension=0, axis_index_groups=HALV...  4.15 us
  transfers between devices with their start and end apart: 25, of which 15 were waited for; matrix products, arithmetic and copies ran while one was open for 6% of the time, Pallas kernels for 11%

profile of v6, /device:TPU:1, one launch (start us, length us, event | category | flops | bytes accessed | tf_op | source)
XLA Modules:
  0.0 158.3 jit_solution(2471183381488365562)
XLA Ops:
  7.3 1.0 fusion
  8.3 3.8 %collective-permute-start.10 = (bf16[2,4,128,128]{3,2,1,0:T(8,128)(2,1)S(1)}, bf16[2,4,128,128]{3,2,1,0:T(8,128)(2,1)S(1)}, u32[]{:S(2)}, u32[]{:S(2)}) collective-permute-start(bf16[2,4,128,128]{3,2,1,0:T(8,128)(2,1)S(1)} %fusion), channel_id=1, source_target_pairs={{0,128},{1,129},{2,130},{3,131},{4,132},{5,133},{6,134},{7,135},{8... | collective-permute-start | bytes 786440 | tf_op jit(solution)/shard_map/ppermute | solution.py:25
  12.1 1.0 fusion.2
  13.1 4.0 %collective-permute-done.10 = bf16[2,4,128,128]{3,2,1,0:T(8,128)(2,1)S(1)} collective-permute-done((bf16[2,4,128,128]{3,2,1,0:T(8,128)(2,1)S(1)}, bf16[2,4,128,128]{3,2,1,0:T(8,128)(2,1)S(1)}, u32[]{:S(2)}, u32[]{:S(2)}) %collective-permute-start.10) | collective-permute-done | bytes 262176 | tf_op jit(solution)/shard_map/ppermute | solution.py:25
  18.1 3.8 %collective-permute-start.2 = (bf16[2,128,512]{2,1,0:T(8,128)(2,1)S(1)}, bf16[2,128,512]{2,1,0:T(8,128)(2,1)S(1)}, u32[]{:S(2)}, u32[]{:S(2)}) collective-permute-start(bf16[2,128,512]{2,1,0:T(8,128)(2,1)S(1)} %get-tuple-element.67), channel_id=1, source_target_pairs={{0,8},{1,129},{2,10},{3,131},{4,12},{5,133},{6,14},{7,135},{8,0},{... | collective-permute-start | bytes 786440 | tf_op jit(solution)/shard_map/ppermute | solution.py:25
  23.3 2.6 %collective-permute-done.2 = bf16[2,128,512]{2,1,0:T(8,128)(2,1)S(1)} collective-permute-done((bf16[2,128,512]{2,1,0:T(8,128)(2,1)S(1)}, bf16[2,128,512]{2,1,0:T(8,128)(2,1)S(1)}, u32[]{:S(2)}, u32[]{:S(2)}) %collective-permute-start.2) | collective-permute-done | bytes 262176 | tf_op jit(solution)/shard_map/ppermute | solution.py:25
  25.9 3.2 %collective-permute-done.1 = bf16[2,128,512]{2,1,0:T(8,128)(2,1)S(1)} collective-permute-done((bf16[2,128,512]{2,1,0:T(8,128)(2,1)S(1)}, bf16[2,128,512]{2,1,0:T(8,128)(2,1)S(1)}, u32[]{:S(2)}, u32[]{:S(2)}) %collective-permute-start.1) | collective-permute-done | bytes 262176 | tf_op jit(solution)/shard_map/ppermute | solution.py:25
  29.5 1.1 collective-permute-start.3
  30.6 1.7 %collective-permute-start.4 = (bf16[4,2,128,512]{3,2,1,0:T(8,128)(2,1)S(1)}, bf16[4,2,128,512]{3,2,1,0:T(8,128)(2,1)S(1)}, u32[]{:S(2)}, u32[]{:S(2)}) collective-permute-start(bf16[4,2,128,512]{3,2,1,0:T(8,128)(2,1)S(1)} %pad_maximum_fusion.refs_0_), channel_id=1, source_target_pairs={{0,130},{1,13},{2,0},{3,15},{4,134},{5,1},{6,4},{7,3},{8,138},{9,5... | collective-permute-start | bytes 3145736 | tf_op jit(solution)/shard_map/ppermute | solution.py:25
  32.3 1.3 collective-permute-start.5
  33.6 4.1 %collective-permute-start.6 = (bf16[4,2,128,512]{3,2,1,0:T(8,128)(2,1)S(1)}, bf16[4,2,128,512]{3,2,1,0:T(8,128)(2,1)}, u32[]{:S(2)}, u32[]{:S(2)}) collective-permute-start(bf16[4,2,128,512]{3,2,1,0:T(8,128)(2,1)S(1)} %pad_maximum_fusion.refs_0_), channel_id=1, source_target_pairs={{0,1},{1,0},{2,3},{3,2},{4,5},{5,4},{6,7},{7,6},{8,9},{9,8},{10,11... | collective-permute-start | bytes 3145736 | tf_op jit(solution)/shard_map/ppermute | solution.py:25
  37.7 7.2 %collective-permute-done.3.refs_1_ = bf16[4,2,128,512]{3,2,1,0:T(8,128)(2,1)S(1)} collective-permute-done((bf16[4,2,128,512]{3,2,1,0:T(8,128)(2,1)S(1)}, bf16[4,2,128,512]{3,2,1,0:T(8,128)(2,1)S(1)}, u32[]{:S(2)}, u32[]{:S(2)}) %collective-permute-start.3) | collective-permute-done | bytes 1048608 | tf_op jit(solution)/shard_map/ppermute | solution.py:25
  44.9 3.6 %collective-permute-start.7 = (bf16[4,2,128,512]{3,2,1,0:T(8,128)(2,1)S(1)}, bf16[4,2,128,512]{3,2,1,0:T(8,128)(2,1)}, u32[]{:S(2)}, u32[]{:S(2)}) collective-permute-start(bf16[4,2,128,512]{3,2,1,0:T(8,128)(2,1)S(1)} %collective-permute-done.3.refs_1_), channel_id=1, source_target_pairs={{0,1},{1,0},{2,3},{3,2},{4,5},{5,4},{6,7},{7,6},{8,9},{9,8},{10,11... | collective-permute-start | bytes 3145736 | tf_op jit(solution)/shard_map/ppermute | solution.py:25
  48.5 6.8 %collective-permute-done.4.refs_2_ = bf16[4,2,128,512]{3,2,1,0:T(8,128)(2,1)S(1)} collective-permute-done((bf16[4,2,128,512]{3,2,1,0:T(8,128)(2,1)S(1)}, bf16[4,2,128,512]{3,2,1,0:T(8,128)(2,1)S(1)}, u32[]{:S(2)}, u32[]{:S(2)}) %collective-permute-start.4) | collective-permute-done | bytes 1048608 | tf_op jit(solution)/shard_map/ppermute | solution.py:25
  55.3 1.8 %collective-permute-done.5.refs_3_ = bf16[4,2,128,512]{3,2,1,0:T(8,128)(2,1)} collective-permute-done((bf16[4,2,128,512]{3,2,1,0:T(8,128)(2,1)S(1)}, bf16[4,2,128,512]{3,2,1,0:T(8,128)(2,1)}, u32[]{:S(2)}, u32[]{:S(2)}) %collective-permute-start.5) | collective-permute-done | bytes 1048608 | tf_op jit(solution)/shard_map/ppermute | solution.py:25
  57.1 4.0 %collective-permute-start.9 = (bf16[4,2,128,512]{3,2,1,0:T(8,128)(2,1)}, bf16[4,2,128,512]{3,2,1,0:T(8,128)(2,1)}, u32[]{:S(2)}, u32[]{:S(2)}) collective-permute-start(bf16[4,2,128,512]{3,2,1,0:T(8,128)(2,1)} %collective-permute-done.5.refs_3_), channel_id=1, source_target_pairs={{0,1},{1,0},{2,3},{3,2},{4,5},{5,4},{6,7},{7,6},{8,9},{9,8},{10,11... | collective-permute-start | bytes 3145736 | tf_op jit(solution)/shard_map/ppermute | solution.py:25
  63.7 8.1 %place.1 = (bf16[16,256,512]{2,1,0:T(8,128)(2,1)}, bf16[16,256,512]{2,1,0:T(8,128)(2,1)}) custom-call(s32[32]{0:T(128)} %pad_add_fusion.spots, bf16[4,2,128,512]{3,2,1,0:T(8,128)(2,1)} %copy-done, bf16[4,2,128,512]{3,2,1,0:T(8,128)(2,1)} %copy-done.1, bf16[4,2,128,512]{3,2,1,0:T(8,128)(2,1)} %copy-done.2, ...), custom_call_target="tpu_custom_call" | custom-call | bytes 16777216 | tf_op jit(solution)/shard_map/place/pallas_call | solution.py:288
  71.8 5.7 %all-gather.3.cloned.1.call-done = bf16[16,2,4,128,128]{4,3,2,1,0:T(8,128)(2,1)} async-done(((bf16[2,2,4,128,128]{4,3,2,1,0:T(8,128)(2,1)}), bf16[16,2,4,128,128]{4,3,2,1,0:T(8,128)(2,1)}) %all-gather.3.cloned.1.call-update) | async-done | bytes 4194320 | tf_op jit(solution)/shard_map/all_gather | solution.py:283
  77.6 9.3 %first.1 = (bf16[4,256,128]{2,1,0:T(8,128)(2,1)}, bf16[4,256,128]{2,1,0:T(8,128)(2,1)}, bf16[8,2,2,4,128,128]{5,4,3,2,1,0:T(8,128)(2,1)}) custom-call(s32[4,16]{1,0:T(4,128)} %add_select_fusion.rows_in.rows, bf16[16,256,512]{2,1,0:T(8,128)(2,1)} %get-tuple-element.24.x_in, bf16[16,256,512]{2,1,0:T(8,128)(2,1)} %get-tuple-element.25.g_in, ...), custom_call_target="tpu_custom_call" | custom-call | flops 2000000000 | bytes 16777216 | tf_op jit(solution)/shard_map/first/pallas_call | solution.py:304
  87.8 8.5 %second.1 = (bf16[4,2,128,512]{3,2,1,0:T(8,128)(2,1)}, bf16[4,2,128,512]{3,2,1,0:T(8,128)(2,1)}, bf16[4,2,128,512]{3,2,1,0:T(8,128)(2,1)}, bf16[4,2,128,512]{3,2...) custom-call(s32[128]{0:T(128)} %add.279.outs_at, ...), custom_call_target="tpu_custom_call" | custom-call | flops 1000000000 | bytes 16777216 | tf_op jit(solution)/shard_map/second/pallas_call | solution.py:333
  97.6 1.9 %collective-permute-done.16 = bf16[4,2,128,512]{3,2,1,0:T(8,128)(2,1)S(1)} collective-permute-done((bf16[4,2,128,512]{3,2,1,0:T(8,128)(2,1)}, bf16[4,2,128,512]{3,2,1,0:T(8,128)(2,1)S(1)}, u32[]{:S(2)}, u32[]{:S(2)}) %collective-permute-start.16) | collective-permute-done | bytes 1048608 | tf_op jit(solution)/shard_map/ppermute | solution.py:25
  99.5 1.5 add_convert_fusion.1
  101.1 2.4 %collective-permute-start.17 = (bf16[4,2,128,512]{3,2,1,0:T(8,128)(2,1)S(1)}, bf16[4,2,128,512]{3,2,1,0:T(8,128)(2,1)S(1)}, u32[]{:S(2)}, u32[]{:S(2)}) collective-permute-start(bf16[4,2,128,512]{3,2,1,0:T(8,128)(2,1)S(1)} %add_convert_fusion.1), channel_id=1, source_target_pairs={{0,130},{1,13},{2,0},{3,15},{4,134},{5,1},{6,4},{7,3},{8,138},{9,5... | collective-permute-start | bytes 3145736 | tf_op jit(solution)/shard_map/ppermute | solution.py:25
  104.3 1.9 %collective-permute-start.13 = (bf16[4,2,128,512]{3,2,1,0:T(8,128)(2,1)S(1)}, bf16[4,2,128,512]{3,2,1,0:T(8,128)(2,1)S(1)}, u32[]{:S(2)}, u32[]{:S(2)}) collective-permute-start(bf16[4,2,128,512]{3,2,1,0:T(8,128)(2,1)S(1)} %add_convert_fusion.3), channel_id=1, source_target_pairs={{0,128},{1,9},{2,130},{3,11},{4,132},{5,13},{6,134},{7,15},{8,136}... | collective-permute-start | bytes 3145736 | tf_op jit(solution)/shard_map/ppermute | solution.py:25
  106.2 20.3 %collective-permute-done.17 = bf16[4,2,128,512]{3,2,1,0:T(8,128)(2,1)S(1)} collective-permute-done((bf16[4,2,128,512]{3,2,1,0:T(8,128)(2,1)S(1)}, bf16[4,2,128,512]{3,2,1,0:T(8,128)(2,1)S(1)}, u32[]{:S(2)}, u32[]{:S(2)}) %collective-permute-start.17) | collective-permute-done | bytes 1048608 | tf_op jit(solution)/shard_map/ppermute | solution.py:25
  126.5 3.9 %collective-permute-done.15 = bf16[4,2,128,512]{3,2,1,0:T(8,128)(2,1)S(1)} collective-permute-done((bf16[4,2,128,512]{3,2,1,0:T(8,128)(2,1)S(1)}, bf16[4,2,128,512]{3,2,1,0:T(8,128)(2,1)S(1)}, u32[]{:S(2)}, u32[]{:S(2)}) %collective-permute-start.15) | collective-permute-done | bytes 1048608 | tf_op jit(solution)/shard_map/ppermute | solution.py:25
  131.3 2.8 %collective-permute-start.18 = (bf16[2,128,512]{2,1,0:T(8,128)(2,1)S(1)}, bf16[2,128,512]{2,1,0:T(8,128)(2,1)S(1)}, u32[]{:S(2)}, u32[]{:S(2)}) collective-permute-start(bf16[2,128,512]{2,1,0:T(8,128)(2,1)S(1)} %get-tuple-element.58), channel_id=1, source_target_pairs={{0,8},{1,129},{2,10},{3,131},{4,12},{5,133},{6,14},{7,135},{8,0},{... | collective-permute-start | bytes 786440 | tf_op jit(solution)/shard_map/ppermute | solution.py:25
  134.4 2.4 %collective-permute-start.20 = (bf16[2,128,512]{2,1,0:T(8,128)(2,1)S(1)}, bf16[2,128,512]{2,1,0:T(8,128)(2,1)S(1)}, u32[]{:S(2)}, u32[]{:S(2)}) collective-permute-start(bf16[2,128,512]{2,1,0:T(8,128)(2,1)S(1)} %get-tuple-element.56), channel_id=1, source_target_pairs={{0,12},{1,131},{2,14},{3,1},{4,0},{5,135},{6,2},{7,5},{8,4},{9,139... | collective-permute-start | bytes 786440 | tf_op jit(solution)/shard_map/ppermute | solution.py:25
  136.8 4.2 %reduce-scatter.2.cloned.1.call-done = bf16[1,2,2,4,128,128]{5,4,3,2,1,0:T(8,128)(2,1)} async-done(((bf16[8,2,2,4,128,128]{5,4,3,2,1,0:T(8,128)(2,1)}), bf16[1,2,2,4,128,128]{5,4,3,2,1,0:T(8,128)(2,1)}) %reduce-scatter.2.cloned.1.call-update) | async-done | bytes 524304 | tf_op jit(solution)/shard_map/reduce_scatter | solution.py:329
  141.0 1.1 slice_bitcast_fusion.5
  142.2 2.8 %collective-permute-start.21 = (bf16[4,128,128]{2,1,0:T(8,128)(2,1)S(1)}, bf16[4,128,128]{2,1,0:T(8,128)(2,1)S(1)}, u32[]{:S(2)}, u32[]{:S(2)}) collective-permute-start(bf16[4,128,128]{2,1,0:T(8,128)(2,1)S(1)} %bitcast.71), channel_id=1, source_target_pairs={{0,128},{1,129},{2,130},{3,131},{4,132},{5,133},{6,134},{7,135},{8... | collective-permute-start | bytes 393224 | tf_op jit(solution)/shard_map/ppermute | solution.py:25
  145.5 2.7 %collective-permute-done.21 = bf16[4,128,128]{2,1,0:T(8,128)(2,1)S(1)} collective-permute-done((bf16[4,128,128]{2,1,0:T(8,128)(2,1)S(1)}, bf16[4,128,128]{2,1,0:T(8,128)(2,1)S(1)}, u32[]{:S(2)}, u32[]{:S(2)}) %collective-permute-start.21) | collective-permute-done | bytes 131104 | tf_op jit(solution)/shard_map/ppermute | solution.py:25
  (77 shorter events, 13.3 us)
Async XLA Ops:
  7.2 10.8 %copy-start.6 = (bf16[128,512]{1,0:T(8,128)(2,1)S(1)}, bf16[128,512]{1,0:T(8,128)(2,1)}, u32[]{:S(2)}) copy-start(bf16[128,512]{1,0:T(8,128)(2,1)} %param.11) | copy-start | bytes 393220
  7.2 10.8 %copy-start.7 = (bf16[128,512]{1,0:T(8,128)(2,1)S(1)}, bf16[128,512]{1,0:T(8,128)(2,1)}, u32[]{:S(2)}) copy-start(bf16[128,512]{1,0:T(8,128)(2,1)} %param.7) | copy-start | bytes 393220
  7.2 70.4 %all-gather.3.cloned.1.call-start = ((), (), s32[]{:S(2)}) async-start(), calls=%async_computation.2 | async-start | bytes 4718592 | tf_op jit(solution)/shard_map/all_gather | solution.py:283
  8.3 8.8 %collective-permute-start.10 = (bf16[2,4,128,128]{3,2,1,0:T(8,128)(2,1)S(1)}, bf16[2,4,128,128]{3,2,1,0:T(8,128)(2,1)S(1)}, u32[]{:S(2)}, u32[]{:S(2)}) collective-permute-start(bf16[2,4,128,128]{3,2,1,0:T(8,128)(2,1)S(1)} %fusion), channel_id=1, source_target_pairs={{0,128},{1,129},{2,130},{3,131},{4,132},{5,133},{6,134},{7,135},{8... | collective-permute-start | bytes 786440 | tf_op jit(solution)/shard_map/ppermute | solution.py:25
  17.1 44.0 %copy-start.9 = (s32[4]{0:T(128)S(1)}, s32[4]{0:T(128)}, u32[]{:S(2)}) copy-start(s32[4]{0:T(128)} %constant.182.clone) | copy-start | bytes 52
  17.1 45.0 %copy-start.8 = (s32[8,16]{1,0:T(8,128)S(1)}, s32[8,16]{1,0:T(8,128)}, u32[]{:S(2)}) copy-start(s32[8,16]{1,0:T(8,128)} %param.8) | copy-start | bytes 1540
  18.0 123.0 %reduce-scatter.2.cloned.1.call-start = ((), (), s32[]{:S(2)}) async-start(), calls=%async_computation.1 | async-start | bytes 4718592 | tf_op jit(solution)/shard_map/reduce_scatter | solution.py:329
  18.1 7.8 %collective-permute-start.2 = (bf16[2,128,512]{2,1,0:T(8,128)(2,1)S(1)}, bf16[2,128,512]{2,1,0:T(8,128)(2,1)S(1)}, u32[]{:S(2)}, u32[]{:S(2)}) collective-permute-start(bf16[2,128,512]{2,1,0:T(8,128)(2,1)S(1)} %get-tuple-element.67), channel_id=1, source_target_pairs={{0,8},{1,129},{2,10},{3,131},{4,12},{5,133},{6,14},{7,135},{8,0},{... | collective-permute-start | bytes 786440 | tf_op jit(solution)/shard_map/ppermute | solution.py:25
  21.9 7.3 %collective-permute-start.1 = (bf16[2,128,512]{2,1,0:T(8,128)(2,1)S(1)}, bf16[2,128,512]{2,1,0:T(8,128)(2,1)S(1)}, u32[]{:S(2)}, u32[]{:S(2)}) collective-permute-start(bf16[2,128,512]{2,1,0:T(8,128)(2,1)S(1)} %get-tuple-element.67), channel_id=1, source_target_pairs={{0,12},{1,131},{2,14},{3,1},{4,0},{5,135},{6,2},{7,5},{8,4},{9,139... | collective-permute-start | bytes 786440 | tf_op jit(solution)/shard_map/ppermute | solution.py:25
  22.6 6.7 %collective-permute-start = (bf16[2,128,512]{2,1,0:T(8,128)(2,1)S(1)}, bf16[2,128,512]{2,1,0:T(8,128)(2,1)S(1)}, u32[]{:S(2)}, u32[]{:S(2)}) collective-permute-start(bf16[2,128,512]{2,1,0:T(8,128)(2,1)S(1)} %get-tuple-element.67), channel_id=1, source_target_pairs={{0,4},{1,3},{2,6},{3,129},{4,8},{5,7},{6,10},{7,133},{8,12},{9,11}... | collective-permute-start | bytes 786440 | tf_op jit(solution)/shard_map/ppermute | solution.py:25
  29.5 34.2 %copy-start = (bf16[4,2,128,512]{3,2,1,0:T(8,128)(2,1)}, bf16[4,2,128,512]{3,2,1,0:T(8,128)(2,1)S(1)}, u32[]{:S(2)}) copy-start(bf16[4,2,128,512]{3,2,1,0:T(8,128)(2,1)S(1)} %pad_maximum_fusion.refs_0_) | copy-start | bytes 3145732
  29.5 15.3 %collective-permute-start.3 = (bf16[4,2,128,512]{3,2,1,0:T(8,128)(2,1)S(1)}, bf16[4,2,128,512]{3,2,1,0:T(8,128)(2,1)S(1)}, u32[]{:S(2)}, u32[]{:S(2)}) collective-permute-start(bf16[4,2,128,512]{3,2,1,0:T(8,128)(2,1)S(1)} %pad_maximum_fusion.refs_0_), channel_id=1, source_target_pairs={{0,2},{1,5},{2,128},{3,7},{4,6},{5,9},{6,132},{7,11},{8,10},{9,13}... | collective-permute-start | bytes 3145736 | tf_op jit(solution)/shard_map/ppermute | solution.py:25
  30.6 24.6 %collective-permute-start.4 = (bf16[4,2,128,512]{3,2,1,0:T(8,128)(2,1)S(1)}, bf16[4,2,128,512]{3,2,1,0:T(8,128)(2,1)S(1)}, u32[]{:S(2)}, u32[]{:S(2)}) collective-permute-start(bf16[4,2,128,512]{3,2,1,0:T(8,128)(2,1)S(1)} %pad_maximum_fusion.refs_0_), channel_id=1, source_target_pairs={{0,130},{1,13},{2,0},{3,15},{4,134},{5,1},{6,4},{7,3},{8,138},{9,5... | collective-permute-start | bytes 3145736 | tf_op jit(solution)/shard_map/ppermute | solution.py:25
  32.3 24.8 %collective-permute-start.5 = (bf16[4,2,128,512]{3,2,1,0:T(8,128)(2,1)S(1)}, bf16[4,2,128,512]{3,2,1,0:T(8,128)(2,1)}, u32[]{:S(2)}, u32[]{:S(2)}) collective-permute-start(bf16[4,2,128,512]{3,2,1,0:T(8,128)(2,1)S(1)} %pad_maximum_fusion.refs_0_), channel_id=1, source_target_pairs={{0,128},{1,9},{2,130},{3,11},{4,132},{5,13},{6,134},{7,15},{8,136}... | collective-permute-start | bytes 3145736 | tf_op jit(solution)/shard_map/ppermute | solution.py:25
  33.6 29.2 %collective-permute-start.6 = (bf16[4,2,128,512]{3,2,1,0:T(8,128)(2,1)S(1)}, bf16[4,2,128,512]{3,2,1,0:T(8,128)(2,1)}, u32[]{:S(2)}, u32[]{:S(2)}) collective-permute-start(bf16[4,2,128,512]{3,2,1,0:T(8,128)(2,1)S(1)} %pad_maximum_fusion.refs_0_), channel_id=1, source_target_pairs={{0,1},{1,0},{2,3},{3,2},{4,5},{5,4},{6,7},{7,6},{8,9},{9,8},{10,11... | collective-permute-start | bytes 3145736 | tf_op jit(solution)/shard_map/ppermute | solution.py:25
  44.9 18.8 %copy-start.1 = (bf16[4,2,128,512]{3,2,1,0:T(8,128)(2,1)}, bf16[4,2,128,512]{3,2,1,0:T(8,128)(2,1)S(1)}, u32[]{:S(2)}) copy-start(bf16[4,2,128,512]{3,2,1,0:T(8,128)(2,1)S(1)} %collective-permute-done.3.refs_1_) | copy-start | bytes 3145732
  44.9 18.0 %collective-permute-start.7 = (bf16[4,2,128,512]{3,2,1,0:T(8,128)(2,1)S(1)}, bf16[4,2,128,512]{3,2,1,0:T(8,128)(2,1)}, u32[]{:S(2)}, u32[]{:S(2)}) collective-permute-start(bf16[4,2,128,512]{3,2,1,0:T(8,128)(2,1)S(1)} %collective-permute-done.3.refs_1_), channel_id=1, source_target_pairs={{0,1},{1,0},{2,3},{3,2},{4,5},{5,4},{6,7},{7,6},{8,9},{9,8},{10,11... | collective-permute-start | bytes 3145736 | tf_op jit(solution)/shard_map/ppermute | solution.py:25
  55.3 7.6 %collective-permute-start.8 = (bf16[4,2,128,512]{3,2,1,0:T(8,128)(2,1)S(1)}, bf16[4,2,128,512]{3,2,1,0:T(8,128)(2,1)}, u32[]{:S(2)}, u32[]{:S(2)}) collective-permute-start(bf16[4,2,128,512]{3,2,1,0:T(8,128)(2,1)S(1)} %collective-permute-done.4.refs_2_), channel_id=1, source_target_pairs={{0,1},{1,0},{2,3},{3,2},{4,5},{5,4},{6,7},{7,6},{8,9},{9,8},{10,11... | collective-permute-start | bytes 3145736 | tf_op jit(solution)/shard_map/ppermute | solution.py:25
  57.1 6.6 %collective-permute-start.9 = (bf16[4,2,128,512]{3,2,1,0:T(8,128)(2,1)}, bf16[4,2,128,512]{3,2,1,0:T(8,128)(2,1)}, u32[]{:S(2)}, u32[]{:S(2)}) collective-permute-start(bf16[4,2,128,512]{3,2,1,0:T(8,128)(2,1)} %collective-permute-done.5.refs_3_), channel_id=1, source_target_pairs={{0,1},{1,0},{2,3},{3,2},{4,5},{5,4},{6,7},{7,6},{8,9},{9,8},{10,11... | collective-permute-start | bytes 3145736 | tf_op jit(solution)/shard_map/ppermute | solution.py:25
  96.3 3.2 %collective-permute-start.16 = (bf16[4,2,128,512]{3,2,1,0:T(8,128)(2,1)}, bf16[4,2,128,512]{3,2,1,0:T(8,128)(2,1)S(1)}, u32[]{:S(2)}, u32[]{:S(2)}) collective-permute-start(bf16[4,2,128,512]{3,2,1,0:T(8,128)(2,1)} %get-tuple-element.37), channel_id=1, source_target_pairs={{0,1},{1,0},{2,3},{3,2},{4,5},{5,4},{6,7},{7,6},{8,9},{9,8},{10,11... | collective-permute-start | bytes 3145736 | tf_op jit(solution)/shard_map/ppermute | solution.py:25
  97.0 6.5 %collective-permute-start.14 = (bf16[4,2,128,512]{3,2,1,0:T(8,128)(2,1)}, bf16[4,2,128,512]{3,2,1,0:T(8,128)(2,1)S(1)}, u32[]{:S(2)}, u32[]{:S(2)}) collective-permute-start(bf16[4,2,128,512]{3,2,1,0:T(8,128)(2,1)} %get-tuple-element.35), channel_id=1, source_target_pairs={{0,1},{1,0},{2,3},{3,2},{4,5},{5,4},{6,7},{7,6},{8,9},{9,8},{10,11... | collective-permute-start | bytes 3145736 | tf_op jit(solution)/shard_map/ppermute | solution.py:25
  97.1 6.8 %collective-permute-start.12 = (bf16[4,2,128,512]{3,2,1,0:T(8,128)(2,1)}, bf16[4,2,128,512]{3,2,1,0:T(8,128)(2,1)S(1)}, u32[]{:S(2)}, u32[]{:S(2)}) collective-permute-start(bf16[4,2,128,512]{3,2,1,0:T(8,128)(2,1)} %get-tuple-element.33), channel_id=1, source_target_pairs={{0,1},{1,0},{2,3},{3,2},{4,5},{5,4},{6,7},{7,6},{8,9},{9,8},{10,11... | collective-permute-start | bytes 3145736 | tf_op jit(solution)/shard_map/ppermute | solution.py:25
  97.5 8.6 %collective-permute-start.11 = (bf16[4,2,128,512]{3,2,1,0:T(8,128)(2,1)}, bf16[4,2,128,512]{3,2,1,0:T(8,128)(2,1)S(1)}, u32[]{:S(2)}, u32[]{:S(2)}) collective-permute-start(bf16[4,2,128,512]{3,2,1,0:T(8,128)(2,1)} %get-tuple-element.31), channel_id=1, source_target_pairs={{0,1},{1,0},{2,3},{3,2},{4,5},{5,4},{6,7},{7,6},{8,9},{9,8},{10,11... | collective-permute-start | bytes 3145736 | tf_op jit(solution)/shard_map/ppermute | solution.py:25
  101.1 25.4 %collective-permute-start.17 = (bf16[4,2,128,512]{3,2,1,0:T(8,128)(2,1)S(1)}, bf16[4,2,128,512]{3,2,1,0:T(8,128)(2,1)S(1)}, u32[]{:S(2)}, u32[]{:S(2)}) collective-permute-start(bf16[4,2,128,512]{3,2,1,0:T(8,128)(2,1)S(1)} %add_convert_fusion.1), channel_id=1, source_target_pairs={{0,130},{1,13},{2,0},{3,15},{4,134},{5,1},{6,4},{7,3},{8,138},{9,5... | collective-permute-start | bytes 3145736 | tf_op jit(solution)/shard_map/ppermute | solution.py:25
  103.9 26.6 %copy-start.5 = (bf16[4,2,128,512]{3,2,1,0:T(8,128)(2,1)S(1)}, bf16[4,2,128,512]{3,2,1,0:T(8,128)(2,1)}, u32[]{:S(2)}) copy-start(bf16[4,2,128,512]{3,2,1,0:T(8,128)(2,1)} %get-tuple-element.30) | copy-start | bytes 3145732
  103.9 26.6 %collective-permute-start.15 = (bf16[4,2,128,512]{3,2,1,0:T(8,128)(2,1)S(1)}, bf16[4,2,128,512]{3,2,1,0:T(8,128)(2,1)S(1)}, u32[]{:S(2)}, u32[]{:S(2)}) collective-permute-start(bf16[4,2,128,512]{3,2,1,0:T(8,128)(2,1)S(1)} %add_convert_fusion.2), channel_id=1, source_target_pairs={{0,2},{1,5},{2,128},{3,7},{4,6},{5,9},{6,132},{7,11},{8,10},{9,13}... | collective-permute-start | bytes 3145736 | tf_op jit(solution)/shard_map/ppermute | solution.py:25
  104.3 26.1 %collective-permute-start.13 = (bf16[4,2,128,512]{3,2,1,0:T(8,128)(2,1)S(1)}, bf16[4,2,128,512]{3,2,1,0:T(8,128)(2,1)S(1)}, u32[]{:S(2)}, u32[]{:S(2)}) collective-permute-start(bf16[4,2,128,512]{3,2,1,0:T(8,128)(2,1)S(1)} %add_convert_fusion.3), channel_id=1, source_target_pairs={{0,128},{1,9},{2,130},{3,11},{4,132},{5,13},{6,134},{7,15},{8,136}... | collective-permute-start | bytes 3145736 | tf_op jit(solution)/shard_map/ppermute | solution.py:25
  131.3 14.2 %collective-permute-start.18 = (bf16[2,128,512]{2,1,0:T(8,128)(2,1)S(1)}, bf16[2,128,512]{2,1,0:T(8,128)(2,1)S(1)}, u32[]{:S(2)}, u32[]{:S(2)}) collective-permute-start(bf16[2,128,512]{2,1,0:T(8,128)(2,1)S(1)} %get-tuple-element.58), channel_id=1, source_target_pairs={{0,8},{1,129},{2,10},{3,131},{4,12},{5,133},{6,14},{7,135},{8,0},{... | collective-permute-start | bytes 786440 | tf_op jit(solution)/shard_map/ppermute | solution.py:25
  134.1 11.4 %collective-permute-start.19 = (bf16[2,128,512]{2,1,0:T(8,128)(2,1)S(1)}, bf16[2,128,512]{2,1,0:T(8,128)(2,1)S(1)}, u32[]{:S(2)}, u32[]{:S(2)}) collective-permute-start(bf16[2,128,512]{2,1,0:T(8,128)(2,1)S(1)} %get-tuple-element.57), channel_id=1, source_target_pairs={{0,4},{1,3},{2,6},{3,129},{4,8},{5,7},{6,10},{7,133},{8,12},{9,11}... | collective-permute-start | bytes 786440 | tf_op jit(solution)/shard_map/ppermute | solution.py:25
  134.4 11.1 %collective-permute-start.20 = (bf16[2,128,512]{2,1,0:T(8,128)(2,1)S(1)}, bf16[2,128,512]{2,1,0:T(8,128)(2,1)S(1)}, u32[]{:S(2)}, u32[]{:S(2)}) collective-permute-start(bf16[2,128,512]{2,1,0:T(8,128)(2,1)S(1)} %get-tuple-element.56), channel_id=1, source_target_pairs={{0,12},{1,131},{2,14},{3,1},{4,0},{5,135},{6,2},{7,5},{8,4},{9,139... | collective-permute-start | bytes 786440 | tf_op jit(solution)/shard_map/ppermute | solution.py:25
  142.2 6.0 %collective-permute-start.21 = (bf16[4,128,128]{2,1,0:T(8,128)(2,1)S(1)}, bf16[4,128,128]{2,1,0:T(8,128)(2,1)S(1)}, u32[]{:S(2)}, u32[]{:S(2)}) collective-permute-start(bf16[4,128,128]{2,1,0:T(8,128)(2,1)S(1)} %bitcast.71), channel_id=1, source_target_pairs={{0,128},{1,129},{2,130},{3,131},{4,132},{5,133},{6,134},{7,135},{8... | collective-permute-start | bytes 393224 | tf_op jit(solution)/shard_map/ppermute | solution.py:25
  145.2 5.4 %collective-permute-start.22 = (bf16[4,128,128]{2,1,0:T(8,128)(2,1)S(1)}, bf16[4,128,128]{2,1,0:T(8,128)(2,1)S(1)}, u32[]{:S(2)}, u32[]{:S(2)}) collective-permute-start(bf16[4,128,128]{2,1,0:T(8,128)(2,1)S(1)} %get-tuple-element.62), channel_id=1, source_target_pairs={{0,128},{1,129},{2,130},{3,131},{4,132},{5,133},{6,134},{7,135},{8... | collective-permute-start | bytes 393224 | tf_op jit(solution)/shard_map/ppermute | solution.py:25
  (3 other events, 18.6 us)
Sparse Core Ops, SparseCore 0:
  18.1 59.4 all-gather.2
  87.0 53.9 reduce-scatter.1
